TPU v7x, 32 devices: a whole 2x2x4 slice. The times are simulated.
32 devices in a mesh: seq: 8 (over z, y), tp: 4 (over x, core).
Axes of the slice: x: 2, y: 2, z: 4, core: 2. Of those that a mesh axis runs over, the one named last changes fastest.
Arguments:
- tokens: bfloat16 [2, 3072, 2048], P(None, ('seq', 'tp')), may hold values from -6 to 6
- seq_cuts: int32 [2], replicated, may hold values from 1024 to 3072, as said below
- w_query: bfloat16 [2048, 2048], P(('seq', 'tp')), may hold values from -2 to 2
- w_key: bfloat16 [2048, 2048], P(('seq', 'tp')), may hold values from -0.125 to 0.125
- w_value: bfloat16 [2048, 2048], P(('seq', 'tp')), may hold values from -0.125 to 0.125
- w_gate_out: bfloat16 [2048, 2048], P(('seq', 'tp')), may hold values from -0.125 to 0.125
- w_output: bfloat16 [2048, 2048], P(('seq', 'tp')), may hold values from -0.125 to 0.125
- w_low: bfloat16 [2048, 16], P(('seq', 'tp')), may hold values from -0.125 to 0.125
- w_rank: bfloat16 [256, 16], P(('seq', 'tp')), may hold values from -1.5 to 1.5
- gate_bias: bfloat16 [256], P(('seq', 'tp')), may hold values from 1 to 12
- attn_gain: bfloat16 [2048], P(('seq', 'tp')), may hold values from 0.099609375 to 1.8984375
- out_gain: bfloat16 [512], P(('seq', 'tp')), may hold values from 0.099609375 to 1.8984375
- ffn_gain: bfloat16 [2048], P(('seq', 'tp')), may hold values from 0.099609375 to 1.8984375
- w_gate: bfloat16 [2048, 5632], P('seq', 'tp'), may hold values from -0.125 to 0.125
- w_up: bfloat16 [2048, 5632], P('seq', 'tp'), may hold values from -0.125 to 0.125
- w_down: bfloat16 [2048, 5632], P('seq', 'tp'), may hold values from -0.078125 to 0.078125
- cotangent: bfloat16 [2, 3072, 2048], P(None, ('seq', 'tp')), may hold values from -6 to 6
Outputs:
- out: bfloat16 [2, 3072, 2048], P(None, ('seq', 'tp'))
- grad_tokens: float32 [2, 3072, 2048], P(None, ('seq', 'tp'))
- grad_w_query: float32 [2048, 2048], P(('seq', 'tp'))
- grad_w_key: float32 [2048, 2048], P(('seq', 'tp'))
- grad_w_value: float32 [2048, 2048], P(('seq', 'tp'))
- grad_w_gate_out: float32 [2048, 2048], P(('seq', 'tp'))
- grad_w_output: float32 [2048, 2048], P(('seq', 'tp'))
- grad_w_low: float32 [2048, 16], P(('seq', 'tp'))
- grad_w_rank: float32 [256, 16], P(('seq', 'tp'))
- grad_gate_bias: float32 [256], P(('seq', 'tp'))
- grad_attn_gain: float32 [2048], P(('seq', 'tp'))
- grad_out_gain: float32 [512], P(('seq', 'tp'))
- grad_ffn_gain: float32 [2048], P(('seq', 'tp'))
- grad_w_gate: float32 [2048, 5632], P('seq', 'tp')
- grad_w_up: float32 [2048, 5632], P('seq', 'tp')
- grad_w_down: float32 [2048, 5632], P('seq', 'tp')
Inputs may be any that keep to these rules, and one draw needn't show every extreme that they name: In stream s the first sequence holds positions 0 to seq_cuts[s] - 1 and the second the rest. One stream, drawn from the seed, is a single sequence (seq_cuts = 3072); in the others seq_cuts lies between 1024 and 2048.
All inputs are finite; a program needn't handle non-finite values.
Results may differ from a plain program's by a relative error of at most 0.03.
Values may be sent and summed in bfloat16 or wider, within the bound.
A program may use at most 448 MiB of HBM per device.

v0:
```python
import jax
import jax.numpy as jnp
from jax import lax
from jax.sharding import PartitionSpec as P

H = 4
BLOCK = 32


GATE_SCALE = 8.0
EPSILON = 1e-05
HIGHEST = lax.Precision.HIGHEST


def entering(part, axis, combine, identity):
    place = lax.axis_index(axis)
    gathered = jax.tree.map(lambda a: lax.all_gather(a, axis), part)
    state = jax.tree.map(lambda a, e: jnp.zeros_like(a) + jnp.asarray(e, a.dtype), part, identity)

    def entering_one(step, state):
        return combine(
            state, jax.tree.map(lambda a: lax.dynamic_index_in_dim(a, step, 0, False), gathered)
        )

    return lax.fori_loop(0, place, entering_one, state)


def carried_in(array, axis, join, neutral):
    count = lax.axis_size(axis)
    place = lax.axis_index(axis)
    ahead = count - 1 - place
    gathered = jax.tree.map(
        lambda a, kind: lax.all_gather(a.astype(kind), axis),
        array,
        jax.tree.map(lambda a: jnp.bfloat16 if a.dtype == jnp.float32 else a.dtype, array),
    )
    state = jax.tree.map(lambda a, e: jnp.zeros_like(a) + jnp.asarray(e, a.dtype), array, neutral)

    def carried_one(step, state):
        source = count - 1 - step
        return join(
            state,
            jax.tree.map(
                lambda a, own: lax.dynamic_index_in_dim(a, source, 0, False).astype(own.dtype),
                gathered,
                array,
            ),
        )

    return lax.fori_loop(0, ahead, carried_one, state)


def root_norm(values, gain_vec):
    return (
        values * lax.rsqrt(jnp.mean(values * values, axis=-1, keepdims=True) + EPSILON) * gain_vec
    )


def to_heads(flat, head_count):
    streams, positions, columns = flat.shape
    return flat.reshape(streams, positions, head_count, columns // head_count).transpose(0, 2, 1, 3)


def from_heads(grouped):
    streams, head_count, positions, piece_len = grouped.shape
    return grouped.transpose(0, 2, 1, 3).reshape(streams, positions, head_count * piece_len)


def to_blocks(values, dim_at, block_len):
    shaped = values.reshape(
        values.shape[:dim_at]
        + (values.shape[dim_at] // block_len, block_len)
        + values.shape[dim_at + 1 :]
    )
    return jnp.moveaxis(shaped, dim_at, 0)


def from_blocks(values, dim_at):
    moved = jnp.moveaxis(values, 0, dim_at)
    return moved.reshape(
        moved.shape[:dim_at]
        + (moved.shape[dim_at] * moved.shape[dim_at + 1],)
        + moved.shape[dim_at + 2 :]
    )


def block_terms(log_keep, starts):
    history = jnp.cumsum(log_keep, axis=2)
    started = jnp.cumsum(starts, axis=1)
    offsets = jnp.arange(log_keep.shape[2])
    causal = offsets[:, None] >= offsets[None, :]
    same_doc = ((started[:, :, None] == started[:, None, :]) & causal[None])[:, None, :, :, None]
    spans = history[:, :, :, None, :] - history[:, :, None, :, :]
    decay = jnp.where(same_doc, jnp.exp(jnp.where(same_doc, spans, 0.0)), 0.0)
    coefficient = decay * (-jnp.expm1(log_keep))[:, :, None, :, :]
    initial = jnp.where((started == 0)[:, None, :, None], jnp.exp(history), 0.0)
    return (coefficient, initial)


def carried(slots_in, coefficient, initial, key_rows, value_rows):
    paired = jnp.concatenate([key_rows, value_rows], axis=-1)
    return (
        jnp.einsum("shjm,shjd->shmd", coefficient[:, :, -1], paired, precision=HIGHEST)
        + initial[:, :, -1, :, None] * slots_in
    )


def carry_scan(slots_in, pieces):
    key_rows, value_rows, log_keep, starts = pieces
    coefficient, initial = block_terms(log_keep, starts)
    return (carried(slots_in, coefficient, initial, key_rows, value_rows), None)


def read_step(slots_in, pieces):
    query, key_rows, value_rows, log_keep, starts = pieces
    coefficient, initial = block_terms(log_keep, starts)
    head_dim = key_rows.shape[-1]
    affinity = jnp.einsum("shtd,shjd->shtj", query, key_rows, precision=HIGHEST)
    scores = jnp.einsum("shtjm,shtj->shtm", coefficient, affinity, precision=HIGHEST)
    scores = scores + initial * jnp.einsum(
        "shtd,shmd->shtm", query, slots_in[..., :head_dim], precision=HIGHEST
    )
    weights_read = jax.nn.softmax(scores, axis=-1)
    mixing = jnp.einsum("shtm,shtjm->shtj", weights_read, coefficient, precision=HIGHEST)
    reading = jnp.einsum("shtj,shjd->shtd", mixing, value_rows, precision=HIGHEST)
    reading = reading + jnp.einsum(
        "shtm,shmd->shtd", weights_read * initial, slots_in[..., head_dim:], precision=HIGHEST
    )
    return (carried(slots_in, coefficient, initial, key_rows, value_rows), reading)


def readout(query, key_rows, value_rows, log_keep, slots_in, starts):
    head_dim = query.shape[-1] // H
    pieces = (
        to_blocks(to_heads(query, H) * head_dim ** (-0.5), 2, BLOCK),
        to_blocks(to_heads(key_rows, H), 2, BLOCK),
        to_blocks(to_heads(value_rows, H), 2, BLOCK),
        to_blocks(to_heads(log_keep, H), 2, BLOCK),
        to_blocks(starts, 1, BLOCK),
    )
    last_state, readings = lax.scan(jax.checkpoint(read_step), slots_in, pieces)
    return from_heads(from_blocks(readings, 2))


def transition(key_rows, value_rows, log_keep, starts):
    pieces = (
        to_blocks(to_heads(key_rows, H), 2, BLOCK),
        to_blocks(to_heads(value_rows, H), 2, BLOCK),
        to_blocks(to_heads(log_keep, H), 2, BLOCK),
        to_blocks(starts, 1, BLOCK),
    )
    slots_zero = jnp.zeros(
        (key_rows.shape[0], H, log_keep.shape[-1] // H, 2 * (key_rows.shape[-1] // H)), jnp.float32
    )
    local_state, unused = lax.scan(jax.checkpoint(carry_scan), slots_zero, pieces)
    survive = (
        jnp.exp(jnp.sum(to_heads(log_keep, H), axis=2))
        * (jnp.sum(starts, axis=1) == 0).astype(jnp.float32)[:, None, None]
    )
    return (survive, local_state)


def gated_read(reading, gate_out, out_gain):
    streams, positions, columns = reading.shape
    grouped = reading.reshape(streams, positions, H, columns // H)
    normed = root_norm(grouped, out_gain)
    return normed.reshape(streams, positions, columns) * jax.nn.silu(gate_out)


def forget_logs(low_rank, w_rank, gate_bias):
    logits = jnp.dot(low_rank, w_rank.T, precision=HIGHEST) + gate_bias
    return jax.nn.log_sigmoid(logits) / GATE_SCALE


def features(query, key_rows, value_rows):
    return (jax.nn.silu(query), jax.nn.silu(key_rows), jax.nn.silu(value_rows))


def chain(earlier, later):
    return (earlier[0] * later[0], later[0][..., None] * earlier[1] + later[1])


def against(rows, weight):
    return lax.dot_general(
        rows, weight, (((2,), (1,)), ((), ())), preferred_element_type=jnp.float32
    )


def pick_rows(entire, seq_count, tp_count, tp_rank):
    piece_len = entire.shape[0] // (seq_count * tp_count)
    shaped = entire.reshape((seq_count, tp_count, piece_len) + entire.shape[1:])
    chosen = lax.dynamic_index_in_dim(shaped, tp_rank, 1, keepdims=False)
    return chosen.reshape((seq_count * piece_len,) + entire.shape[1:])


def pick_columns(values, seq_count, tp_count, tp_rank):
    streams, positions, columns = values.shape
    piece_len = columns // (seq_count * tp_count)
    shaped = values.reshape(streams, positions, seq_count, tp_count, piece_len)
    chosen = lax.dynamic_index_in_dim(shaped, tp_rank, 3, keepdims=False)
    return chosen.reshape(streams, positions, seq_count * piece_len)


def on_device(
    tokens,
    seq_cuts,
    w_query,
    w_key,
    w_value,
    w_gate_out,
    w_output,
    w_low,
    w_rank,
    gate_bias,
    attn_gain,
    out_gain,
    ffn_gain,
    w_gate,
    w_up,
    w_down,
    cotangent,
):
    seq_count = lax.axis_size("seq")
    tp_count = lax.axis_size("tp")
    seq_rank = lax.axis_index("seq")
    tp_rank = lax.axis_index("tp")
    local_len = tokens.shape[1]
    rows_in, grad_rows = (
        lax.all_gather(tokens, "tp", axis=1, tiled=True),
        lax.all_gather(cotangent, "tp", axis=1, tiled=True),
    )
    mixer_local = (
        w_query,
        w_key,
        w_value,
        w_gate_out,
        w_output,
        w_low,
        w_rank,
        gate_bias,
        attn_gain,
        out_gain,
        ffn_gain,
    )
    entire = (
        lax.all_gather(mixer_local[0], ("seq", "tp"), axis=0, tiled=True),
        lax.all_gather(mixer_local[1], ("seq", "tp"), axis=0, tiled=True),
        lax.all_gather(mixer_local[2], ("seq", "tp"), axis=0, tiled=True),
        lax.all_gather(mixer_local[3], ("seq", "tp"), axis=0, tiled=True),
        lax.all_gather(mixer_local[4], ("seq", "tp"), axis=0, tiled=True),
        lax.all_gather(mixer_local[5], ("seq", "tp"), axis=0, tiled=True),
        lax.all_gather(mixer_local[6], ("seq", "tp"), axis=0, tiled=True),
        lax.all_gather(mixer_local[7], ("seq", "tp"), axis=0, tiled=True),
        lax.all_gather(mixer_local[8], ("seq", "tp"), axis=0, tiled=True),
        lax.all_gather(mixer_local[9], ("seq", "tp"), axis=0, tiled=True),
        lax.all_gather(mixer_local[10], ("seq", "tp"), axis=0, tiled=True),
    )
    (
        full_query,
        full_key,
        full_value,
        full_gate,
        full_output,
        full_low,
        full_rank,
        full_bias,
        full_attn,
        full_out,
        full_ffn,
    ) = entire
    ffn_gate, ffn_up, ffn_down = (
        lax.all_gather(w_gate, "seq", axis=0, tiled=True),
        lax.all_gather(w_up, "seq", axis=0, tiled=True),
        lax.all_gather(w_down, "seq", axis=0, tiled=True),
    )
    positions = rows_in.shape[1]
    offsets = seq_rank * positions + jnp.arange(positions)
    starts = ((offsets[None, :] == 0) | (offsets[None, :] == seq_cuts[:, None])).astype(jnp.float32)
    inputs = rows_in.astype(jnp.float32)
    normed_f, attn_pull = jax.vjp(root_norm, inputs, full_attn.astype(jnp.float32))
    normed = normed_f.astype(jnp.bfloat16)
    query = jnp.dot(normed, full_query, preferred_element_type=jnp.float32)
    key_rows = jnp.dot(normed, full_key, preferred_element_type=jnp.float32)
    value_rows = jnp.dot(normed, full_value, preferred_element_type=jnp.float32)
    gate_out = jnp.dot(normed, full_gate, preferred_element_type=jnp.float32)
    low_rank = jnp.dot(normed, full_low, preferred_element_type=jnp.float32)
    (query_feat, key_feat, value_feat), feature_pull = jax.vjp(
        features, query, key_rows, value_rows
    )
    log_keep, gate_pull = jax.vjp(
        forget_logs, low_rank, full_rank.astype(jnp.float32), full_bias.astype(jnp.float32)
    )

    def carry_fn(key_in, value_in, keep_in):
        return transition(key_in, value_in, keep_in, starts)

    (survive, local_state), carry_pull = jax.vjp(carry_fn, key_feat, value_feat, log_keep)
    identity = (jnp.ones_like(survive), jnp.zeros_like(local_state))
    unused_keep, slots_in = entering((survive, local_state), "seq", chain, identity)

    def read_fn(query_in, key_in, value_in, keep_in, state_in):
        return readout(query_in, key_in, value_in, keep_in, state_in, starts)

    reading, read_pull = jax.vjp(read_fn, query_feat, key_feat, value_feat, log_keep, slots_in)
    branch_f, branch_pull = jax.vjp(gated_read, reading, gate_out, full_out.astype(jnp.float32))
    branch = branch_f.astype(jnp.bfloat16)
    hidden = inputs + jnp.dot(branch, full_output, preferred_element_type=jnp.float32)
    ffn_f, ffn_pull = jax.vjp(root_norm, hidden, full_ffn.astype(jnp.float32))
    ffn_in = ffn_f.astype(jnp.bfloat16)
    gate_pre = jnp.dot(ffn_in, ffn_gate, preferred_element_type=jnp.float32)
    up_pre = jnp.dot(ffn_in, ffn_up, preferred_element_type=jnp.float32)
    gate_sig = jax.nn.sigmoid(gate_pre)
    product_in = (gate_pre * gate_sig * up_pre).astype(jnp.bfloat16)
    partial_out = against(product_in, ffn_down)
    ffn_out = lax.psum_scatter(
        partial_out.astype(jnp.bfloat16), "tp", scatter_dimension=1, tiled=True
    ).astype(jnp.float32)
    own_hidden = lax.dynamic_slice_in_dim(hidden, tp_rank * local_len, local_len, 1)
    result = (own_hidden + ffn_out).astype(jnp.bfloat16)
    grad_product = jnp.dot(grad_rows, ffn_down, preferred_element_type=jnp.float32)
    grad_gate_pre = (grad_product * up_pre * gate_sig * (1.0 + gate_pre * (1.0 - gate_sig))).astype(
        jnp.bfloat16
    )
    grad_up_pre = (grad_product * gate_pre * gate_sig).astype(jnp.bfloat16)
    grad_w_down = jnp.einsum(
        "spd,spf->df", grad_rows, product_in, preferred_element_type=jnp.float32
    )
    grad_w_gate = jnp.einsum(
        "spd,spf->df", ffn_in, grad_gate_pre, preferred_element_type=jnp.float32
    )
    grad_w_up = jnp.einsum("spd,spf->df", ffn_in, grad_up_pre, preferred_element_type=jnp.float32)
    grad_ffn_part = against(grad_gate_pre, ffn_gate) + against(grad_up_pre, ffn_up)
    grad_ffn_in = lax.psum(grad_ffn_part.astype(jnp.bfloat16), "tp").astype(jnp.float32)
    grad_norm_h, grad_ffn_gain = ffn_pull(grad_ffn_in)
    grad_hidden = grad_rows.astype(jnp.float32) + grad_norm_h
    grad_mixed = grad_hidden.astype(jnp.bfloat16)
    entire = (
        lax.all_gather(mixer_local[0], ("seq", "tp"), axis=0, tiled=True),
        lax.all_gather(mixer_local[1], ("seq", "tp"), axis=0, tiled=True),
        lax.all_gather(mixer_local[2], ("seq", "tp"), axis=0, tiled=True),
        lax.all_gather(mixer_local[3], ("seq", "tp"), axis=0, tiled=True),
        lax.all_gather(mixer_local[4], ("seq", "tp"), axis=0, tiled=True),
        lax.all_gather(mixer_local[5], ("seq", "tp"), axis=0, tiled=True),
        lax.all_gather(mixer_local[6], ("seq", "tp"), axis=0, tiled=True),
        lax.all_gather(mixer_local[7], ("seq", "tp"), axis=0, tiled=True),
        lax.all_gather(mixer_local[8], ("seq", "tp"), axis=0, tiled=True),
        lax.all_gather(mixer_local[9], ("seq", "tp"), axis=0, tiled=True),
        lax.all_gather(mixer_local[10], ("seq", "tp"), axis=0, tiled=True),
    )
    back_query, back_key, back_value, back_gate, back_output, back_low = entire[:6]
    picked_branch = pick_columns(branch, seq_count, tp_count, tp_rank)
    grad_w_output = jnp.einsum(
        "spc,spe->ce", picked_branch, grad_mixed, preferred_element_type=jnp.float32
    )
    grad_branch = against(grad_mixed, back_output)
    grad_reading, grad_gate_out, grad_out_gain = branch_pull(grad_branch)
    grad_q_read, grad_k_read, grad_v_read, grad_keep_read, direct = read_pull(grad_reading)
    unused_after, after_sum = carried_in(
        (survive, direct), "seq", chain, (jnp.ones_like(survive), jnp.zeros_like(direct))
    )
    grad_k_carry, grad_v_carry, grad_keep_carry = carry_pull(
        (jnp.sum(after_sum * slots_in, axis=-1), after_sum)
    )
    grad_low_rank, grad_rank, grad_bias = gate_pull(grad_keep_read + grad_keep_carry)
    grad_q_raw, grad_k_raw, grad_v_raw = feature_pull(
        (grad_q_read, grad_k_read + grad_k_carry, grad_v_read + grad_v_carry)
    )
    grad_query = grad_q_raw.astype(jnp.bfloat16)
    grad_key = grad_k_raw.astype(jnp.bfloat16)
    grad_value = grad_v_raw.astype(jnp.bfloat16)
    grad_gate_rounded = grad_gate_out.astype(jnp.bfloat16)
    grad_normed = against(grad_query, back_query) + against(grad_key, back_key)
    grad_normed = (
        grad_normed + against(grad_value, back_value) + against(grad_gate_rounded, back_gate)
    )
    grad_normed = grad_normed + lax.dot_general(
        grad_low_rank, back_low.astype(jnp.float32), (((2,), (1,)), ((), ())), precision=HIGHEST
    )
    picked = pick_columns(normed, seq_count, tp_count, tp_rank)
    grad_w_query = jnp.einsum("spc,spe->ce", picked, grad_query, preferred_element_type=jnp.float32)
    grad_w_key = jnp.einsum("spc,spe->ce", picked, grad_key, preferred_element_type=jnp.float32)
    grad_w_value = jnp.einsum("spc,spe->ce", picked, grad_value, preferred_element_type=jnp.float32)
    grad_w_gate_out = jnp.einsum(
        "spc,spe->ce", picked, grad_gate_rounded, preferred_element_type=jnp.float32
    )
    grad_w_low = jnp.einsum(
        "spc,spr->cr", picked.astype(jnp.float32), grad_low_rank, precision=HIGHEST
    )
    grad_inputs_norm, grad_attn_gain = attn_pull(grad_normed)
    grad_inputs = grad_hidden + grad_inputs_norm
    own_grad = lax.dynamic_slice_in_dim(grad_inputs, tp_rank * local_len, local_len, 1)
    mixer_sums = (
        lax.psum_scatter(
            grad_w_query.astype(jnp.bfloat16), "seq", scatter_dimension=0, tiled=True
        ).astype(jnp.float32),
        lax.psum_scatter(
            grad_w_key.astype(jnp.bfloat16), "seq", scatter_dimension=0, tiled=True
        ).astype(jnp.float32),
        lax.psum_scatter(
            grad_w_value.astype(jnp.bfloat16), "seq", scatter_dimension=0, tiled=True
        ).astype(jnp.float32),
        lax.psum_scatter(
            grad_w_gate_out.astype(jnp.bfloat16), "seq", scatter_dimension=0, tiled=True
        ).astype(jnp.float32),
        lax.psum_scatter(
            grad_w_output.astype(jnp.bfloat16), "seq", scatter_dimension=0, tiled=True
        ).astype(jnp.float32),
        lax.psum_scatter(
            grad_w_low.astype(jnp.bfloat16), "seq", scatter_dimension=0, tiled=True
        ).astype(jnp.float32),
        lax.psum_scatter(
            pick_rows(grad_rank, seq_count, tp_count, tp_rank).astype(jnp.bfloat16),
            "seq",
            scatter_dimension=0,
            tiled=True,
        ).astype(jnp.float32),
        lax.psum_scatter(
            pick_rows(grad_bias, seq_count, tp_count, tp_rank).astype(jnp.bfloat16),
            "seq",
            scatter_dimension=0,
            tiled=True,
        ).astype(jnp.float32),
        lax.psum_scatter(
            pick_rows(grad_attn_gain, seq_count, tp_count, tp_rank).astype(jnp.bfloat16),
            "seq",
            scatter_dimension=0,
            tiled=True,
        ).astype(jnp.float32),
        lax.psum_scatter(
            pick_rows(grad_out_gain, seq_count, tp_count, tp_rank).astype(jnp.bfloat16),
            "seq",
            scatter_dimension=0,
            tiled=True,
        ).astype(jnp.float32),
        lax.psum_scatter(
            pick_rows(grad_ffn_gain, seq_count, tp_count, tp_rank).astype(jnp.bfloat16),
            "seq",
            scatter_dimension=0,
            tiled=True,
        ).astype(jnp.float32),
    )
    ffn_sums = (
        lax.psum_scatter(
            grad_w_gate.astype(jnp.bfloat16), "seq", scatter_dimension=0, tiled=True
        ).astype(jnp.float32),
        lax.psum_scatter(
            grad_w_up.astype(jnp.bfloat16), "seq", scatter_dimension=0, tiled=True
        ).astype(jnp.float32),
        lax.psum_scatter(
            grad_w_down.astype(jnp.bfloat16), "seq", scatter_dimension=0, tiled=True
        ).astype(jnp.float32),
    )
    return (result, own_grad) + tuple(mixer_sums) + tuple(ffn_sums)


def solution(mesh):
    placed = (
        P(None, ("seq", "tp"), None),
        P(),
        P(("seq", "tp"), None),
        P(("seq", "tp"), None),
        P(("seq", "tp"), None),
        P(("seq", "tp"), None),
        P(("seq", "tp"), None),
        P(("seq", "tp"), None),
        P(("seq", "tp"), None),
        P(("seq", "tp")),
        P(("seq", "tp")),
        P(("seq", "tp")),
        P(("seq", "tp")),
        P("seq", "tp"),
        P("seq", "tp"),
        P("seq", "tp"),
        P(None, ("seq", "tp"), None),
    )
    return jax.shard_map(
        on_device,
        mesh=mesh,
        in_specs=placed,
        out_specs=(
            P(None, ("seq", "tp"), None),
            P(None, ("seq", "tp"), None),
            P(("seq", "tp"), None),
            P(("seq", "tp"), None),
            P(("seq", "tp"), None),
            P(("seq", "tp"), None),
            P(("seq", "tp"), None),
            P(("seq", "tp"), None),
            P(("seq", "tp"), None),
            P(("seq", "tp")),
            P(("seq", "tp")),
            P(("seq", "tp")),
            P(("seq", "tp")),
            P("seq", "tp"),
            P("seq", "tp"),
            P("seq", "tp"),
        ),
        check_vma=False,
    )
```

profile of v0, /device:TPU:0, one launch (start us, length us, event | category | flops | bytes accessed | tf_op | source)
XLA Modules:
  0.0 2953.1 jit_solution(4395062473121685084)
XLA Ops:
  14.7 42.4 %all-reduce.15 = (bf16[2048]{0:T(1024)(128)(2,1)S(1)}, bf16[256]{0:T(256)(128)(2,1)S(1)}, bf16[512]{0:T(512)(128)(2,1)S(1)}, bf16[2048]{0:T(1024)(128)(2,1)S(1)}) all-reduce(bf16[2048]{0:T(1024)(128)(2,1)S(1)} %dynamic-update-slice, bf16[256]{0:T(256)(128)(2,1)S(1)} %dynamic-update-slice.1, ...), channel_id=1, replica_groups=mesh['seq'=8,'tp'=4] {'seq','tp'}, use_global_device_ids=true, to_apply=%add.6 | all-reduce | flops 4864 | bytes 19456
  57.1 41.4 %all-gather.2 = bf16[32,64,16]{1,2,0:T(8,128)(2,1)S(1)} all-gather(bf16[1,64,16]{1,2,0:T(8,128)(2,1)} %bitcast.682), channel_id=1, replica_groups=mesh['seq'=8,'tp'=4] {'seq','tp'}, dimensions={0}, use_global_device_ids=true | all-gather | bytes 67584 | tf_op jit(solution)/shard_map/all_gather | solution.py:251
  98.7 37.3 %all_gather.77 = bf16[256,16]{1,0:T(8,128)(2,1)S(1)} all-gather(bf16[8,16]{1,0:T(8,128)(2,1)} %param.37), channel_id=1, replica_groups=mesh['seq'=8,'tp'=4] {'seq','tp'}, dimensions={0}, use_global_device_ids=true | all-gather | bytes 8448 | tf_op jit(solution)/shard_map/all_gather | solution.py:252
  149.6 12.7 fusion.147
  166.7 34.7 %all-gather.20.cloned.1.call-done = bf16[2048,2048]{1,0:T(8,128)(2,1)} async-done(((bf16[64,2048]{1,0:T(8,128)(2,1)}), bf16[2048,2048]{1,0:T(8,128)(2,1)}) %all-gather.20.cloned.1.call-update) | async-done | bytes 8388624 | tf_op jit(solution)/shard_map/all_gather | solution.py:248
  201.4 12.4 fusion.146
  218.0 11.7 broadcast.396.clone
  229.7 94.1 %while.105 = (s32[]{:T(128)}, f32[2,4,64,1024]{3,2,1,0:T(8,128)S(1)}, f32[12,2,4,64,1024]{4,3,2,1,0:T(8,128)}, f32[12,2,32]{2,1,0:T(2,128)}, f32[12,2,4,32,64]{4...) while((s32[]{:T(128)}, ...), condition=%wide.region_6.7_spmd.clone, body=%wide.region_3.6_spmd.clone.sunk | while | flops 204283392 | bytes 12014730 | solution.py:155
  330.4 30.6 %all_gather.79 = f32[8,2,4,64]{3,2,1,0:T(4,128)S(1)} all-gather(f32[1,2,4,64]{3,2,1,0:T(4,128)S(1)} %get-tuple-element.1314), channel_id=1, replica_groups=mesh['seq'=8,'tp'=4] {'seq'}, dimensions={0}, use_global_device_ids=true | all-gather | bytes 18432 | tf_op jit(solution)/shard_map/all_gather | solution.py:17
  370.9 32.3 %all-gather.22.cloned.1.call-done = bf16[2048,2048]{1,0:T(8,128)(2,1)} async-done(((bf16[64,2048]{1,0:T(8,128)(2,1)}), bf16[2048,2048]{1,0:T(8,128)(2,1)}) %all-gather.22.cloned.1.call-update) | async-done | bytes 8388624 | tf_op jit(solution)/shard_map/all_gather | solution.py:246
  419.0 212.6 %all-gather.36.cloned.1.call-done = f32[16,4,64,1024]{3,2,1,0:T(8,128)} async-done(((f32[2,4,64,1024]{3,2,1,0:T(8,128)}), f32[16,4,64,1024]{3,2,1,0:T(8,128)}) %all-gather.36.cloned.1.call-update) | async-done | bytes 16777232 | tf_op jit(solution)/shard_map/all_gather | solution.py:17
  634.7 11.8 broadcast.396
  650.0 337.5 %while.104 = (s32[]{:T(128)}, f32[2,4,64,1024]{3,2,1,0:T(8,128)S(1)}, f32[12,2,4,32,512]{4,3,0,2,1:T(8,128)}, f32[12,2,4,64,1024]{4,3,2,1,0:T(8,128)}, f32[12,2,...) while((s32[]{:T(128)}, ...), condition=%wide.region_14.15_spmd.clone, body=%wide.region_9.14_spmd.clone.sunk | while | flops 524278848 | bytes 21849088 | solution.py:141
  996.7 13.5 multiply_convert_fusion.1
  1034.4 11.9 multiply_convert_fusion.4
  1058.0 80.1 %all-reduce.19.cloned.1.call-done = bf16[2,384,2048]{2,1,0:T(8,128)(2,1)} async-done(((bf16[2,384,2048]{2,1,0:T(8,128)(2,1)}), bf16[2,384,2048]{2,1,0:T(8,128)(2,1)}) %all-reduce.19.cloned.1.call-update) | async-done | bytes 3145744 | tf_op jit(solution)/shard_map/psum | solution.py:333
  1149.1 16.8 fusion.141
  1189.6 829.1 %while.106 = (s32[]{:T(128)}, f32[2,4,64,1024]{3,2,1,0:T(8,128)}, f32[12,2,4,32,512]{4,3,0,2,1:T(8,128)}, f32[12,2,4,32,512]{4,3,0,2,1:T(8,128)}, f32[12,2,4,32,...) while((s32[]{:T(128)}, f32[2,4,64,1024]{3,2,1,0:T(8,128)}, ...), condition=%wide.region_32.33_spmd.clone, body=%wide.region_21.32_spmd.clone.sunk | while | flops 1206459392 | bytes 73477264 | solution.py:141
  2090.0 28.6 all_gather.93
  2130.1 16.8 all-gather.38.cloned.1.call-done
  2147.2 12.3 while.102
  2170.6 233.6 %while.103 = (s32[]{:T(128)}, f32[2,4,64,1024]{3,2,1,0:T(8,128)S(1)}, f32[12,2,4,32,512]{4,3,0,2,1:T(8,128)}, f32[12,2,4,32,512]{4,3,0,2,1:T(8,128)}, f32[12,2,4...) while((s32[]{:T(128)}, ...), condition=%wide.region_43.44_spmd, body=%wide.region_35.43_spmd.sunk | while | flops 411393024 | bytes 33641096 | solution.py:155
  2434.1 12.2 fusion.112
  2446.6 11.9 fusion.108
  2466.6 43.5 %reduce-scatter.27.cloned.1.call-done = bf16[256,1408]{1,0:T(8,128)(2,1)} async-done(((bf16[2048,1408]{1,0:T(8,128)(2,1)}), bf16[256,1408]{1,0:T(8,128)(2,1)}) %reduce-scatter.27.cloned.1.call-update) | async-done | bytes 720912 | tf_op jit(solution)/shard_map/reduce_scatter | solution.py:446
  2512.4 111.6 %reduce-scatter.25.cloned.1.call-done = bf16[256,1408]{1,0:T(8,128)(2,1)} async-done(((bf16[2048,1408]{1,0:T(8,128)(2,1)}), bf16[256,1408]{1,0:T(8,128)(2,1)}) %reduce-scatter.25.cloned.1.call-update) | async-done | bytes 720912 | tf_op jit(solution)/shard_map/reduce_scatter | solution.py:443
  2626.3 111.9 %reduce-scatter.29.cloned.1.call-done = bf16[256,1408]{0,1:T(8,128)(2,1)} async-done(((bf16[2048,1408]{0,1:T(8,128)(2,1)}), bf16[256,1408]{0,1:T(8,128)(2,1)}) %reduce-scatter.29.cloned.1.call-update) | async-done | bytes 720912 | tf_op jit(solution)/shard_map/reduce_scatter | solution.py:449
  2757.5 12.0 fusion.116
  2774.2 19.5 multiply_reduce_fusion.4
  2796.1 36.3 %all-reduce.16 = (bf16[64,16]{1,0:T(8,128)(2,1)S(1)}, bf16[64]{0:T(256)(128)(2,1)S(1)}, bf16[512]{0:T(512)(128)(2,1)S(1)}, bf16[128]{0:T(256)(128)(2,1)S(1)}, bf16[512]{0:T(512)(128)(2,1)S(1)}) all-reduce(bf16[64,16]{1,0:T(8,128)(2,1)S(1)} %fusion.188, ...), channel_id=11, replica_groups=mesh['seq'=8,'tp'=4] {'seq'}, use_global_device_ids=true, to_apply=%region_52.53.clone | all-reduce | flops 2240 | bytes 8960
  2840.8 33.1 %reduce-scatter.17.cloned.1.call-done = bf16[64,2048]{1,0:T(8,128)(2,1)} async-done(((bf16[512,2048]{1,0:T(8,128)(2,1)}), bf16[64,2048]{1,0:T(8,128)(2,1)}) %reduce-scatter.17.cloned.1.call-update) | async-done | bytes 262160 | tf_op jit(solution)/shard_map/reduce_scatter | solution.py:396
  2875.6 68.9 %reduce-scatter.19.cloned.1.call-done = bf16[64,2048]{1,0:T(8,128)(2,1)} async-done(((bf16[512,2048]{1,0:T(8,128)(2,1)}), bf16[64,2048]{1,0:T(8,128)(2,1)}) %reduce-scatter.19.cloned.1.call-update) | async-done | bytes 262160 | tf_op jit(solution)/shard_map/reduce_scatter | solution.py:399
  (2073 shorter events, 1808.1 us)
Async XLA Ops:
  7.2 130.1 %all-gather.16.cloned.1.call-start = ((), (), s32[]{:S(2)}) async-start(), calls=%async_computation.10 | async-start | bytes 3932160 | tf_op jit(solution)/shard_map/all_gather | solution.py:229
  7.9 141.7 %all-gather.18.cloned.1.call-start = ((), (), s32[]{:S(2)}) async-start(), calls=%async_computation.11 | async-start | bytes 8650752 | tf_op jit(solution)/shard_map/all_gather | solution.py:247
  8.7 192.7 %all-gather.20.cloned.1.call-start = ((), (), s32[]{:S(2)}) async-start(), calls=%async_computation.12 | async-start | bytes 8650752 | tf_op jit(solution)/shard_map/all_gather | solution.py:248
  9.4 351.6 %all-gather.34.cloned.1.call-start = ((), (), s32[]{:S(2)}) async-start(), calls=%async_computation.20 | async-start | bytes 3932160 | tf_op jit(solution)/shard_map/all_gather | solution.py:230
  10.0 351.0 %all-gather.32.cloned.1.call-start = ((), (), s32[]{:S(2)}) async-start(), calls=%async_computation.18 | async-start | bytes 6488064 | tf_op jit(solution)/shard_map/all_gather | solution.py:274
  10.6 392.6 %all-gather.22.cloned.1.call-start = ((), (), s32[]{:S(2)}) async-start(), calls=%async_computation.13 | async-start | bytes 8650752 | tf_op jit(solution)/shard_map/all_gather | solution.py:246
  11.1 620.4 %all-gather.36.cloned.1.call-start = ((), (), s32[]{:S(2)}) async-start(), calls=%async_computation.30 | async-start | bytes 18874368 | tf_op jit(solution)/shard_map/all_gather | solution.py:17
  57.1 83.9 %copy-start.55 = (f32[2048]{0:T(1024)}, f32[2048]{0:T(1024)S(1)}, u32[]{:S(2)}) copy-start(f32[2048]{0:T(1024)S(1)} %convert_element_type.223) | copy-start | bytes 24580
  98.7 42.3 %copy-start.42 = (bf16[2048,16,1]{0,1,2:T(8,128)(2,1)}, bf16[2048,16,1]{0,1,2:T(8,128)(2,1)S(1)}, u32[]{:S(2)}) copy-start(bf16[2048,16,1]{0,1,2:T(8,128)(2,1)S(1)} %reshape.480) | copy-start | bytes 196612
  229.7 98.3 %copy-start.66 = (s32[2]{0:T(128)S(1)}, s32[2]{0:T(128)}, u32[]{:S(2)}) copy-start(s32[2]{0:T(128)} %param.30) | copy-start | bytes 28
  325.1 671.5 %all-gather.24.cloned.1.call-start = ((), (), s32[]{:S(2)}) async-start(), calls=%async_computation.14 | async-start | bytes 8650752 | tf_op jit(solution)/shard_map/all_gather | solution.py:249
  325.9 684.3 %all-gather.26.cloned.1.call-start = ((), (), s32[]{:S(2)}) async-start(), calls=%async_computation.15 | async-start | bytes 8650752 | tf_op jit(solution)/shard_map/all_gather | solution.py:250
  326.6 697.5 %all-gather.30.cloned.1.call-start = ((), (), s32[]{:S(2)}) async-start(), calls=%async_computation.17 | async-start | bytes 6488064 | tf_op jit(solution)/shard_map/all_gather | solution.py:273
  327.2 707.2 %all-gather.28.cloned.1.call-start = ((), (), s32[]{:S(2)}) async-start(), calls=%async_computation.16 | async-start | bytes 6488064 | tf_op jit(solution)/shard_map/all_gather | solution.py:272
  327.9 810.2 %all-reduce.19.cloned.1.call-start = ((), (), s32[]{:S(2)}) async-start(), calls=%async_computation.21 | async-start | bytes 6291456 | tf_op jit(solution)/shard_map/psum | solution.py:333
  361.0 42.2 %copy-start.19 = (bf16[2,384,2048]{2,1,0:T(8,128)(2,1)S(1)}, bf16[2,384,2048]{2,1,0:T(8,128)(2,1)}, u32[]{:S(2)}) copy-start(bf16[2,384,2048]{2,1,0:T(8,128)(2,1)} %copy-done.18) | copy-start | bytes 9437188
  1058.0 1089.0 %all-gather.38.cloned.1.call-start = ((), (), s32[]{:S(2)}) async-start(), calls=%async_computation.31 | async-start | bytes 9437184 | tf_op jit(solution)/shard_map/all_gather | solution.py:33
  1058.0 85.6 %copy-start.33 = (bf16[2,384,2048]{2,1,0:T(8,128)(2,1)S(1)}, bf16[2,384,2048]{2,1,0:T(8,128)(2,1)}, u32[]{:S(2)}) copy-start(bf16[2,384,2048]{2,1,0:T(8,128)(2,1)} %all-gather.34.cloned.1.call-done) | copy-start | bytes 9437188
  2021.5 437.0 %reduce-scatter.23.cloned.1.call-start = ((), (), s32[]{:S(2)}) async-start(), calls=%async_computation.26 | async-start | bytes 2359296 | tf_op jit(solution)/shard_map/reduce_scatter | solution.py:405
  2031.3 429.0 %reduce-scatter.15.cloned.1.call-start = ((), (), s32[]{:S(2)}) async-start(), calls=%async_computation.22 | async-start | bytes 2359296 | tf_op jit(solution)/shard_map/reduce_scatter | solution.py:393
  2049.8 412.3 %reduce-scatter.21.cloned.1.call-start = ((), (), s32[]{:S(2)}) async-start(), calls=%async_computation.25 | async-start | bytes 2359296 | tf_op jit(solution)/shard_map/reduce_scatter | solution.py:402
  2054.9 408.9 %reduce-scatter.13.cloned.1.call-start = ((), (), s32[]{:S(2)}) async-start(), calls=%async_computation.19 | async-start | bytes 3932160 | tf_op jit(solution)/shard_map/reduce_scatter | solution.py:315
  2064.1 446.0 %reduce-scatter.27.cloned.1.call-start = ((), (), s32[]{:S(2)}) async-start(), calls=%async_computation.28 | async-start | bytes 6488064 | tf_op jit(solution)/shard_map/reduce_scatter | solution.py:446
  2073.1 551.0 %reduce-scatter.25.cloned.1.call-start = ((), (), s32[]{:S(2)}) async-start(), calls=%async_computation.27 | async-start | bytes 6488064 | tf_op jit(solution)/shard_map/reduce_scatter | solution.py:443
  2082.1 656.0 %reduce-scatter.29.cloned.1.call-start = ((), (), s32[]{:S(2)}) async-start(), calls=%async_computation.29 | async-start | bytes 6488064 | tf_op jit(solution)/shard_map/reduce_scatter | solution.py:449
  2086.0 34.7 %copy-start.34 = (bf16[2,384,2048]{2,1,0:T(8,128)(2,1)S(1)}, bf16[2,384,2048]{2,1,0:T(8,128)(2,1)}, u32[]{:S(2)}) copy-start(bf16[2,384,2048]{2,1,0:T(8,128)(2,1)} %all-gather.34.cloned.1.call-done) | copy-start | bytes 9437188
  2086.0 34.7 %copy-start.73 = (bf16[2,384,1408]{2,1,0:T(8,128)(2,1)S(1)}, bf16[2,384,1408]{2,1,0:T(8,128)(2,1)}, u32[]{:S(2)}) copy-start(bf16[2,384,1408]{2,1,0:T(8,128)(2,1)} %get-tuple-element.1343) | copy-start | bytes 6488068
  2127.3 712.1 %reduce-scatter.31.cloned.1.call-start = ((), (), s32[]{:S(2)}) async-start(), calls=%async_computation.32 | async-start | bytes 147456
  2428.9 445.0 %reduce-scatter.17.cloned.1.call-start = ((), (), s32[]{:S(2)}) async-start(), calls=%async_computation.23 | async-start | bytes 2359296 | tf_op jit(solution)/shard_map/reduce_scatter | solution.py:396
  2434.0 510.5 %reduce-scatter.19.cloned.1.call-start = ((), (), s32[]{:S(2)}) async-start(), calls=%async_computation.24 | async-start | bytes 2359296 | tf_op jit(solution)/shard_map/reduce_scatter | solution.py:399
  2774.1 60.6 %copy-start.58 = (f32[2,384]{1,0:T(2,128)S(1)}, f32[2,384]{1,0:T(2,128)}, u32[]{:S(2)}) copy-start(f32[2,384]{1,0:T(2,128)} %copy-done.57) | copy-start | bytes 9220
  2774.1 61.3 %copy-start.65 = (f32[2,96]{1,0:T(2,128)S(1)}, f32[2,96]{1,0:T(2,128)}, u32[]{:S(2)}) copy-start(f32[2,96]{1,0:T(2,128)} %constant_dynamic-slice_fusion.4) | copy-start | bytes 2308
  (270 other events, 1713.0 us)
Sparse Core Ops, SparseCore 0:
  9.6 31.9 all-gather.15
  44.4 78.0 all-gather.17
  125.4 75.9 all-gather.19
  202.8 27.1 all-gather.33
  232.0 92.7 all-gather.31
  327.5 75.6 all-gather.21
  405.3 226.1 all-gather.35
  634.4 75.6 all-gather.23
  713.0 76.1 all-gather.25
  791.2 91.3 all-gather.29
  884.8 90.7 all-gather.27
  1058.1 79.9 all-reduce.18
  2021.6 125.2 all-gather.37
  2150.3 65.9 reduce-scatter.22
  2219.7 66.9 reduce-scatter.14
  2290.0 66.6 reduce-scatter.20
  2359.1 36.9 reduce-scatter.12
  2400.1 110.0 reduce-scatter.26
  2514.2 109.7 reduce-scatter.24
  2628.0 110.1 reduce-scatter.28
  2742.4 60.6 reduce-scatter.30
  2807.1 66.7 reduce-scatter.16
  2877.8 66.6 reduce-scatter.18
where the time goes:
time: 2970 us; the launch traced here: 2950 us
  matrix products  1060 us (36%)
  waiting for transfers between devices  752 us (25%)
  other arithmetic  476 us (16%)
  local copies, waits for them, and re-layouts  408 us (14%)
  blocking collectives  217 us (7%)
    dot_general x36, matrix products, read_step(): jnp.einsum('shtm,shtjm->shtj', weights_read, coefficient, precision=HIGHEST)  243 us
    all_gather x1, waiting for transfers between devices, entering(): gathered = jax.tree.map(lambda a: lax.all_gather(a, axis), part)  213 us
    dot_general x36, matrix products, read_step(): jnp.einsum('shtjm,shtj->shtm', coefficient, affinity, precision=HIGHEST)  205 us
    dot_general x72, matrix products, carried(): jnp.einsum('shjm,shjd->shmd', coefficient[:, :, -1], paired, precision=HI...  162 us
    squeeze x144, local copies, waits for them, and re-layouts, transition(): lax.scan(jax.checkpoint(carry_scan), slots_zero, pieces)  155 us
    reduce_scatter x1, waiting for transfers between devices, on_device(): lax.psum_scatter(grad_w_down.astype(jnp.bfloat16), 'seq', scatter_dimensi...  112 us
    reduce_scatter x1, waiting for transfers between devices, on_device(): lax.psum_scatter(grad_w_gate.astype(jnp.bfloat16), 'seq', scatter_dimensi...  112 us
    reduce_sum x24, other arithmetic, block_terms(): spans = history[:, :, :, None, :] - history[:, :, None, :, :]  98.4 us
  transfers between devices with their start and end apart: 23, of which 10 were waited for; matrix products, arithmetic and copies ran while one was open for 35% of the time, Pallas kernels for 0%

commit v1 on v0

v1 whole, which is shorter than its diff:
```python
import functools

import jax
import jax.numpy as jnp
from jax import lax
from jax.experimental import pallas as pl
from jax.experimental.pallas import tpu as pltpu
from jax.sharding import PartitionSpec as P

H = 4
GATE_SCALE = 8.0
EPSILON = 1e-05
BF = jnp.bfloat16
F32 = jnp.float32
CHUNK = 128
SUB = 16
HALVES = (16, 32, 64)


def mm(left, right, dims):
    return lax.dot_general(
        left.astype(BF), right.astype(BF), (dims, ((), ())), preferred_element_type=F32
    )


def mm_fine(left, right, dims):
    left_hi, right_hi = left.astype(BF), right.astype(BF)
    left_lo = (left - left_hi.astype(F32)).astype(BF)
    right_lo = (right - right_hi.astype(F32)).astype(BF)

    def part(a, b):
        return lax.dot_general(a, b, (dims, ((), ())), preferred_element_type=F32)

    return part(left_hi, right_hi) + (part(left_hi, right_lo) + part(left_lo, right_hi))


NN = ((1,), (0,))
NT = ((1,), (1,))
TN = ((0,), (0,))


def turn(values, amount):
    return pltpu.roll(values, amount % values.shape[1], 1)


def column(shape):
    return lax.broadcasted_iota(jnp.int32, shape, 1)


def row(shape):
    return lax.broadcasted_iota(jnp.int32, shape, 0)


def ahead_product(keep, size):
    place = column(keep.shape) & (size - 1)
    total, step = keep, 1
    while step < size:
        total = total * jnp.where(place >= step, turn(total, step), 1.0)
        step *= 2
    return total


def behind_product(keep, size):
    place = column(keep.shape) & (size - 1)
    total = jnp.where(place == size - 1, 1.0, turn(keep, -1))
    step = 1
    while step < size:
        total = total * jnp.where(place < size - step, turn(total, -step), 1.0)
        step *= 2
    return total


def chunks_of(values):
    return [values[:, at : at + CHUNK] for at in range(0, values.shape[1], CHUNK)]


def rows_of(values):
    return [values[at : at + CHUNK] for at in range(0, values.shape[0], CHUNK)]


class Decays:
    def __init__(self, keep):
        self.keep = chunks_of(keep)
        self.count = len(self.keep)
        self.ahead = [ahead_product(k, CHUNK) for k in self.keep]
        self.behind = [behind_product(k, CHUNK) for k in self.keep]
        self.total = [a[:, CHUNK - 1 :] for a in self.ahead]

    def levels(self):
        self.ahead_in = [{h: ahead_product(k, h) for h in HALVES} for k in self.keep]
        self.behind_in = [{h: behind_product(k, h) for h in HALVES} for k in self.keep]
        inside = (column(self.keep[0].shape) & (SUB - 1)) != 0
        self.short = [jnp.where(inside, k, 0.0) for k in self.keep]

    def from_start(self, c):
        out = self.ahead[c]
        for earlier in range(c):
            out = out * self.total[earlier]
        return out

    def to_end(self, c):
        out = self.behind[c]
        for later in range(c + 1, self.count):
            out = out * self.total[later]
        return out

    def to_chunk(self, c):
        parts = []
        for earlier in range(c):
            out = self.behind[earlier]
            for between in range(earlier + 1, c):
                out = out * self.total[between]
            parts.append(out)
        return parts

    def survive(self):
        out = self.total[0]
        for t in self.total[1:]:
            out = out * t
        return out


def level_mask(half):
    shape = (CHUNK, CHUNK)
    source, target = row(shape) // half, column(shape) // half
    return ((source & 1) == 0) & (target == source + 1)


def diagonals(square):
    shape = (SUB, CHUNK)
    group = column(shape) // SUB
    out = jnp.zeros(shape, F32)
    for b in range(CHUNK // SUB):
        out = out + jnp.where(group == b, square[b * SUB : (b + 1) * SUB], 0.0)
    return out


def at_lag(compact, lag):
    shape = (SUB, CHUNK)
    hit = row(shape) == (column(shape) & (SUB - 1)) - lag
    return jnp.sum(jnp.where(hit, compact, 0.0), axis=0, keepdims=True)


def undiagonal(lagged):
    shape = (SUB, CHUNK)
    place = (column(shape) & (SUB - 1)) - row(shape)
    compact = jnp.zeros(shape, F32)
    for lag, values in enumerate(lagged):
        compact = jnp.where(place == lag, values, compact)
    group = column(shape) // SUB
    return jnp.concatenate(
        [jnp.where(group == b, compact, 0.0) for b in range(CHUNK // SUB)], axis=0
    )


def read_slots(decays, written, c, affinity, entering, dot):
    near = affinity[c * CHUNK :]
    out = decays.from_start(c) * entering
    if c > 0:
        far = jnp.concatenate(
            [b * w for b, w in zip(decays.to_chunk(c), written[:c])], axis=1
        )
        out = out + decays.ahead[c] * dot(far, affinity[: c * CHUNK], NN)
    for h in HALVES:
        part = dot(decays.behind_in[c][h] * written[c], jnp.where(level_mask(h), near, 0.0), NN)
        out = out + decays.ahead_in[c][h] * part
    compact = diagonals(near)
    weight = written[c]
    for lag in range(SUB):
        out = out + weight * at_lag(compact, lag)
        if lag + 1 < SUB:
            weight = decays.short[c] * turn(weight, 1)
    return out


def mix_sources(decays, written, c, shares):
    lagged = [[] for _ in shares]
    weight = written[c]
    for lag in range(SUB):
        for place, share in enumerate(shares):
            lagged[place].append(jnp.sum(weight * share, axis=0, keepdims=True))
        if lag + 1 < SUB:
            weight = decays.short[c] * turn(weight, 1)
    outs = []
    for place, share in enumerate(shares):
        near = undiagonal(lagged[place])
        for h in HALVES:
            part = mm(decays.behind_in[c][h] * written[c], decays.ahead_in[c][h] * share, TN)
            near = near + jnp.where(level_mask(h), part, 0.0)
        if c > 0:
            far = jnp.concatenate(
                [b * w for b, w in zip(decays.to_chunk(c), written[:c])], axis=1
            )
            near = jnp.concatenate([mm(far, decays.ahead[c] * share, TN), near], axis=0)
        outs.append(near)
    return outs


def gather_back(decays, c, shares, affinities):
    outs = []
    if c > 0:
        pulled = sum(
            mm_fine(decays.ahead[c] * s, a[: c * CHUNK], NT) for s, a in zip(shares, affinities)
        )
        outs = [b * p for b, p in zip(decays.to_chunk(c), chunks_of(pulled))]
    nears = [a[c * CHUNK :] for a in affinities]
    own = 0.0
    for h in HALVES:
        mask = level_mask(h)
        pulled = sum(
            mm_fine(decays.ahead_in[c][h] * s, jnp.where(mask, a, 0.0), NT)
            for s, a in zip(shares, nears)
        )
        own = own + decays.behind_in[c][h] * pulled
    compacts = [diagonals(a) for a in nears]
    held = 0.0
    for lag in range(SUB - 1, -1, -1):
        if lag < SUB - 1:
            held = turn(decays.short[c] * held, -1)
        for s, a in zip(shares, compacts):
            held = held + s * at_lag(a, lag)
    outs.append(own + held)
    return outs


def silu(x):
    return x * jax.nn.sigmoid(x)


def silu_slope(x):
    sig = jax.nn.sigmoid(x)
    return sig * (1.0 + x * (1.0 - sig))


def piece_state(key_raw, value_raw, keep, written):
    decays = Decays(keep)
    left = jnp.concatenate(
        [decays.to_end(c) * w for c, w in enumerate(chunks_of(written))], axis=1
    )
    state = jnp.concatenate([mm(left, silu(key_raw), NN), mm(left, silu(value_raw), NN)], axis=1)
    return state, decays.survive()


def piece_read(query_raw, key_raw, value_raw, keep, written, slots_in):
    width = query_raw.shape[1]
    query, keys, values = silu(query_raw) * width**-0.5, silu(key_raw), silu(value_raw)
    slot_keys, slot_values = slots_in[:, :width], slots_in[:, width:]
    decays = Decays(keep)
    decays.levels()
    writes = chunks_of(written)
    entering = mm_fine(slot_keys, query, NT)
    readings, scores_all, shares = [], [], []
    for c in range(decays.count):
        last = (c + 1) * CHUNK
        affinity = mm_fine(keys[:last], query[c * CHUNK : last], NT)
        scores = read_slots(
            decays, writes, c, affinity, chunks_of(entering)[c], mm_fine
        )
        spread = jnp.exp(scores - jnp.max(scores, axis=0, keepdims=True))
        share = spread / jnp.sum(spread, axis=0, keepdims=True)
        (mixing,) = mix_sources(decays, writes, c, [share])
        reading = mm(mixing, values[:last], TN)
        reading = reading + mm(decays.from_start(c) * share, slot_values, TN)
        readings.append(reading)
        scores_all.append(scores)
        shares.append(share)
    return (
        jnp.concatenate(readings, axis=0),
        jnp.concatenate(scores_all, axis=1),
        jnp.concatenate(shares, axis=1),
    )


def add_chunks(total, extra):
    return [t + e for t, e in zip(total, extra)] + total[len(extra) :]


def piece_back(query_raw, key_raw, value_raw, keep, written, slots_in, scores, share, grad_read):
    width = query_raw.shape[1]
    query, keys, values = silu(query_raw) * width**-0.5, silu(key_raw), silu(value_raw)
    slot_keys, slot_values = slots_in[:, :width], slots_in[:, width:]
    decays = Decays(keep)
    decays.levels()
    writes = chunks_of(written)
    count = decays.count
    entering = chunks_of(mm_fine(slot_values, grad_read, NT))
    grad_q = []
    grad_k = [jnp.zeros((CHUNK, width), F32)] * count
    grad_v = [jnp.zeros((CHUNK, width), F32)] * count
    back = [jnp.zeros(writes[0].shape, F32)] * count
    direct_k, direct_v, own = 0.0, 0.0, []
    for c in range(count):
        last = (c + 1) * CHUNK
        here = slice(c * CHUNK, last)
        p = chunks_of(share)[c]
        affinity = mm_fine(keys[:last], query[here], NT)
        pull = mm_fine(values[:last], grad_read[here], NT)
        grad_p = read_slots(decays, writes, c, pull, entering[c], mm_fine)
        weighed = p * grad_p
        grad_s = weighed - p * jnp.sum(weighed, axis=0, keepdims=True)
        own.append(weighed + grad_s * chunks_of(scores)[c])
        mix_k, mix_v = mix_sources(decays, writes, c, [grad_s, p])
        from_start = decays.from_start(c)
        far_s, far_p = from_start * grad_s, from_start * p
        grad_q.append(mm(mix_k, keys[:last], TN) + mm(far_s, slot_keys, TN))
        grad_k = add_chunks(grad_k, rows_of(mm(mix_k, query[here], NN)))
        grad_v = add_chunks(grad_v, rows_of(mm(mix_v, grad_read[here], NN)))
        direct_k = direct_k + mm(far_s, query[here], NN)
        direct_v = direct_v + mm(far_p, grad_read[here], NN)
        back = add_chunks(back, gather_back(decays, c, [grad_s, p], [affinity, pull]))
    grad_query = jnp.concatenate(grad_q, axis=0) * width**-0.5 * silu_slope(query_raw)
    return (
        grad_query,
        jnp.concatenate(grad_k, axis=0),
        jnp.concatenate(grad_v, axis=0),
        jnp.concatenate([direct_k, direct_v], axis=1),
        jnp.concatenate(back, axis=1),
        jnp.concatenate(own, axis=1),
    )


def piece_after(
    key_raw, value_raw, keep, true_keep, written, grad_k, grad_v, back, own, after, slots_end
):
    width = key_raw.shape[1]
    keys, values = silu(key_raw), silu(value_raw)
    decays = Decays(keep)
    writes = chunks_of(written)
    to_end = jnp.concatenate([decays.to_end(c) for c in range(decays.count)], axis=1)
    left = to_end * written
    grad_k = grad_k + mm(left, after[:, :width], TN)
    grad_v = grad_v + mm(left, after[:, width:], TN)
    pulled = mm_fine(after[:, :width], keys, NT)
    pulled = pulled + mm_fine(after[:, width:], values, NT)
    back = back + to_end * pulled
    flow = own - written * back
    held = jnp.sum(after * slots_end, axis=1, keepdims=True)
    parts = chunks_of(flow)
    outs = []
    for part in reversed(parts):
        place, total, step = column(part.shape), part, 1
        while step < CHUNK:
            total = total + jnp.where(place < CHUNK - step, turn(total, -step), 0.0)
            step *= 2
        outs.append(total + held)
        held = held + total[:, :1]
    grad_log = jnp.concatenate(outs[::-1], axis=1) - true_keep * back
    return grad_k * silu_slope(key_raw), grad_v * silu_slope(value_raw), grad_log


def tie(value, *after):
    if not after:
        return value

    def body(*refs):
        pass

    anywhere = pl.BlockSpec(memory_space=pl.ANY)
    return pl.pallas_call(
        body,
        in_specs=[anywhere] * (1 + len(after)),
        out_specs=anywhere,
        out_shape=jax.ShapeDtypeStruct(value.shape, value.dtype),
        input_output_aliases={0: 0},
        cost_estimate=pl.CostEstimate(flops=0, bytes_accessed=0, transcendentals=0),
    )(value, *after)


def per_stream(work, arrays, outs, flops):
    def body(*refs):
        results = work(*[ref[...] for ref in refs[: len(arrays)]])
        for ref, result in zip(refs[len(arrays) :], results):
            ref[...] = result.astype(ref.dtype)

    def whole(shape):
        return pl.BlockSpec((None,) + tuple(shape[1:]), lambda s: (s, 0, 0))

    streams = arrays[0].shape[0]
    outs = [jax.ShapeDtypeStruct((streams,) + shape, kind) for shape, kind in outs]
    return pl.pallas_call(
        body,
        grid=(streams,),
        in_specs=[whole(a.shape) for a in arrays],
        out_specs=[whole(o.shape) for o in outs],
        out_shape=outs,
        compiler_params=pltpu.CompilerParams(vmem_limit_bytes=40 * 1024 * 1024),
        cost_estimate=pl.CostEstimate(flops=flops, bytes_accessed=1 << 16, transcendentals=0),
    )(*arrays)


def inverse_rms(values):
    return lax.rsqrt(jnp.mean(values * values, axis=-1, keepdims=True) + EPSILON)


def norm_back(values, scale, gain, grad):
    pulled = gain * grad
    along = jnp.mean(values * pulled, axis=-1, keepdims=True)
    return scale * pulled - values * (scale * scale * scale) * along


def product(left, right, dims):
    return lax.dot_general(left, right, (dims, ((), ())), preferred_element_type=F32)


def chain(earlier, later):
    return (earlier[0] * later[0], later[0][..., None] * earlier[1] + later[1])


CORE, X, Y, NEAR, FAR = 1, 2, 4, 8, 16


class Place:
    def __init__(self):
        self.seq, self.tp = lax.axis_index("seq"), lax.axis_index("tp")
        self.core, self.x = self.tp % 2, self.tp // 2
        self.y, self.z = self.seq % 2, self.seq // 2
        self.near, self.far = self.z % 2, self.z // 2
        self.flat = self.seq * 4 + self.tp

    def partner(self, mask):
        seq, tp = self.seq, self.tp
        if mask & CORE:
            tp = tp + 1 - 2 * self.core
        if mask & X:
            tp = tp + 2 - 4 * self.x
        if mask & Y:
            seq = seq + 1 - 2 * self.y
        if mask & NEAR:
            seq = seq + 2 - 4 * self.near
        if mask & FAR:
            seq = seq + 4 - 8 * self.far
        return seq, tp

    def z_turn(self, index):
        low, high = index % 2, index // 2
        low = low + self.near - 2 * low * self.near
        high = high + self.far - 2 * high * self.far
        return 2 * high + low


class Wire:
    def __init__(self, place, sends, receives, locals_):
        self.place, self.sends, self.receives, self.locals = place, sends, receives, locals_
        self.remote, self.near_by, self.seen = [], [], set()

    def greet(self, masks):
        barrier = pltpu.get_barrier_semaphore()
        for mask in masks:
            pl.semaphore_signal(
                barrier,
                inc=1,
                device_id=self.place.partner(mask),
                device_id_type=pl.DeviceIdType.MESH,
            )
        pl.semaphore_wait(barrier, len(masks))

    def send(self, source, target, mask):
        at = len(self.remote)
        copy = pltpu.make_async_remote_copy(
            src_ref=source,
            dst_ref=target,
            send_sem=self.sends.at[at],
            recv_sem=self.receives.at[at],
            device_id=self.place.partner(mask),
            device_id_type=pl.DeviceIdType.MESH,
        )
        copy.start()
        self.remote.append(copy)
        return ("remote", at)

    def keep(self, source, target):
        at = len(self.near_by)
        copy = pltpu.make_async_copy(source, target, self.locals.at[at])
        copy.start()
        self.near_by.append(copy)
        return ("local", at)

    def arrived(self, *handles):
        for handle in handles:
            if handle in self.seen:
                continue
            self.seen.add(handle)
            if handle[0] == "remote":
                self.remote[handle[1]].wait_recv()
            else:
                self.near_by[handle[1]].wait()

    def run(self, *tasks):
        live = [(task, next(task)) for task in tasks]
        while live:
            later = []
            for task, handles in live:
                self.arrived(*handles)
                try:
                    later.append((task, next(task)))
                except StopIteration:
                    pass
            live = later

    def finish(self):
        for at, copy in enumerate(self.remote):
            self.arrived(("remote", at))
            copy.wait_send()
        for at in range(len(self.near_by)):
            self.arrived(("local", at))


def comm_call(work, number, masks, arrays, in_vmem, outs, out_vmem, scratch, copies, stay, mb=48):
    def space(fast):
        return pl.BlockSpec(memory_space=pltpu.VMEM if fast else pl.ANY)

    def body(*refs):
        n, m = len(arrays), len(outs)
        place = Place()
        wire = Wire(place, *refs[-3:])
        wire.greet(masks)
        work(place, wire, refs[:n], refs[n : n + m], refs[n + m : -3])
        wire.finish()

    return pl.pallas_call(
        body,
        in_specs=[space(v) for v in in_vmem],
        out_specs=[space(v) for v in out_vmem],
        out_shape=[jax.ShapeDtypeStruct(shape, kind) for shape, kind in outs],
        scratch_shapes=list(scratch)
        + [
            pltpu.SemaphoreType.DMA((copies,)),
            pltpu.SemaphoreType.DMA((copies,)),
            pltpu.SemaphoreType.DMA((max(stay, 1),)),
        ],
        compiler_params=pltpu.CompilerParams(
            collective_id=number, has_side_effects=True, vmem_limit_bytes=mb * 1024 * 1024
        ),
        cost_estimate=pl.CostEstimate(flops=0, bytes_accessed=1 << 16, transcendentals=0),
    )(*arrays)


def head_gather(place, wire, weight, out):
    rows, width = weight.shape[0], out.shape[1]
    block = 4 * rows
    base = place.y * 4 * block

    def columns(tp):
        return weight.at[:, pl.ds(pl.multiple_of(tp * width, 128), width)]

    def part(m):
        return out.at[pl.ds(pl.multiple_of(base + m * block, 16), block)]

    own = out.at[pl.ds(pl.multiple_of(base + place.tp * rows, 16), rows)]
    handles = [wire.keep(columns(place.tp), own)]
    for mask in (X, X | CORE, CORE):
        handles.append(wire.send(columns(place.partner(mask)[1]), own, mask))
    yield handles
    far = wire.send(part(0), part(2), FAR)
    near = wire.send(part(0), part(1), NEAR)
    over = [wire.send(part(0), part(0), Y)]
    yield [far]
    last = wire.send(part(2), part(3), NEAR)
    over.append(wire.send(part(2), part(2), Y))
    yield [near]
    over.append(wire.send(part(1), part(1), Y))
    yield [last]
    over.append(wire.send(part(3), part(3), Y))
    yield over


def output_gather(place, wire, block, out):
    def part(m):
        return out.at[m, place.y]

    yield [wire.keep(block, part(0))]
    far = wire.send(part(0), part(2), FAR)
    near = wire.send(part(0), part(1), NEAR)
    over = [wire.send(part(0), part(0), Y)]
    yield [far]
    last = wire.send(part(2), part(3), NEAR)
    over.append(wire.send(part(2), part(2), Y))
    yield [near]
    over.append(wire.send(part(1), part(1), Y))
    yield [last]
    over.append(wire.send(part(3), part(3), Y))
    yield over


def ffn_trade(place, wire, halves, out):
    own = out.at[0, place.y]
    yield [
        wire.send(halves.at[1 - place.y], own, Y),
        wire.keep(halves.at[place.y], own),
    ]


def later(task, rounds):
    for unused in range(rounds):
        yield []
    yield from task


def ffn_gather(place, wire, halves, out, rounds):
    yield from ffn_trade(place, wire, halves, out)
    yield from later(ffn_spread(place, wire, None, out), rounds)


def ffn_spread(place, wire, block, out):
    start = out.at[0] if block is None else block
    stay = [] if block is None else [wire.keep(block, out.at[0])]
    far = wire.send(start, out.at[2], FAR)
    near = wire.send(start, out.at[1], NEAR)
    yield [far]
    last = wire.send(out.at[2], out.at[3], NEAR)
    yield [near, last] + stay


def rows_gather(place, wire, own, out):
    mine = out.at[:, place.tp]
    stay = wire.keep(own, mine)
    across = wire.send(own, mine, X)
    beside = wire.send(own, mine, CORE)
    yield [across]
    theirs = out.at[:, place.partner(X)[1]]
    yield [stay, beside, wire.send(theirs, theirs, CORE)]


def small_gather(place, wire, own, out):
    handles = [
        wire.keep(own, out.at[pl.ds(place.flat, 1)]),
        wire.send(own, out.at[pl.ds(place.flat, 1)], CORE),
    ]
    size = 2
    for mask in (X, Y, NEAR, FAR):
        yield handles
        part = out.at[pl.ds(place.flat // size * size, size)]
        handles = [wire.send(part, part, mask)]
        size *= 2
    yield handles


def plane_gather(place, wire, first, second, out):
    line_a = [out.at[0, 0, m] for m in range(4)]
    line_b = [out.at[0, 1, m] for m in range(4)]
    beside = []

    def pass_on(half, m):
        beside.append(wire.send(out.at[0, half, m], out.at[1, half, m], CORE))

    stay = [wire.keep(first, line_a[0]), wire.keep(second, line_b[0])]
    a_x = wire.send(first, line_a[1], X)
    b_y = wire.send(second, line_b[1], Y)
    a_y = wire.send(first, line_a[2], Y)
    b_x = wire.send(second, line_b[2], X)
    beside.append(wire.send(first, out.at[1, 0, 0], CORE))
    beside.append(wire.send(second, out.at[1, 1, 0], CORE))
    yield [a_x]
    a_xy = wire.send(line_a[1], line_a[3], Y)
    pass_on(0, 1)
    yield [b_y]
    b_xy = wire.send(line_b[1], line_b[3], X)
    pass_on(1, 1)
    yield [a_y, b_x]
    pass_on(0, 2)
    pass_on(1, 2)
    yield [a_xy, b_xy]
    pass_on(0, 3)
    pass_on(1, 3)
    yield stay + beside


def heads_trade(place, wire, branch, out):
    width = out.shape[1] // 4

    def columns(ref, index):
        return ref.at[:, pl.ds(pl.multiple_of(index * width, 128), width)]

    mine = columns(out, place.z_turn(place.tp))
    handles = [wire.keep(columns(branch, place.tp), mine)]
    for mask in (X, X | CORE, CORE):
        handles.append(wire.send(columns(branch, place.partner(mask)[1]), mine, mask))
    yield handles


def heads_return(place, wire, grads, out):
    width = out.shape[1] // 4

    def columns(ref, index):
        return ref.at[:, pl.ds(pl.multiple_of(index * width, 128), width)]

    mine = columns(out, place.tp)
    handles = [wire.keep(columns(grads, place.z_turn(place.tp)), mine)]
    for mask in (X, X | CORE, CORE):
        there = place.z_turn(place.partner(mask)[1])
        handles.append(wire.send(columns(grads, there), mine, mask))
    yield handles


def pieces_scan(place, wire, reverse, survive, state, out, bufs):
    send_s, send_b, got_s, got_b = bufs
    wide = state.shape[-1] // survive.shape[-1]
    total_s, total_b = survive[...], state[...]
    before_s = before_b = None

    def join(first_s, first_b, second_s, second_b):
        spread = jnp.concatenate([second_s] * wide, axis=-1)
        return first_s * second_s, spread * first_b + second_b

    for step, (mask, bit) in enumerate(((Y, place.y), (NEAR, place.near), (FAR, place.far))):
        send_s[step] = total_s
        send_b[step] = total_b.astype(BF)
        yield [
            wire.send(send_b.at[step], got_b.at[step], mask),
            wire.send(send_s.at[step], got_s.at[step], mask),
        ]
        other_s, other_b = got_s[step], got_b[step].astype(F32)
        later = bit == (0 if reverse else 1)
        if before_s is None:
            before_s = jnp.where(later, other_s, 1.0)
            before_b = jnp.where(later, other_b, 0.0)
        else:
            joined_s, joined_b = join(other_s, other_b, before_s, before_b)
            before_s = jnp.where(later, joined_s, before_s)
            before_b = jnp.where(later, joined_b, before_b)
        if mask != FAR:
            first_s, first_b = jnp.where(later, other_s, total_s), jnp.where(later, other_b, total_b)
            second_s = jnp.where(later, total_s, other_s)
            second_b = jnp.where(later, total_b, other_b)
            total_s, total_b = join(first_s, first_b, second_s, second_b)
    out[...] = before_b


def scan_buffers(state_shape, survive_shape):
    return [
        pltpu.VMEM((3,) + survive_shape, F32),
        pltpu.VMEM((3,) + state_shape, BF),
        pltpu.VMEM((3,) + survive_shape, F32),
        pltpu.VMEM((3,) + state_shape, BF),
    ]


def row_loop(count, step, work):
    def body(i, carry):
        work(pl.ds(pl.multiple_of(i * step, step), step))
        return carry

    lax.fori_loop(0, count // step, body, 0)


def hidden_rows(place, wire, mixed, tokens, gain, hidden, ready, sums, got_core, got_x):
    streams, count, width = tokens.shape
    other_x = 1 - place.x
    beside = [wire.send(mixed.at[s, :, 1 - place.core], got_core.at[s], CORE) for s in range(streams)]
    across = []
    for s in range(streams):
        yield [beside[s]]

        def to_send(rows, s=s):
            part = mixed[s, other_x, place.core, rows].astype(F32)
            sums[s, rows] = (part + got_core[s, other_x, rows].astype(F32)).astype(BF)

        row_loop(count, 16, to_send)
        across.append(wire.send(sums.at[s], got_x.at[s], X))
    for s in range(streams):
        yield [across[s]]

        def to_norm(rows, s=s):
            part = mixed[s, place.x, place.core, rows].astype(F32)
            part = part + got_core[s, place.x, rows].astype(F32) + got_x[s, rows].astype(F32)
            values = tokens[s, rows].astype(F32) + part
            hidden[s, rows] = values
            normed = (values * inverse_rms(values) * gain[...]).astype(BF)
            size = width // 4
            for m in range(4):
                there = pl.ds(pl.multiple_of(place.z_turn(m) * size, 128), size)
                ready[s, rows, there] = normed[:, m * size : (m + 1) * size]

        row_loop(count, 16, to_norm)


class Bits:
    CORE, X, Y, NEAR, FAR = 1, 2, 4, 8, 16

    def __init__(self):
        seq, tp = lax.axis_index("seq"), lax.axis_index("tp")
        self.core, self.x = tp & 1, tp >> 1
        self.y, self.z = seq & 1, seq >> 1

    def steps(self):
        return (
            (self.CORE, self.core),
            (self.X, self.x),
            (self.Y, self.y),
            (self.NEAR, self.z & 1),
            (self.FAR, self.z >> 1),
        )


def swap(values, mask):
    pairs = [(i, i ^ mask) for i in range(32)]
    return lax.ppermute(values, ("seq", "tp"), pairs)


def half(values, axis, which):
    size = values.shape[axis] // 2
    return lax.dynamic_slice_in_dim(values, which * size, size, axis)


def trade(values, mask, bit, axis, kind=None):
    other = half(values, axis, 1 - bit)
    if kind is not None:
        other = other.astype(kind)
    return half(values, axis, bit), swap(other, mask)


def in_order(mine, theirs, bit):
    first = bit == 0
    return jnp.where(first, mine, theirs), jnp.where(first, theirs, mine)


def z_blocks(block):
    far = swap(block, Bits.FAR)
    return [block, swap(block, Bits.NEAR), far, swap(far, Bits.NEAR)]


def z_fold(blocks, kind=BF):
    first = blocks[0] + swap(blocks[1].astype(kind), Bits.NEAR).astype(F32)
    second = blocks[2] + swap(blocks[3].astype(kind), Bits.NEAR).astype(F32)
    return first + swap(second.astype(kind), Bits.FAR).astype(F32)


def z_relative(values, z, axis):
    size = values.shape[axis] // 4
    return jnp.concatenate(
        [lax.dynamic_slice_in_dim(values, (m ^ z) * size, size, axis) for m in range(4)], axis
    )


def spread_tp(values, at):
    streams, count, width = values.shape
    pair = jnp.stack(in_order(values, swap(values, Bits.X), at.x), axis=1)
    both = jnp.stack(in_order(pair, swap(pair, Bits.CORE), at.core), axis=2)
    return both.reshape(streams, 4 * count, width)


def fold_tp(part, at):
    streams, count, width = part.shape
    parts = part.reshape(streams, 2, 2, count // 4, width)
    mine, got = trade(parts, Bits.CORE, at.core, 2, BF)
    mine, got = trade(mine + got.astype(F32), Bits.X, at.x, 1, BF)
    return (mine + got.astype(F32)).reshape(streams, count // 4, width)


def spread_plane(rows):
    count = rows.shape[0] // 2
    first, second = rows[:count], rows[count:]
    first = jnp.concatenate([first, swap(first, Bits.X)], axis=0)
    second = jnp.concatenate([second, swap(second, Bits.Y)], axis=0)
    four = [first, swap(first, Bits.Y), second, swap(second, Bits.X)]
    four = jnp.concatenate(four, axis=0)
    return jnp.concatenate([four, swap(four, Bits.CORE)], axis=0)


def fold_half(part, mask):
    size = part.shape[0] // 2
    return part[:size] + swap(part[size:].astype(BF), mask).astype(F32)


def fold_plane(work):
    sent = swap(work(1).astype(BF), Bits.CORE)
    part = work(0) + sent.astype(F32)
    size = part.shape[0] // 2
    first = fold_half(fold_half(part[:size], Bits.Y), Bits.X)
    second = fold_half(fold_half(part[size:], Bits.X), Bits.Y)
    return jnp.concatenate([first, second], axis=0)


def gather_head(weight, at):
    rows, width = weight.shape
    mine, got = trade(weight, Bits.X, at.x, 1)
    both = jnp.stack(in_order(mine, got, at.x), axis=0)
    mine, got = trade(both, Bits.CORE, at.core, 2)
    both = jnp.stack(in_order(mine, got, at.core), axis=1).reshape(4 * rows, width // 4)
    line = jnp.concatenate(z_blocks(both), axis=0)
    return jnp.concatenate(in_order(line, swap(line, Bits.Y), at.y), axis=0)


def fold_head(grad, at):
    mine, got = trade(grad, Bits.Y, at.y, 0, BF)
    line = mine + got.astype(F32)
    rows = line.shape[0] // 4
    own = z_fold([line[m * rows : (m + 1) * rows] for m in range(4)])
    width = own.shape[1]
    own = own.reshape(2, 2, rows // 4, width)
    mine, got = trade(own, Bits.CORE, at.core, 1, BF)
    own = jnp.concatenate(in_order(mine, got.astype(F32), at.core), axis=-1)
    mine, got = trade(own, Bits.X, at.x, 0, BF)
    own = jnp.concatenate(in_order(mine, got.astype(F32), at.x), axis=-1)
    return own.reshape(rows // 4, 4 * width)


def turn_bits(values, back):
    pairs = []
    for i in range(32):
        z, y, x, core = i >> 3, (i >> 2) & 1, (i >> 1) & 1, i & 1
        there = z * 8 + core * 4 + y * 2 + x
        pairs.append((there, i) if back else (i, there))
    return lax.ppermute(values, ("seq", "tp"), pairs)


def gather_output(weight, at):
    block = turn_bits(weight, False)
    line = jnp.stack(z_blocks(block), axis=0)
    both = jnp.stack(in_order(line, swap(line, Bits.Y), at.y), axis=1)
    return both.reshape(8 * weight.shape[0], weight.shape[1])


def fold_output(grad, at):
    rows, width = grad.shape
    parts = grad.reshape(4, 2, rows // 8, width)
    mine, got = trade(parts, Bits.Y, at.y, 1, BF)
    line = (mine + got.astype(F32)).reshape(4, rows // 8, width)
    own = z_fold([line[m] for m in range(4)])
    return turn_bits(own.astype(BF), True).astype(F32)


def heads_to_rows(values, at):
    mine, got = trade(values, Bits.X, at.x, 1)
    both = jnp.stack(in_order(mine, got, at.x), axis=0)
    mine, got = trade(both, Bits.CORE, at.core, 2)
    both = jnp.stack(in_order(mine, got, at.core), axis=1)
    parts = both.reshape((4,) + both.shape[2:])
    return jnp.concatenate(
        [lax.dynamic_index_in_dim(parts, m ^ at.z, 0, False) for m in range(4)], axis=1
    )


def rows_to_heads(values, at):
    width = values.shape[1] // 4
    parts = jnp.stack(
        [
            lax.dynamic_slice_in_dim(values, (m ^ at.z) * width, width, 1)
            for m in range(4)
        ],
        axis=0,
    ).reshape(2, 2, values.shape[0], width)
    mine, got = trade(parts, Bits.X, at.x, 0)
    first, second = in_order(mine[0], got[0], at.x)
    both = jnp.stack([first, second], axis=0)
    mine, got = trade(both, Bits.CORE, at.core, 1)
    first, second = in_order(mine[:, 0], got[:, 0], at.core)
    both = jnp.stack([first, second], axis=1)
    return jnp.concatenate([both[0, 0], both[0, 1], both[1, 0], both[1, 1]], axis=1)


class FfnGather:
    def __init__(self, weight, at):
        mine, got = trade(weight, Bits.Y, at.y, 1)
        self.block = jnp.concatenate(in_order(mine, got, at.y), axis=0)

    def far(self, *after):
        self.block = tie(self.block, *after)
        self.far_block = swap(self.block, Bits.FAR)
        return (self.far_block,)

    def near(self, *after):
        self.block = tie(self.block, *after)
        self.near_block = swap(self.block, Bits.NEAR)
        self.last_block = swap(self.far_block, Bits.NEAR)
        return (self.near_block, self.last_block)

    def whole(self):
        parts = [self.block, self.near_block, self.far_block, self.last_block]
        return jnp.concatenate(parts, axis=0)


class FfnFold:
    def __init__(self, grad, at):
        self.at = at
        rows = grad.shape[0] // 4
        self.parts = [grad[m * rows : (m + 1) * rows] for m in range(4)]

    def near(self, *after):
        sent = [tie(self.parts[1].astype(BF), *after), self.parts[3].astype(BF)]
        self.got = [swap(s, Bits.NEAR) for s in sent]
        return tuple(self.got)

    def far(self, *after):
        second = self.parts[2] + self.got[1].astype(F32)
        self.last = swap(tie(second.astype(BF), *after), Bits.FAR)
        return (self.last,)

    def whole(self):
        own = self.parts[0] + self.got[0].astype(F32) + self.last.astype(F32)
        mine, got = trade(own, Bits.Y, self.at.y, 0, BF)
        return jnp.concatenate(in_order(mine, got.astype(F32), self.at.y), axis=1)


class PlainWhole:
    def __init__(self, value):
        self.value = value

    def far(self, *after):
        return ()

    near = far

    def whole(self):
        return self.value


def spread_all(values, at):
    for mask, bit in at.steps():
        values = jnp.concatenate(in_order(values, swap(values, mask), bit), axis=0)
    return values


def fold_all(values, at):
    for mask, bit in reversed(at.steps()):
        mine, got = trade(values, mask, bit, 0)
        values = mine + got
    return values


def scan_pieces(part, at, reverse):
    total, before = part, None
    steps = ((Bits.Y, at.y), (Bits.NEAR, at.z & 1), (Bits.FAR, at.z >> 1))
    for mask, bit in steps:
        other = (swap(total[0], mask), swap(total[1].astype(BF), mask).astype(F32))
        later = bit == (0 if reverse else 1)
        if before is None:
            before = (
                jnp.where(later, other[0], 1.0),
                jnp.where(later, other[1], 0.0),
            )
        else:
            joined = chain(other, before)
            before = tuple(jnp.where(later, a, b) for a, b in zip(joined, before))
        if mask != Bits.FAR:
            first = tuple(jnp.where(later, o, t) for o, t in zip(other, total))
            second = tuple(jnp.where(later, t, o) for o, t in zip(other, total))
            total = chain(first, second)
    return before


class Plain:
    def __init__(self):
        self.seq, self.tp = lax.axis_index("seq"), lax.axis_index("tp")
        self.seq_count, self.tp_count = lax.axis_size("seq"), lax.axis_size("tp")
        self.sharing = self.tp_count // H
        self.head, self.member = self.tp // self.sharing, self.tp % self.sharing


def plain_scan(part, at, reverse):
    gathered = (
        lax.all_gather(part[0], "seq"),
        lax.all_gather(part[1].astype(BF), "seq"),
    )
    state = (jnp.ones_like(part[0]), jnp.zeros_like(part[1]))

    def step(count, state):
        source = at.seq_count - 1 - count if reverse else count
        piece = tuple(lax.dynamic_index_in_dim(a, source, 0, False) for a in gathered)
        return chain(state, (piece[0], piece[1].astype(F32)))

    steps = at.seq_count - 1 - at.seq if reverse else at.seq
    return lax.fori_loop(0, steps, step, state)


class PlainMoves:
    def small(self, packed):
        return lax.all_gather(packed, ("seq", "tp"))

    def small_sum(self, packed):
        return lax.psum_scatter(packed, ("seq", "tp"), scatter_dimension=0, tiled=True)[0]

    def begin(self, packed, tokens, weights, w_output, ffn):
        self.weights, self.w_output, self.ffn = weights, w_output, ffn
        return self.small(packed), self.piece(tokens), [self.head_weight(w) for w in weights[:2]]

    def scan_in(self, survive, state):
        weights = [self.head_weight(w) for w in self.weights[2:]]
        return self.scan((survive, state), False)[1], weights, self.output_weight(self.w_output)

    def hidden(self, mixed, tokens, gain, cotangent):
        streams, count, width = tokens.shape
        hidden = tokens.astype(F32) + self.sum_piece(mixed)
        hidden = hidden.reshape(streams * count, width)
        ready = (hidden * inverse_rms(hidden) * gain).astype(BF)
        cot = self.ffn_rows(cotangent.reshape(streams * count, width))
        return hidden, self.ffn_rows(ready), cot

    def ffn_weights(self):
        return [lax.all_gather(w, "seq", axis=0, tiled=True) for w in self.ffn]

    def __init__(self):
        self.at = Plain()
        self.head, self.member = self.at.head, self.at.member

    def own_streams(self, values):
        count = values.shape[0] // self.at.sharing
        return lax.dynamic_slice_in_dim(values, self.member * count, count, 0)

    def piece(self, own):
        return self.own_streams(lax.all_gather(own, "tp", axis=1, tiled=True))

    def sum_piece(self, part):
        streams = part.shape[0] * self.at.sharing
        entire = jnp.zeros((streams,) + part.shape[1:], BF)
        entire = lax.dynamic_update_slice_in_dim(
            entire, part.astype(BF), self.member * part.shape[0], 0
        )
        own = lax.psum_scatter(entire, "tp", scatter_dimension=1, tiled=True)
        return own.astype(F32)

    def mixer_order(self, values):
        return values

    mixer_unorder = ffn_order = ffn_unorder = mixer_order

    def head_weight(self, weight):
        entire = lax.all_gather(weight, ("seq", "tp"), axis=0, tiled=True)
        width = entire.shape[1] // H
        return lax.dynamic_slice_in_dim(entire, self.head * width, width, 1)

    def head_grad(self, grad):
        entire = jnp.zeros((grad.shape[0], grad.shape[1] * H), BF)
        entire = lax.dynamic_update_slice_in_dim(
            entire, grad.astype(BF), self.head * grad.shape[1], 1
        )
        own = lax.psum_scatter(entire, ("seq", "tp"), scatter_dimension=0, tiled=True)
        return own.astype(F32)

    def output_weight(self, weight):
        entire = lax.all_gather(weight, ("seq", "tp"), axis=0, tiled=True)
        rows = entire.shape[0] // H
        return lax.dynamic_slice_in_dim(entire, self.head * rows, rows, 0)

    def output_grad(self, grad):
        entire = jnp.zeros((grad.shape[0] * H, grad.shape[1]), BF)
        entire = lax.dynamic_update_slice_in_dim(
            entire, grad.astype(BF), self.head * grad.shape[0], 0
        )
        own = lax.psum_scatter(entire, ("seq", "tp"), scatter_dimension=0, tiled=True)
        return own.astype(F32)

    def to_output(self, branch):
        return branch

    def from_output(self, grad):
        return grad

    def scan(self, part, reverse):
        return plain_scan(part, self.at, reverse)

    def ffn_rows(self, own):
        entire = lax.all_gather(own, "tp", axis=0)
        return entire.reshape((-1,) + own.shape[1:])

    def ffn_sum(self, work):
        part = jnp.concatenate([work(0), work(1)], axis=0)
        parts = part.reshape((self.at.tp_count, -1) + part.shape[1:])
        own = lax.psum_scatter(parts.astype(BF), "tp", scatter_dimension=0, tiled=True)
        return own.reshape((-1,) + part.shape[1:]).astype(F32)

    def ffn_weight(self, weight):
        return PlainWhole(lax.all_gather(weight, "seq", axis=0, tiled=True))

    def ffn_grad(self, grad):
        own = lax.psum_scatter(grad.astype(BF), "seq", scatter_dimension=0, tiled=True)
        return PlainWhole(own.astype(F32))

    def tie(self, value, *after):
        return value


class BitMoves:
    def __init__(self):
        self.at = Bits()
        self.head, self.member = lax.axis_index("tp"), 0

    def begin(self, packed, tokens, weights, w_output, ffn):
        block = turn_bits(w_output, False)
        streams, count, width = tokens.shape
        length = -(-packed.size // 2048) * 16
        own = jnp.pad(packed, (0, length * 128 - packed.size)).reshape(1, length, 128)
        self.rest, self.block = weights[2:], block
        self.halves = [jnp.swapaxes(w.reshape(w.shape[0], 2, -1), 0, 1) for w in ffn]
        ffn_shape = (4,) + self.halves[0].shape
        head = (weights[0].shape[0] * 32, width // 4)

        def work(place, wire, given, outs, scratch):
            wire.run(
                small_gather(place, wire, given[0], outs[0]),
                head_gather(place, wire, given[2], outs[2]),
                head_gather(place, wire, given[3], outs[3]),
                rows_gather(place, wire, given[1], outs[1]),
                ffn_gather(place, wire, given[4], outs[4], 2),
            )

        small, rows, key_w, value_w, self.down = comm_call(
            work,
            1,
            (CORE, X, X | CORE, Y, NEAR, FAR),
            [own, self.mixer_order(tokens), weights[0], weights[1], self.halves[0]],
            [False] * 5,
            [
                ((32, length, 128), BF),
                ((streams, 4, count, width), BF),
                (head, BF),
                (head, BF),
                (ffn_shape, BF),
            ],
            [False] * 5,
            [],
            40,
            8,
        )
        small = small.reshape(32, length * 128)[:, : packed.size]
        return small, rows.reshape(streams, 4 * count, width), [key_w, value_w]

    def scan_in(self, survive, state):
        streams, slots, width = state.shape
        head = (self.rest[0].shape[0] * 32, self.rest[0].shape[1] // 4)
        rows = self.block.shape
        spread = jnp.broadcast_to(survive[..., None], (streams, slots, 128))

        def work(place, wire, given, outs, scratch):
            wire.run(
                pieces_scan(place, wire, False, given[0], given[1], outs[0], scratch),
                head_gather(place, wire, given[2], outs[1]),
                head_gather(place, wire, given[3], outs[2]),
                output_gather(place, wire, given[4], outs[3]),
                ffn_gather(place, wire, given[5], outs[4], 2),
                ffn_trade(place, wire, given[6], outs[5]),
            )

        ffn_shape = (4,) + self.halves[0].shape
        slots_in, query_w, gate_w, output_w, self.gate, self.up = comm_call(
            work,
            2,
            (CORE, X, X | CORE, Y, NEAR, FAR),
            [spread, state] + list(self.rest) + [self.block] + self.halves[1:],
            [True, True] + [False] * 5,
            [
                (state.shape, F32),
                (head, BF),
                (head, BF),
                ((4, 2) + rows, BF),
                (ffn_shape, BF),
                (ffn_shape, BF),
            ],
            [True] + [False] * 5,
            scan_buffers(state.shape, spread.shape),
            60,
            8,
        )
        return slots_in, [query_w, gate_w], output_w.reshape(8 * rows[0], rows[1])

    def hidden(self, mixed, tokens, gain, cotangent):
        streams, count, width = tokens.shape
        cot = self.ffn_order(cotangent)
        plane = (2, 2, 4, count, width)

        def work(place, wire, given, outs, scratch):
            ready, sums, got_core, got_x = scratch
            rows = hidden_rows(
                place, wire, given[0], given[1], given[2], outs[0], ready, sums, got_core, got_x
            )

            def then():
                yield from rows
                yield from plane_gather(place, wire, ready.at[0], ready.at[1], outs[1])

            wire.run(
                then(),
                ffn_spread(place, wire, given[4].at[0], outs[3]),
                plane_gather(place, wire, given[3].at[0], given[3].at[1], outs[2]),
            )

        hidden, ready, cot, self.up = comm_call(
            work,
            3,
            (CORE, X, Y, NEAR, FAR),
            [mixed.reshape(streams, 2, 2, count, width), tokens, gain[None], cot, self.up],
            [True, True, True, False, False],
            [
                ((streams, count, width), F32),
                (plane, BF),
                (plane, BF),
                (self.up.shape, BF),
            ],
            [True, False, False, False],
            [
                pltpu.VMEM((streams, count, width), BF),
                pltpu.VMEM((streams, count, width), BF),
                pltpu.VMEM((streams, 2, count, width), BF),
                pltpu.VMEM((streams, count, width), BF),
            ],
            60,
            8,
        )
        flat = 16 * count
        return (
            hidden.reshape(streams * count, width),
            ready.reshape(flat, width),
            cot.reshape(flat, width),
        )

    def ffn_weights(self):
        return [w.reshape(-1, w.shape[-1]) for w in (self.down, self.gate, self.up)]

    def small_sum(self, packed):
        return fold_all(packed, self.at)[0]

    def own_streams(self, values):
        return values

    def piece(self, own):
        return spread_tp(own, self.at)

    def sum_piece(self, part):
        return fold_tp(part, self.at)

    def mixer_order(self, values):
        lead, width = values.shape[:-1], values.shape[-1]
        parts = jnp.swapaxes(values.reshape(lead + (4, 2, width // 8)), -3, -2)
        return z_relative(parts, self.at.z, len(lead) + 1).reshape(lead + (width,))

    def mixer_unorder(self, values):
        lead, width = values.shape[:-1], values.shape[-1]
        parts = z_relative(values.reshape(lead + (2, 4, width // 8)), self.at.z, len(lead) + 1)
        return jnp.swapaxes(parts, -3, -2).reshape(lead + (width,))

    def ffn_order(self, values):
        return z_relative(values, self.at.z, values.ndim - 1)

    ffn_unorder = ffn_order

    def head_weight(self, weight):
        return gather_head(weight, self.at)

    def head_grad(self, grad):
        return fold_head(grad, self.at)

    def output_weight(self, weight):
        return gather_output(weight, self.at)

    def output_grad(self, grad):
        return fold_output(grad, self.at)

    def to_output(self, branch):
        def work(place, wire, given, outs, scratch):
            wire.run(heads_trade(place, wire, given[0], outs[0]))

        (out,) = comm_call(
            work,
            4,
            (CORE, X, X | CORE),
            [branch],
            [False],
            [(branch.shape, BF)],
            [False],
            [],
            4,
            1,
        )
        return out

    def from_output(self, grad):
        return rows_to_heads(grad, self.at)

    def scan(self, part, reverse):
        return scan_pieces(part, self.at, reverse)

    def ffn_rows(self, own):
        return spread_plane(own)

    def ffn_sum(self, work):
        return fold_plane(work)

    def ffn_weight(self, weight):
        return FfnGather(weight, self.at)

    def ffn_grad(self, grad):
        return FfnFold(grad, self.at)

    def tie(self, value, *after):
        return tie(value, *after)


def on_device(
    tokens,
    seq_cuts,
    w_query,
    w_key,
    w_value,
    w_gate_out,
    w_output,
    w_low,
    w_rank,
    gate_bias,
    attn_gain,
    out_gain,
    ffn_gain,
    w_gate,
    w_up,
    w_down,
    cotangent,
):
    seq_count, tp_count = lax.axis_size("seq"), lax.axis_size("tp")
    devices = seq_count * tp_count
    seq_rank = lax.axis_index("seq")
    move = BitMoves() if (seq_count, tp_count) == (8, 4) else PlainMoves()
    streams, local_len, width = tokens.shape
    rank = w_low.shape[1]

    small = (w_low, w_rank, gate_bias, attn_gain, out_gain, ffn_gain)
    packed = jnp.concatenate([a.reshape(-1) for a in small])
    gathered, rows_in, (key_w, value_w) = move.begin(
        packed, tokens, (w_key, w_value, w_query, w_gate_out), w_output, (w_down, w_gate, w_up)
    )
    unpacked, taken = [], 0
    for a in small:
        part = gathered[:, taken : taken + a.size]
        unpacked.append(part.reshape((devices * a.shape[0],) + a.shape[1:]))
        taken += a.size
    full_low, full_rank, full_bias, full_attn, full_out, full_ffn = unpacked
    slots = full_bias.shape[0] // H
    head_rank = lax.dynamic_slice_in_dim(full_rank, move.head * slots, slots, 0).astype(F32)
    head_bias = lax.dynamic_slice_in_dim(full_bias, move.head * slots, slots, 0).astype(F32)
    attn_vec, ffn_vec = full_attn.astype(F32), full_ffn.astype(F32)
    out_vec = full_out.astype(F32)
    order_low = jnp.swapaxes(move.mixer_order(jnp.swapaxes(full_low, 0, 1)), 0, 1)

    held, piece_len = rows_in.shape[:2]
    flat = held * piece_len
    positions = seq_rank * piece_len + jnp.arange(piece_len)
    cuts = move.own_streams(seq_cuts)
    starts = (positions[None, :] == 0) | (positions[None, :] == cuts[:, None])
    inputs = rows_in.reshape(flat, width).astype(F32)
    attn_scale = inverse_rms(inputs)
    normed = (inputs * attn_scale * move.mixer_order(attn_vec)).astype(BF)
    low_rank = product(normed, order_low, NN)
    logits = lax.dot_general(
        head_rank,
        low_rank.reshape(held, piece_len, rank),
        (((1,), (2,)), ((), ())),
        precision=lax.Precision.HIGHEST,
    )
    logits = jnp.swapaxes(logits, 0, 1) + head_bias[None, :, None]
    log_keep = jax.nn.log_sigmoid(logits) / GATE_SCALE
    true_keep, written = jnp.exp(log_keep), -jnp.expm1(log_keep)
    keep = jnp.where(starts[:, None, :], 0.0, true_keep)

    def project(weight):
        out = product(normed, weight, NN)
        return out.reshape(held, piece_len, weight.shape[1])

    key_rows, value_rows = project(key_w), project(value_w)
    hd = key_rows.shape[-1]
    gflop = 1000 * 1000 * 1000
    state, survive = per_stream(
        piece_state,
        [key_rows, value_rows, keep, written],
        [((slots, 2 * hd), F32), ((slots, 1), F32)],
        gflop,
    )
    survive = survive[..., 0]
    slots_in, (query_w, gate_w), output_w = move.scan_in(survive, state)
    query, gate_out = project(query_w), project(gate_w)
    slots_end = survive[..., None] * slots_in + state
    reading, scores, share = per_stream(
        piece_read,
        [query, key_rows, value_rows, keep, written, slots_in],
        [
            ((piece_len, hd), F32),
            ((slots, piece_len), F32),
            ((slots, piece_len), F32),
        ],
        gflop,
    )
    read_scale = inverse_rms(reading)
    gate_act = silu(gate_out)
    read_normed = reading * read_scale * out_vec
    branch = (read_normed * gate_act).astype(BF).reshape(flat, hd)
    branch_out = move.to_output(branch)
    mixed = product(branch_out, output_w, NN).reshape(held, piece_len, width)
    own_tokens = tokens.astype(F32)
    own_rows = streams * local_len
    hidden, ffn_in, cot_all = move.hidden(mixed.astype(BF), tokens, ffn_vec, cotangent)
    ffn_down, ffn_gate, ffn_up = move.ffn_weights()

    ffn_scale = inverse_rms(hidden)
    grad_product = product(cot_all, ffn_down, NN)
    gate_pre = product(ffn_in, ffn_gate, NN)
    up_pre = product(ffn_in, ffn_up, NN)
    gate_sig = jax.nn.sigmoid(gate_pre)
    product_in = (gate_pre * gate_sig * up_pre).astype(BF)
    slope = gate_sig * (1.0 + gate_pre * (1.0 - gate_sig))
    grad_gate_pre = (grad_product * up_pre * slope).astype(BF)
    grad_up_pre = (grad_product * gate_pre * gate_sig).astype(BF)
    half_rows = grad_gate_pre.shape[0] // 2

    def grad_ffn_half(which):
        here = slice(which * half_rows, (which + 1) * half_rows)
        part = product(grad_gate_pre[here], ffn_gate, NT)
        return part + product(grad_up_pre[here], ffn_up, NT)

    grad_ffn_in = move.ffn_unorder(move.ffn_sum(grad_ffn_half))
    gate_fold = move.ffn_grad(product(ffn_in, grad_gate_pre, TN))
    up_fold = move.ffn_grad(product(ffn_in, grad_up_pre, TN))
    down_fold = move.ffn_grad(product(cot_all, product_in, TN))
    moved = gate_fold.near()
    grad_ffn_in = move.tie(grad_ffn_in, *moved)
    moved = gate_fold.far(grad_ffn_in) + up_fold.near(grad_ffn_in)

    def ffn_out_half(which):
        here = slice(which * half_rows, (which + 1) * half_rows)
        return product(product_late[here], ffn_down, NT)

    product_late = move.tie(product_in, grad_ffn_in)
    ffn_out = move.ffn_unorder(move.ffn_sum(ffn_out_half))
    result = (hidden + ffn_out).astype(BF).reshape(tokens.shape)
    grad_ffn_gain = jnp.sum(grad_ffn_in * hidden * ffn_scale, axis=0)
    grad_hidden = cotangent.reshape(own_rows, width).astype(F32)
    grad_hidden = grad_hidden + norm_back(hidden, ffn_scale, ffn_vec, grad_ffn_in)

    grad_mixed = move.piece(grad_hidden.astype(BF).reshape(tokens.shape)).reshape(flat, width)
    grad_branch_out = product(grad_mixed, output_w, NT).astype(BF)
    grad_branch = move.from_output(grad_branch_out).astype(F32).reshape(held, piece_len, hd)
    grad_w_output = move.output_grad(product(branch_out, grad_mixed, TN))
    grad_gate_rounded = (grad_branch * read_normed * silu_slope(gate_out)).astype(BF)
    grad_read_normed = grad_branch * gate_act
    grad_out_gain = jnp.sum(grad_read_normed * reading * read_scale, axis=(0, 1))
    grad_reading = norm_back(reading, read_scale, out_vec, grad_read_normed)
    grad_reading = move.tie(grad_reading, *moved)
    moved = up_fold.far(grad_reading) + down_fold.near(grad_reading)
    grad_query, grad_k, grad_v, direct, back, own = per_stream(
        piece_back,
        [query, key_rows, value_rows, keep, written, slots_in, scores, share, grad_reading],
        [
            ((piece_len, hd), BF),
            ((piece_len, hd), F32),
            ((piece_len, hd), F32),
            ((slots, 2 * hd), F32),
            ((slots, piece_len), F32),
            ((slots, piece_len), F32),
        ],
        gflop,
    )
    unused, after = move.scan((survive, direct), True)
    after = move.tie(after, *moved)
    down_fold.far(after)
    grad_key, grad_value, grad_log = per_stream(
        piece_after,
        [
            key_rows,
            value_rows,
            keep,
            true_keep,
            written,
            grad_k,
            grad_v,
            back,
            own,
            after,
            slots_end,
        ],
        [((piece_len, hd), BF), ((piece_len, hd), BF), ((slots, piece_len), F32)],
        gflop,
    )
    grad_f = grad_log * jax.nn.sigmoid(-logits) / GATE_SCALE
    grad_bias = jnp.sum(grad_f, axis=(0, 2))
    low_pieces = low_rank.reshape(held, piece_len, rank)
    highest = lax.Precision.HIGHEST
    grad_rank = jnp.einsum("smt,str->mr", grad_f, low_pieces, precision=highest)
    grad_low_rank = jnp.einsum("smt,mr->str", grad_f, head_rank, precision=highest)
    grad_low_rank = grad_low_rank.reshape(flat, rank)
    grads = [g.reshape(flat, hd) for g in (grad_query, grad_key, grad_value, grad_gate_rounded)]
    grad_normed = sum(
        product(g, w, NT) for g, w in zip(grads, (query_w, key_w, value_w, gate_w))
    )
    grad_normed = grad_normed + product(grad_low_rank, order_low.astype(F32), NT)
    grad_normed = move.sum_piece(grad_normed.reshape(held, piece_len, width))
    grad_normed = move.mixer_unorder(grad_normed)
    own_scale = inverse_rms(own_tokens)
    grad_tokens = grad_hidden.reshape(tokens.shape)
    grad_tokens = grad_tokens + norm_back(own_tokens, own_scale, attn_vec, grad_normed)
    grad_attn_gain = jnp.sum(grad_normed * own_tokens * own_scale, axis=(0, 1))
    grad_w_query, grad_w_key, grad_w_value, grad_w_gate_out = (
        move.head_grad(product(normed, g, TN)) for g in grads
    )
    grad_low = product(grad_low_rank, normed.astype(F32), TN)
    grad_low = jnp.swapaxes(move.mixer_unorder(grad_low), 0, 1)

    def placed(part):
        entire = jnp.zeros((part.shape[0] * H,) + part.shape[1:], F32)
        return lax.dynamic_update_slice_in_dim(entire, part, move.head * part.shape[0], 0)

    sums = (
        grad_low,
        placed(grad_rank),
        placed(grad_bias),
        grad_attn_gain,
        grad_out_gain,
        grad_ffn_gain,
    )
    packed = jnp.concatenate([a.reshape(devices, -1) for a in sums], axis=1)
    own_sums = move.small_sum(packed)
    small_grads, taken = [], 0
    for a in small:
        small_grads.append(own_sums[taken : taken + a.size].reshape(a.shape))
        taken += a.size
    return (
        (result, grad_tokens)
        + (grad_w_query, grad_w_key, grad_w_value, grad_w_gate_out, grad_w_output)
        + tuple(small_grads)
        + (gate_fold.whole(), up_fold.whole(), down_fold.whole())
    )


def solution(mesh):
    both, row_split, line = ("seq", "tp"), P(("seq", "tp"), None), P(("seq", "tp"))
    tokens_at, ffn_at = P(None, both, None), P("seq", "tp")
    params = (row_split,) * 7 + (line,) * 4 + (ffn_at,) * 3
    return jax.shard_map(
        on_device,
        mesh=mesh,
        in_specs=(tokens_at, P()) + params + (tokens_at,),
        out_specs=(tokens_at, tokens_at) + params,
        check_vma=False,
    )
```

time: 2970 us -> 1070 us (0.36)
  matrix products: 1060 us -> 147 us
  waiting for transfers between devices: 752 us -> 177 us
  Pallas kernels: 0 us -> 363 us
  other arithmetic: 476 us -> 125 us
  local copies, waits for them, and re-layouts: 408 us -> 177 us
  blocking collectives: 217 us -> 0 us
  starting transfers between devices: 0.92 us -> 66.6 us
    dot_general x342 -> x33, matrix products: 1060 us -> 147 us  [the longest x30 143 us: product(): lax.dot_general(left, right, (dims, ((), ())), preferred_element_type=F32)]
    reduce_scatter x9 -> x0, waiting for transfers between devices: 369 us -> none  [the longest x1 112 us: on_device(): lax.psum_scatter(grad_w_down.astype(jnp.bfloat16), 'seq', scatter_dimensi...]
    pallas_call x0 -> x17, Pallas kernels: none -> 363 us  [the longest x4 334 us: comm_call(): pl.pallas_call(body, in_specs=[space(v) for v in in_vmem], out_specs=[spa...]
    all_gather x12 -> x0, waiting for transfers between devices: 296 us -> none  [the longest x1 213 us: entering(): gathered = jax.tree.map(lambda a: lax.all_gather(a, axis), part)]
    squeeze x168 -> x0, local copies, waits for them, and re-layouts: 232 us -> none  [the longest x144 155 us: transition(): lax.scan(jax.checkpoint(carry_scan), slots_zero, pieces)]
    ppermute x0 -> x68, waiting for transfers between devices: none -> 177 us  [the longest x66 177 us: swap(): return lax.ppermute(values, ('seq', 'tp'), pairs)]
    reduce_sum x56 -> x8, other arithmetic: 152 us -> 8.49 us  [the longest x4 4.13 us: inverse_rms(): jnp.mean(values * values, axis=-1, keepdims=True) + EPSILON]
    all_gather x4 -> x0, blocking collectives: 138 us -> none  [the longest x1 41.4 us: on_device(): lax.all_gather(mixer_local[5], ('seq', 'tp'), axis=0, tiled=True)]
  transfers between devices with their start and end apart: 23 -> 68, of which waited for: 10 -> 33; matrix products, arithmetic and copies ran while one was open for 35% -> 32% of each run, Pallas kernels for 0% -> 11%
where the time goes in v1:
time: 1070 us; the launch traced here: 1060 us
  Pallas kernels  363 us (34%)
  local copies, waits for them, and re-layouts  177 us (17%)
  waiting for transfers between devices  177 us (17%)
  matrix products  147 us (14%)
  other arithmetic  125 us (12%)
  starting transfers between devices  66.6 us (6%)
    pallas_call x4, Pallas kernels, comm_call(): pl.pallas_call(body, in_specs=[space(v) for v in in_vmem], out_specs=[spa...  334 us
    ppermute x66, waiting for transfers between devices, swap(): return lax.ppermute(values, ('seq', 'tp'), pairs)  177 us
    dot_general x30, matrix products, product(): lax.dot_general(left, right, (dims, ((), ())), preferred_element_type=F32)  143 us
    ppermute x66, starting transfers between devices, swap(): return lax.ppermute(values, ('seq', 'tp'), pairs)  59.4 us
    unnamed x315, local copies, waits for them, and re-layouts  57.3 us
    another operation x8, other arithmetic  30.4 us
    pallas_call x4, Pallas kernels, per_stream(): pl.pallas_call(body, grid=(streams,), in_specs=[whole(a.shape) for a in a...  28.6 us
  transfers between devices with their start and end apart: 68, of which 33 were waited for; matrix products, arithmetic and copies ran while one was open for 32% of the time, Pallas kernels for 11%

profile of v1, /device:TPU:0, one launch (start us, length us, event | category | flops | bytes accessed | tf_op | source)
XLA Modules:
  0.0 1058.4 jit_solution(10874751410932886807)
XLA Ops:
  16.0 98.9 %shard_map.288 = (bf16[32,16,128]{2,1,0:T(8,128)(2,1)S(1)}, bf16[2,4,96,2048]{3,2,1,0:T(8,128)(2,1)}, bf16[2048,512]{1,0:T(8,128)(2,1)S(1)}, bf16[2048,512]{1,0:T(8,128)(2,1)}, bf16[4,2,256,704]{3,2,1,0:T(8,128)(2,1)}) custom-call(bf16[1,16,128]{2,1,0:T(8,128)(2,1)S(1)} %pad_bitcast_fusion.refs_0_, bf16[2,96,2048]{2,1,0:T(8,128)(2,1)S(1)} %reshape.556.refs_1_, ...), custom_call_target="tpu_custom_call" | custom-call | bytes 65536 | tf_op jit(solution)/shard_map/pallas_call | solution.py:520
  166.7 127.7 %shard_map.290 = (f32[2,64,1024]{2,1,0:T(8,128)S(1)}, bf16[2048,512]{1,0:T(8,128)(2,1)S(1)}, bf16[2048,512]{1,0:T(8,128)(2,1)}, bf16[4,2,64,2048]{3,2,1,0:T(8,12...) custom-call(f32[2,64,128]{2,1,0:T(8,128)S(1)} %broadcast_in_dim.31.refs_0_, ...), custom_call_target="tpu_custom_call" | custom-call | bytes 65536 | tf_op jit(solution)/shard_map/pallas_call | solution.py:520
  299.1 8.7 shard_map.291
  312.0 11.1 %shard_map.292 = bf16[768,512]{1,0:T(8,128)(2,1)S(1)} custom-call(bf16[768,512]{1,0:T(8,128)(2,1)S(1)} %bitcast.274), custom_call_target="tpu_custom_call" | custom-call | bytes 65536 | tf_op jit(solution)/shard_map/pallas_call | solution.py:520
  326.6 96.4 %shard_map.293 = (f32[2,96,2048]{2,1,0:T(8,128)S(1)}, bf16[2,2,4,96,2048]{4,3,2,1,0:T(8,128)(2,1)}, bf16[2,2,4,96,2048]{4,3,2,1,0:T(8,128)(2,1)}, bf16[4,2,256,704]{3,2,1,0:T(8,128)(2,1)}) custom-call(bf16[2,2,2,96,2048]{4,3,2,1,0:T(8,128)(2,1)} %bitcast.292, bf16[2,96,2048]{2,1,0:T(8,128)(2,1)S(1)} %copy-done.1, f32[1,2048]{1,0:T(1,128)S(1)} %reshape.604.refs_2_, ...), custom_call_target="tpu_custom_call" | custom-call | bytes 65536 | tf_op jit(solution)/shard_map/pallas_call | solution.py:520
  423.1 8.8 fusion.120
  432.0 6.6 fusion.119
  438.6 9.5 multiply_convert_fusion.2
  463.6 10.5 fusion.104
  476.4 10.9 %fusion.116 = (bf16[2048,704]{0,1:T(8,128)(2,1)S(1)}, f32[2048,704]{0,1:T(8,128)}) fusion(bf16[1536,2048]{1,0:T(8,128)(2,1)} %bitcast.337, bf16[1536,704]{1,0:T(8,128)(2,1)S(1)} %copy-done.138), kind=kOutput, calls=%fused_computation.372 | convolution fusion | flops 4430626816 | bytes 17104896 | tf_op jit(solution)/shard_map/dot_general | solution.py:402
  499.1 7.1 fusion.123
  508.9 13.2 %collective-permute-done.7 = bf16[512,704]{0,1:T(8,128)(2,1)} collective-permute-done((bf16[512,704]{0,1:T(8,128)(2,1)}, bf16[512,704]{0,1:T(8,128)(2,1)}, u32[]{:S(2)}, u32[]{:S(2)}) %collective-permute-start.7) | collective-permute-done | bytes 720928 | tf_op jit(solution)/shard_map/ppermute | solution.py:797
  527.0 8.6 collective-permute-done.5
  537.1 6.5 convolution_convert_fusion.1
  549.7 8.5 fusion.117
  569.8 9.4 collective-permute-done.11
  606.2 10.0 fusion.121
  616.1 6.4 copy.266
  624.5 6.6 copy.257
  663.0 15.1 %collective-permute-done.27 = bf16[512,704]{0,1:T(8,128)(2,1)} collective-permute-done((bf16[512,704]{0,1:T(8,128)(2,1)}, bf16[512,704]{0,1:T(8,128)(2,1)}, u32[]{:S(2)}, u32[]{:S(2)}) %collective-permute-start.27) | collective-permute-done | bytes 720928 | tf_op jit(solution)/shard_map/ppermute | solution.py:797
  696.8 6.4 collective-permute-done.18
  740.0 12.3 %shard_map.299 = (bf16[2,384,512]{2,1,0:T(8,128)(2,1)S(1)}, f32[2,384,512]{2,1,0:T(8,128)S(1)}, f32[2,384,512]{2,1,0:T(8,128)S(1)}, f32[2,64,1024]{2,1,0:T(8,128...) custom-call(f32[2,384,512]{2,1,0:T(8,128)S(1)} %copy-done.11, f32[2,384,512]{2,1,0:T(8,128)S(1)} %copy-done.6, ...), custom_call_target="tpu_custom_call" | custom-call | flops 1000000000 | bytes 65536 | tf_op jit(solution)/shard_map/pallas_call | solution.py:380
  789.5 13.4 %collective-permute-done.56 = bf16[64,2048]{1,0:T(8,128)(2,1)} collective-permute-done((bf16[64,2048]{1,0:T(8,128)(2,1)}, bf16[64,2048]{1,0:T(8,128)(2,1)}, u32[]{:S(2)}, u32[]{:S(2)}) %collective-permute-start.56) | collective-permute-done | bytes 262176 | tf_op jit(solution)/shard_map/ppermute | solution.py:797
  804.7 5.6 collective-permute-done.23
  827.0 6.5 collective-permute-done.57
  848.9 5.1 shard_map.303
  865.3 9.8 add_add_fusion
  910.1 11.5 %collective-permute-done.32 = bf16[256,512]{1,0:T(8,128)(2,1)} collective-permute-done((bf16[256,512]{1,0:T(8,128)(2,1)S(1)}, bf16[256,512]{1,0:T(8,128)(2,1)}, u32[]{:S(2)}, u32[]{:S(2)}) %collective-permute-start.32) | collective-permute-done | bytes 262176 | tf_op jit(solution)/shard_map/ppermute | solution.py:797
  940.0 8.3 collective-permute-done.33
  954.3 7.4 collective-permute-done.51
  981.0 13.9 %collective-permute-done.44 = bf16[256,512]{1,0:T(8,128)(2,1)} collective-permute-done((bf16[256,512]{1,0:T(8,128)(2,1)S(1)}, bf16[256,512]{1,0:T(8,128)(2,1)}, u32[]{:S(2)}, u32[]{:S(2)}) %collective-permute-start.44) | collective-permute-done | bytes 262176 | tf_op jit(solution)/shard_map/ppermute | solution.py:797
  1002.1 8.6 collective-permute-done.45
  (711 shorter events, 465.8 us)
Async XLA Ops:
  0.6 162.3 %collective-permute-start = (bf16[64,2048]{1,0:T(8,128)(2,1)}, bf16[64,2048]{1,0:T(8,128)(2,1)}, u32[]{:S(2)}, u32[]{:S(2)}) collective-permute-start(bf16[64,2048]{1,0:T(8,128)(2,1)} %param.23), channel_id=1, source_target_pairs={{0,0},{1,4},{2,1},{3,5},{4,2},{5,6},{6,3},{7,7},{8,8},{9,12},{10,9... | collective-permute-start | bytes 786440 | tf_op jit(solution)/shard_map/ppermute | solution.py:904
  490.7 31.4 %collective-permute-start.7 = (bf16[512,704]{0,1:T(8,128)(2,1)}, bf16[512,704]{0,1:T(8,128)(2,1)}, u32[]{:S(2)}, u32[]{:S(2)}) collective-permute-start(bf16[512,704]{0,1:T(8,128)(2,1)} %get-tuple-element.181), channel_id=1, source_target_pairs={{0,8},{1,9},{2,10},{3,11},{4,12},{5,13},{6,14},{7,15},{8,0},{9,1},... | collective-permute-start | bytes 2162696 | tf_op jit(solution)/shard_map/ppermute | solution.py:797
  497.7 28.0 %collective-permute-start.3 = (bf16[96,2048]{1,0:T(8,128)(2,1)}, bf16[96,2048]{1,0:T(8,128)(2,1)}, u32[]{:S(2)}, u32[]{:S(2)}) collective-permute-start(bf16[96,2048]{1,0:T(8,128)(2,1)} %slice.512), channel_id=1, source_target_pairs={{0,2},{1,3},{2,0},{3,1},{4,6},{5,7},{6,4},{7,5},{8,10},{9,11},{10,... | collective-permute-start | bytes 1179656 | tf_op jit(solution)/shard_map/ppermute | solution.py:797
  543.7 41.7 %collective-permute-start.20 = (f32[2,64]{1,0:T(2,128)}, f32[2,64]{1,0:T(2,128)}, u32[]{:S(2)}, u32[]{:S(2)}) collective-permute-start(f32[2,64]{1,0:T(2,128)} %reduce.2), channel_id=1, source_target_pairs={{0,4},{1,5},{2,6},{3,7},{4,0},{5,1},{6,2},{7,3},{8,12},{9,13},{10,... | collective-permute-start | bytes 1544 | tf_op jit(solution)/shard_map/ppermute | solution.py:797
  559.2 19.9 %collective-permute-start.11 = (bf16[192,2048]{1,0:T(8,128)(2,1)}, bf16[192,2048]{1,0:T(8,128)(2,1)}, u32[]{:S(2)}, u32[]{:S(2)}) collective-permute-start(bf16[192,2048]{1,0:T(8,128)(2,1)} %get-tuple-element.177), channel_id=1, source_target_pairs={{0,2},{1,3},{2,0},{3,1},{4,6},{5,7},{6,4},{7,5},{8,10},{9,11},{10,... | collective-permute-start | bytes 2359304 | tf_op jit(solution)/shard_map/ppermute | solution.py:797
  605.8 40.4 %collective-permute-start.13 = (bf16[2,96,2048]{2,1,0:T(8,128)(2,1)}, bf16[2,96,2048]{2,1,0:T(8,128)(2,1)}, u32[]{:S(2)}, u32[]{:S(2)}) collective-permute-start(bf16[2,96,2048]{2,1,0:T(8,128)(2,1)} %bitcast.43), channel_id=1, source_target_pairs={{0,2},{1,3},{2,0},{3,1},{4,6},{5,7},{6,4},{7,5},{8,10},{9,11},{10,... | collective-permute-start | bytes 2359304 | tf_op jit(solution)/shard_map/ppermute | solution.py:797
  636.4 21.8 %collective-permute-start.19 = (bf16[512,704]{0,1:T(8,128)(2,1)}, bf16[512,704]{0,1:T(8,128)(2,1)}, u32[]{:S(2)}, u32[]{:S(2)}) collective-permute-start(bf16[512,704]{0,1:T(8,128)(2,1)} %copy.259), channel_id=1, source_target_pairs={{0,8},{1,9},{2,10},{3,11},{4,12},{5,13},{6,14},{7,15},{8,0},{9,1},... | collective-permute-start | bytes 2162696 | tf_op jit(solution)/shard_map/ppermute | solution.py:797
  643.1 35.0 %collective-permute-start.27 = (bf16[512,704]{0,1:T(8,128)(2,1)}, bf16[512,704]{0,1:T(8,128)(2,1)}, u32[]{:S(2)}, u32[]{:S(2)}) collective-permute-start(bf16[512,704]{0,1:T(8,128)(2,1)} %copy.268), channel_id=1, source_target_pairs={{0,8},{1,9},{2,10},{3,11},{4,12},{5,13},{6,14},{7,15},{8,0},{9,1},... | collective-permute-start | bytes 2162696 | tf_op jit(solution)/shard_map/ppermute | solution.py:797
  649.0 56.5 %collective-permute-start.14 = (bf16[2,2,96,2048]{3,2,0,1:T(8,128)(2,1)}, bf16[2,2,96,2048]{3,2,0,1:T(8,128)(2,1)}, u32[]{:S(2)}, u32[]{:S(2)}) collective-permute-start(bf16[2,2,96,2048]{3,2,0,1:T(8,128)(2,1)} %pad_maximum_fusion.2), channel_id=1, source_target_pairs={{0,1},{1,0},{2,3},{3,2},{4,5},{5,4},{6,7},{7,6},{8,9},{9,8},{10,11... | collective-permute-start | bytes 4718600 | tf_op jit(solution)/shard_map/ppermute | solution.py:797
  653.4 36.1 %collective-permute-start.17 = (bf16[512,704]{0,1:T(8,128)(2,1)}, bf16[512,704]{0,1:T(8,128)(2,1)}, u32[]{:S(2)}, u32[]{:S(2)}) collective-permute-start(bf16[512,704]{0,1:T(8,128)(2,1)} %copy.256), channel_id=1, source_target_pairs={{0,16},{1,17},{2,18},{3,19},{4,20},{5,21},{6,22},{7,23},{8,24},{9,... | collective-permute-start | bytes 2162696 | tf_op jit(solution)/shard_map/ppermute | solution.py:797
  693.3 19.9 %collective-permute-start.64 = (bf16[256,704]{0,1:T(8,128)(2,1)}, bf16[256,704]{0,1:T(8,128)(2,1)S(1)}, u32[]{:S(2)}, u32[]{:S(2)}) collective-permute-start(bf16[256,704]{0,1:T(8,128)(2,1)} %dynamic-slice_convert_fusion.9), channel_id=1, source_target_pairs={{0,4},{1,5},{2,6},{3,7},{4,0},{5,1},{6,2},{7,3},{8,12},{9,13},{10,... | collective-permute-start | bytes 1081352 | tf_op jit(solution)/shard_map/ppermute | solution.py:797
  727.0 53.7 %collective-permute-start.54 = (bf16[4,1,64,2048]{3,2,1,0:T(8,128)(2,1)}, bf16[4,1,64,2048]{3,2,1,0:T(8,128)(2,1)}, u32[]{:S(2)}, u32[]{:S(2)}) collective-permute-start(bf16[4,1,64,2048]{3,2,1,0:T(8,128)(2,1)} %dynamic-slice_convert_fusion.1), channel_id=1, source_target_pairs={{0,4},{1,5},{2,6},{3,7},{4,0},{5,1},{6,2},{7,3},{8,12},{9,13},{10,... | collective-permute-start | bytes 3145736 | tf_op jit(solution)/shard_map/ppermute | solution.py:797
  757.4 30.0 %collective-permute-start.22 = (bf16[2,64,1024]{2,1,0:T(8,128)(2,1)}, bf16[2,64,1024]{2,1,0:T(8,128)(2,1)}, u32[]{:S(2)}, u32[]{:S(2)}) collective-permute-start(bf16[2,64,1024]{2,1,0:T(8,128)(2,1)} %convert_element_type.484), channel_id=1, source_target_pairs={{0,4},{1,5},{2,6},{3,7},{4,0},{5,1},{6,2},{7,3},{8,12},{9,13},{10,... | collective-permute-start | bytes 786440 | tf_op jit(solution)/shard_map/ppermute | solution.py:797
  760.6 51.9 %collective-permute-start.25 = (bf16[512,704]{0,1:T(8,128)(2,1)}, bf16[512,704]{0,1:T(8,128)(2,1)}, u32[]{:S(2)}, u32[]{:S(2)}) collective-permute-start(bf16[512,704]{0,1:T(8,128)(2,1)} %copy.265), channel_id=1, source_target_pairs={{0,16},{1,17},{2,18},{3,19},{4,20},{5,21},{6,22},{7,23},{8,24},{9,... | collective-permute-start | bytes 2162696 | tf_op jit(solution)/shard_map/ppermute | solution.py:797
  763.0 57.4 %collective-permute-start.26 = (bf16[512,704]{0,1:T(8,128)(2,1)}, bf16[512,704]{0,1:T(8,128)(2,1)}, u32[]{:S(2)}, u32[]{:S(2)}) collective-permute-start(bf16[512,704]{0,1:T(8,128)(2,1)} %copy.267), channel_id=1, source_target_pairs={{0,8},{1,9},{2,10},{3,11},{4,12},{5,13},{6,14},{7,15},{8,0},{9,1},... | collective-permute-start | bytes 2162696 | tf_op jit(solution)/shard_map/ppermute | solution.py:797
  772.7 122.8 %collective-permute-start.30 = (bf16[1024,512]{1,0:T(8,128)(2,1)}, bf16[1024,512]{1,0:T(8,128)(2,1)}, u32[]{:S(2)}, u32[]{:S(2)}) collective-permute-start(bf16[1024,512]{1,0:T(8,128)(2,1)} %dynamic-slice_convert_fusion.5), channel_id=1, source_target_pairs={{0,4},{1,5},{2,6},{3,7},{4,0},{5,1},{6,2},{7,3},{8,12},{9,13},{10,... | collective-permute-start | bytes 3145736 | tf_op jit(solution)/shard_map/ppermute | solution.py:797
  787.4 111.9 %collective-permute-start.48 = (bf16[1024,512]{1,0:T(8,128)(2,1)}, bf16[1024,512]{1,0:T(8,128)(2,1)}, u32[]{:S(2)}, u32[]{:S(2)}) collective-permute-start(bf16[1024,512]{1,0:T(8,128)(2,1)} %dynamic-slice_convert_fusion.2), channel_id=1, source_target_pairs={{0,4},{1,5},{2,6},{3,7},{4,0},{5,1},{6,2},{7,3},{8,12},{9,13},{10,... | collective-permute-start | bytes 3145736 | tf_op jit(solution)/shard_map/ppermute | solution.py:797
  812.5 21.0 %collective-permute-start.57 = (bf16[64,2048]{1,0:T(8,128)(2,1)}, bf16[64,2048]{1,0:T(8,128)(2,1)}, u32[]{:S(2)}, u32[]{:S(2)}) collective-permute-start(bf16[64,2048]{1,0:T(8,128)(2,1)} %fusion.44), channel_id=1, source_target_pairs={{0,16},{1,17},{2,18},{3,19},{4,20},{5,21},{6,22},{7,23},{8,24},{9,... | collective-permute-start | bytes 786440 | tf_op jit(solution)/shard_map/ppermute | solution.py:797
  825.2 82.1 %collective-permute-start.65 = (bf16[256,704]{0,1:T(8,128)(2,1)}, bf16[256,704]{0,1:T(8,128)(2,1)}, u32[]{:S(2)}, u32[]{:S(2)}) collective-permute-start(bf16[256,704]{0,1:T(8,128)(2,1)} %dynamic-slice_convert_fusion.8), channel_id=1, source_target_pairs={{0,4},{1,5},{2,6},{3,7},{4,0},{5,1},{6,2},{7,3},{8,12},{9,13},{10,... | collective-permute-start | bytes 1081352 | tf_op jit(solution)/shard_map/ppermute | solution.py:797
  835.5 66.8 %collective-permute-start.58 = (bf16[64,2048]{1,0:T(8,128)(2,1)}, bf16[64,2048]{1,0:T(8,128)(2,1)}, u32[]{:S(2)}, u32[]{:S(2)}) collective-permute-start(bf16[64,2048]{1,0:T(8,128)(2,1)} %fusion.47), channel_id=1, source_target_pairs={{0,0},{4,1},{1,2},{5,3},{2,4},{6,5},{3,6},{7,7},{8,8},{12,9},{9,10... | collective-permute-start | bytes 786440 | tf_op jit(solution)/shard_map/ppermute | solution.py:904
  878.5 117.6 %collective-permute-start.28 = (bf16[2,2,1,96,2048]{4,3,2,1,0:T(8,128)(2,1)}, bf16[2,2,1,96,2048]{4,3,2,1,0:T(8,128)(2,1)}, u32[]{:S(2)}, u32[]{:S(2)}) collective-permute-start(bf16[2,2,1,96,2048]{4,3,2,1,0:T(8,128)(2,1)} %dynamic-slice_convert_fusion), channel_id=1, source_target_pairs={{0,1},{1,0},{2,3},{3,2},{4,5},{5,4},{6,7},{7,6},{8,9},{9,8},{10,11... | collective-permute-start | bytes 4718600 | tf_op jit(solution)/shard_map/ppermute | solution.py:797
  895.4 70.9 %collective-permute-start.36 = (bf16[1024,512]{1,0:T(8,128)(2,1)}, bf16[1024,512]{1,0:T(8,128)(2,1)S(1)}, u32[]{:S(2)}, u32[]{:S(2)}) collective-permute-start(bf16[1024,512]{1,0:T(8,128)(2,1)} %dynamic-slice_convert_fusion.4), channel_id=1, source_target_pairs={{0,4},{1,5},{2,6},{3,7},{4,0},{5,1},{6,2},{7,3},{8,12},{9,13},{10,... | collective-permute-start | bytes 3145736 | tf_op jit(solution)/shard_map/ppermute | solution.py:797
  899.3 34.5 %collective-permute-start.66 = (bf16[512,704]{0,1:T(8,128)(2,1)}, bf16[512,704]{0,1:T(8,128)(2,1)}, u32[]{:S(2)}, u32[]{:S(2)}) collective-permute-start(bf16[512,704]{0,1:T(8,128)(2,1)} %copy.284), channel_id=1, source_target_pairs={{0,16},{1,17},{2,18},{3,19},{4,20},{5,21},{6,22},{7,23},{8,24},{9,... | collective-permute-start | bytes 2162696 | tf_op jit(solution)/shard_map/ppermute | solution.py:797
  907.2 19.8 %collective-permute-start.50 = (bf16[256,512]{1,0:T(8,128)(2,1)}, bf16[256,512]{1,0:T(8,128)(2,1)}, u32[]{:S(2)}, u32[]{:S(2)}) collective-permute-start(bf16[256,512]{1,0:T(8,128)(2,1)} %get-tuple-element.212), channel_id=1, source_target_pairs={{0,8},{1,9},{2,10},{3,11},{4,12},{5,13},{6,14},{7,15},{8,0},{9,1},... | collective-permute-start | bytes 786440 | tf_op jit(solution)/shard_map/ppermute | solution.py:797
  921.6 47.0 %collective-permute-start.42 = (bf16[1024,512]{1,0:T(8,128)(2,1)}, bf16[1024,512]{1,0:T(8,128)(2,1)S(1)}, u32[]{:S(2)}, u32[]{:S(2)}) collective-permute-start(bf16[1024,512]{1,0:T(8,128)(2,1)} %dynamic-slice_convert_fusion.3), channel_id=1, source_target_pairs={{0,4},{1,5},{2,6},{3,7},{4,0},{5,1},{6,2},{7,3},{8,12},{9,13},{10,... | collective-permute-start | bytes 3145736 | tf_op jit(solution)/shard_map/ppermute | solution.py:797
  953.1 22.4 %collective-permute-start.67 = (bf16[256,704]{0,1:T(8,128)(2,1)S(1)}, bf16[256,704]{0,1:T(8,128)(2,1)S(1)}, u32[]{:S(2)}, u32[]{:S(2)}) collective-permute-start(bf16[256,704]{0,1:T(8,128)(2,1)S(1)} %dynamic-slice_convert_fusion.7), channel_id=1, source_target_pairs={{0,4},{1,5},{2,6},{3,7},{4,0},{5,1},{6,2},{7,3},{8,12},{9,13},{10,... | collective-permute-start | bytes 1081352 | tf_op jit(solution)/shard_map/ppermute | solution.py:797
  971.6 29.2 %collective-permute-start.37 = (bf16[256,512]{1,0:T(8,128)(2,1)S(1)}, bf16[256,512]{1,0:T(8,128)(2,1)S(1)}, u32[]{:S(2)}, u32[]{:S(2)}) collective-permute-start(bf16[256,512]{1,0:T(8,128)(2,1)S(1)} %get-tuple-element.215), channel_id=1, source_target_pairs={{0,8},{1,9},{2,10},{3,11},{4,12},{5,13},{6,14},{7,15},{8,0},{9,1},... | collective-permute-start | bytes 786440 | tf_op jit(solution)/shard_map/ppermute | solution.py:797
  973.2 21.6 %collective-permute-start.44 = (bf16[256,512]{1,0:T(8,128)(2,1)S(1)}, bf16[256,512]{1,0:T(8,128)(2,1)}, u32[]{:S(2)}, u32[]{:S(2)}) collective-permute-start(bf16[256,512]{1,0:T(8,128)(2,1)S(1)} %get-tuple-element.214), channel_id=1, source_target_pairs={{0,8},{1,9},{2,10},{3,11},{4,12},{5,13},{6,14},{7,15},{8,0},{9,1},... | collective-permute-start | bytes 786440 | tf_op jit(solution)/shard_map/ppermute | solution.py:797
  975.5 26.5 %collective-permute-start.43 = (bf16[256,512]{1,0:T(8,128)(2,1)S(1)}, bf16[256,512]{1,0:T(8,128)(2,1)S(1)}, u32[]{:S(2)}, u32[]{:S(2)}) collective-permute-start(bf16[256,512]{1,0:T(8,128)(2,1)S(1)} %get-tuple-element.213), channel_id=1, source_target_pairs={{0,8},{1,9},{2,10},{3,11},{4,12},{5,13},{6,14},{7,15},{8,0},{9,1},... | collective-permute-start | bytes 786440 | tf_op jit(solution)/shard_map/ppermute | solution.py:797
  979.9 20.9 %collective-permute-start.39 = (bf16[256,512]{1,0:T(8,128)(2,1)S(1)}, bf16[256,512]{1,0:T(8,128)(2,1)S(1)}, u32[]{:S(2)}, u32[]{:S(2)}) collective-permute-start(bf16[256,512]{1,0:T(8,128)(2,1)S(1)} %fusion.52), channel_id=1, source_target_pairs={{0,16},{1,17},{2,18},{3,19},{4,20},{5,21},{6,22},{7,23},{8,24},{9,... | collective-permute-start | bytes 786440 | tf_op jit(solution)/shard_map/ppermute | solution.py:797
  999.1 22.0 %collective-permute-start.29 = (bf16[2,1,1,96,2048]{4,3,2,1,0:T(8,128)(2,1)S(1)}, bf16[2,1,1,96,2048]{4,3,2,1,0:T(8,128)(2,1)S(1)}, u32[]{:S(2)}, u32[]{:S(2)}) collective-permute-start(bf16[2,1,1,96,2048]{4,3,2,1,0:T(8,128)(2,1)S(1)} %dynamic-slice_convert_fusion.6), channel_id=1, source_target_pairs={{0,2},{1,3},{2,0},{3,1},{4,6},{5,7},{6,4},{7,5},{8,10},{9,11},{10,... | collective-permute-start | bytes 2359304 | tf_op jit(solution)/shard_map/ppermute | solution.py:797
  1014.3 22.7 %collective-permute-start.47 = (bf16[1,1,64,1024]{3,2,1,0:T(8,128)(2,1)}, bf16[1,1,64,1024]{3,2,1,0:T(8,128)(2,1)}, u32[]{:S(2)}, u32[]{:S(2)}) collective-permute-start(bf16[1,1,64,1024]{3,2,1,0:T(8,128)(2,1)} %fusion.71), channel_id=1, source_target_pairs={{0,2},{1,3},{2,0},{3,1},{4,6},{5,7},{6,4},{7,5},{8,10},{9,11},{10,... | collective-permute-start | bytes 393224 | tf_op jit(solution)/shard_map/ppermute | solution.py:797
  (184 other events, 1621.2 us)

commit v2 on v1

--- a/solution.py
+++ b/solution.py
@@ -1,4 +1,5 @@
-import functools
+import dataclasses
+import math
 
 import jax
 import jax.numpy as jnp
@@ -232,12 +233,28 @@
     return sig * (1.0 + x * (1.0 - sig))
 
 
+def gates(logits):
+    small = jnp.exp(-jnp.abs(logits))
+    ratio = small / (2.0 + small)
+    square = ratio * ratio
+    series = jnp.full_like(square, 1.0 / 17.0)
+    for odd in (15, 13, 11, 9, 7, 5, 3, 1):
+        series = series * square + 1.0 / odd
+    log_keep = (jnp.minimum(logits, 0.0) - 2.0 * ratio * series) / GATE_SCALE
+    keep = jnp.exp(log_keep)
+    near = jnp.ones_like(log_keep)
+    for order in (9, 8, 7, 6, 5, 4, 3, 2):
+        near = 1.0 + log_keep / order * near
+    return keep, jnp.where(log_keep > -0.5, -log_keep * near, 1.0 - keep)
+
+
 def piece_state(key_raw, value_raw, keep, written):
     decays = Decays(keep)
     left = jnp.concatenate(
         [decays.to_end(c) * w for c, w in enumerate(chunks_of(written))], axis=1
     )
-    state = jnp.concatenate([mm(left, silu(key_raw), NN), mm(left, silu(value_raw), NN)], axis=1)
+    keys, values = mm_fine(left, silu(key_raw), NN), mm_fine(left, silu(value_raw), NN)
+    state = jnp.concatenate([keys, values], axis=1)
     return state, decays.survive()
 
 
@@ -439,9 +456,13 @@
 
 
 class Wire:
+    LATENCY, LINK, BESIDE, AHEAD = 2.5, 2 / 91e3, 1 / 400e3, 5.0
+
     def __init__(self, place, sends, receives, locals_):
         self.place, self.sends, self.receives, self.locals = place, sends, receives, locals_
         self.remote, self.near_by, self.seen = [], [], set()
+        self.now, self.due, self.free, self.rank = 0.0, {}, {}, 0
+        self.queues = {"x": [], "y": [], "side": [], "middle": []}
 
     def greet(self, masks):
         barrier = pltpu.get_barrier_semaphore()
@@ -454,8 +475,11 @@
             )
         pl.semaphore_wait(barrier, len(masks))
 
-    def send(self, source, target, mask):
-        at = len(self.remote)
+    def spend(self, time):
+        self.now += time
+
+    def issue(self, at):
+        source, target, mask = self.remote[at]
         copy = pltpu.make_async_remote_copy(
             src_ref=source,
             dst_ref=target,
@@ -465,14 +489,50 @@
             device_id_type=pl.DeviceIdType.MESH,
         )
         copy.start()
-        self.remote.append(copy)
+        self.remote[at] = copy
+        size = math.prod(source.shape) * jnp.dtype(source.dtype).itemsize
+        if mask == CORE:
+            uses = (("core", size * self.BESIDE),)
+        elif mask & X:
+            uses = (("x", size * self.LINK),)
+        elif mask == Y:
+            uses = (("y", size * self.LINK),)
+        elif mask == NEAR:
+            uses = (("side", size * self.LINK),)
+        else:
+            uses = (("side", size * self.LINK), ("middle", 2 * size * self.LINK))
+        end = 0.0
+        for link, time in uses:
+            self.free[link] = max(self.now, self.free.get(link, 0.0)) + time
+            end = max(end, self.free[link])
+        self.due["remote", at] = end + self.LATENCY
+
+    def send(self, source, target, mask):
+        at = len(self.remote)
+        self.remote.append((source, target, mask))
+        if mask == CORE:
+            self.issue(at)
+        else:
+            link = {Y: "y", NEAR: "side", FAR: "middle"}.get(mask, "x")
+            self.queues[link].append((self.rank, at))
         return ("remote", at)
+
+    def feed(self, until):
+        fed = False
+        for link, queue in self.queues.items():
+            while queue and self.free.get(link, 0.0) < until + self.AHEAD:
+                first = min(queue)
+                queue.remove(first)
+                self.issue(first[1])
+                fed = True
+        return fed
 
     def keep(self, source, target):
         at = len(self.near_by)
         copy = pltpu.make_async_copy(source, target, self.locals.at[at])
         copy.start()
         self.near_by.append(copy)
+        self.due["local", at] = self.now + 2.0
         return ("local", at)
 
     def arrived(self, *handles):
@@ -480,22 +540,39 @@
             if handle in self.seen:
                 continue
             self.seen.add(handle)
+            self.now = max(self.now, self.due[handle])
             if handle[0] == "remote":
                 self.remote[handle[1]].wait_recv()
             else:
                 self.near_by[handle[1]].wait()
 
     def run(self, *tasks):
-        live = [(task, next(task)) for task in tasks]
+        live = []
+        for rank, task in enumerate(tasks):
+            self.rank = rank
+            live.append([rank, task, next(task)])
+
+        def waits(entry):
+            return entry[2]() if callable(entry[2]) else entry[2]
+
+        def when(entry):
+            handles = waits(entry)
+            if handles is None:
+                return 1e9, entry[0]
+            dues = [self.due.get(h, 1e9) for h in handles if h not in self.seen]
+            return max([self.now] + dues), entry[0]
+
         while live:
-            later = []
-            for task, handles in live:
-                self.arrived(*handles)
-                try:
-                    later.append((task, next(task)))
-                except StopIteration:
-                    pass
-            live = later
+            entry = min(live, key=when)
+            if self.feed(min(when(entry)[0], self.now + 1e6)):
+                continue
+            self.arrived(*waits(entry))
+            self.rank = entry[0]
+            try:
+                entry[2] = next(entry[1])
+            except StopIteration:
+                live.remove(entry)
+        self.feed(1e9)
 
     def finish(self):
         for at, copy in enumerate(self.remote):
@@ -503,6 +580,22 @@
             copy.wait_send()
         for at in range(len(self.near_by)):
             self.arrived(("local", at))
+
+
+class Flags:
+    def __init__(self):
+        self.set = {}
+
+    def raised(self, key, handles=()):
+        self.set[key] = list(handles)
+
+    def wait(self, *keys, more=()):
+        def ask():
+            if any(key not in self.set for key in keys):
+                return None
+            return [h for key in keys for h in self.set[key]] + list(more)
+
+        return ask
 
 
 def comm_call(work, number, masks, arrays, in_vmem, outs, out_vmem, scratch, copies, stay, mb=48):
@@ -535,13 +628,13 @@
     )(*arrays)
 
 
-def head_gather(place, wire, weight, out):
+def head_gather(place, wire, weight, out, flags=None, key=None, alike=False):
     rows, width = weight.shape[0], out.shape[1]
     block = 4 * rows
     base = place.y * 4 * block
 
     def columns(tp):
-        return weight.at[:, pl.ds(pl.multiple_of(tp * width, 128), width)]
+        return weight if alike else weight.at[:, pl.ds(pl.multiple_of(tp * width, 128), width)]
 
     def part(m):
         return out.at[pl.ds(pl.multiple_of(base + m * block, 16), block)]
@@ -562,9 +655,11 @@
     yield [last]
     over.append(wire.send(part(3), part(3), Y))
     yield over
-
-
-def output_gather(place, wire, block, out):
+    if flags is not None:
+        flags.raised(key)
+
+
+def output_gather(place, wire, block, out, flags, key):
     def part(m):
         return out.at[m, place.y]
 
@@ -580,9 +675,17 @@
     yield [last]
     over.append(wire.send(part(3), part(3), Y))
     yield over
-
-
-def ffn_trade(place, wire, halves, out):
+    flags.raised(key)
+
+
+def ffn_trade(place, wire, weight, halves, out):
+    cols = halves.shape[2]
+
+    def to_cut(rows):
+        for y in range(2):
+            halves[y, rows] = weight[rows, y * cols : (y + 1) * cols]
+
+    row_loop(weight.shape[0], 32, to_cut)
     own = out.at[0, place.y]
     yield [
         wire.send(halves.at[1 - place.y], own, Y),
@@ -590,25 +693,20 @@
     ]
 
 
-def later(task, rounds):
-    for unused in range(rounds):
-        yield []
-    yield from task
-
-
-def ffn_gather(place, wire, halves, out, rounds):
-    yield from ffn_trade(place, wire, halves, out)
-    yield from later(ffn_spread(place, wire, None, out), rounds)
+def ffn_gather(place, wire, weight, halves, out):
+    yield from ffn_trade(place, wire, weight, halves, out)
+    yield from ffn_spread(place, wire, None, out)
 
 
 def ffn_spread(place, wire, block, out):
     start = out.at[0] if block is None else block
-    stay = [] if block is None else [wire.keep(block, out.at[0])]
-    far = wire.send(start, out.at[2], FAR)
-    near = wire.send(start, out.at[1], NEAR)
-    yield [far]
-    last = wire.send(out.at[2], out.at[3], NEAR)
-    yield [near, last] + stay
+    waits = [] if block is None else [wire.keep(block, out.at[0])]
+    far = [wire.send(start.at[y], out.at[2, y], FAR) for y in range(2)]
+    waits += [wire.send(start.at[y], out.at[1, y], NEAR) for y in range(2)]
+    for y in range(2):
+        yield [far[y]]
+        waits.append(wire.send(out.at[2, y], out.at[3, y], NEAR))
+    yield waits
 
 
 def rows_gather(place, wire, own, out):
@@ -635,21 +733,22 @@
     yield handles
 
 
-def plane_gather(place, wire, first, second, out):
+def plane_gather(place, wire, first, second, out, flags=None):
     line_a = [out.at[0, 0, m] for m in range(4)]
     line_b = [out.at[0, 1, m] for m in range(4)]
-    beside = []
-
-    def pass_on(half, m):
-        beside.append(wire.send(out.at[0, half, m], out.at[1, half, m], CORE))
-
-    stay = [wire.keep(first, line_a[0]), wire.keep(second, line_b[0])]
+    beside = [[], []]
+
+    def pass_on(half, m, source=None):
+        source = out.at[0, half, m] if source is None else source
+        beside[half].append(wire.send(source, out.at[1, half, m], CORE))
+
     a_x = wire.send(first, line_a[1], X)
     b_y = wire.send(second, line_b[1], Y)
     a_y = wire.send(first, line_a[2], Y)
     b_x = wire.send(second, line_b[2], X)
-    beside.append(wire.send(first, out.at[1, 0, 0], CORE))
-    beside.append(wire.send(second, out.at[1, 1, 0], CORE))
+    stay = [wire.keep(first, line_a[0]), wire.keep(second, line_b[0])]
+    pass_on(0, 0, first)
+    pass_on(1, 0, second)
     yield [a_x]
     a_xy = wire.send(line_a[1], line_a[3], Y)
     pass_on(0, 1)
@@ -659,10 +758,18 @@
     yield [a_y, b_x]
     pass_on(0, 2)
     pass_on(1, 2)
-    yield [a_xy, b_xy]
+    if flags is not None:
+        flags.raised((0, 0), [stay[0], a_xy])
+        flags.raised((0, 1), [stay[1], b_xy])
+    yield [a_xy]
     pass_on(0, 3)
+    if flags is not None:
+        flags.raised((1, 0), beside[0])
+    yield [b_xy]
     pass_on(1, 3)
-    yield stay + beside
+    if flags is not None:
+        flags.raised((1, 1), beside[1])
+    yield stay + beside[0] + beside[1]
 
 
 def heads_trade(place, wire, branch, out):
@@ -743,35 +850,238 @@
     lax.fori_loop(0, count // step, body, 0)
 
 
-def hidden_rows(place, wire, mixed, tokens, gain, hidden, ready, sums, got_core, got_x):
-    streams, count, width = tokens.shape
+def rows_fold(place, wire, part, sums, got_core, got_x, finish):
+    streams, count = part.shape[0], part.shape[3]
     other_x = 1 - place.x
-    beside = [wire.send(mixed.at[s, :, 1 - place.core], got_core.at[s], CORE) for s in range(streams)]
+    beside = [wire.send(part.at[s, :, 1 - place.core], got_core.at[s], CORE) for s in range(streams)]
     across = []
     for s in range(streams):
         yield [beside[s]]
 
         def to_send(rows, s=s):
-            part = mixed[s, other_x, place.core, rows].astype(F32)
-            sums[s, rows] = (part + got_core[s, other_x, rows].astype(F32)).astype(BF)
+            term = part[s, other_x, place.core, rows].astype(F32)
+            sums[s, rows] = (term + got_core[s, other_x, rows].astype(F32)).astype(BF)
 
         row_loop(count, 16, to_send)
         across.append(wire.send(sums.at[s], got_x.at[s], X))
     for s in range(streams):
         yield [across[s]]
 
-        def to_norm(rows, s=s):
-            part = mixed[s, place.x, place.core, rows].astype(F32)
-            part = part + got_core[s, place.x, rows].astype(F32) + got_x[s, rows].astype(F32)
-            values = tokens[s, rows].astype(F32) + part
-            hidden[s, rows] = values
-            normed = (values * inverse_rms(values) * gain[...]).astype(BF)
-            size = width // 4
-            for m in range(4):
-                there = pl.ds(pl.multiple_of(place.z_turn(m) * size, 128), size)
-                ready[s, rows, there] = normed[:, m * size : (m + 1) * size]
-
-        row_loop(count, 16, to_norm)
+        def to_finish(rows, s=s):
+            term = part[s, place.x, place.core, rows].astype(F32)
+            term = term + got_core[s, place.x, rows].astype(F32)
+            finish(s, rows, term + got_x[s, rows].astype(F32))
+
+        row_loop(count, 16, to_finish)
+
+
+def rows_buffers(part_shape):
+    streams, _, _, count, width = part_shape
+    return [
+        pltpu.VMEM((streams, count, width), BF),
+        pltpu.VMEM((streams, 2, count, width), BF),
+        pltpu.VMEM((streams, count, width), BF),
+    ]
+
+
+def plane_fold(place, wire, near_part, far_part, bufs, finish, flags=None):
+    got_core, send_two, got_two, send_one, got_one = bufs
+    count = near_part.shape[2]
+    if flags is None:
+        flags = Flags()
+        for h in range(2):
+            flags.raised(("far", h))
+            flags.raised(("near", h))
+    beside = {}
+    for h in range(2):
+        yield flags.wait(("far", h))
+        for m in (2, 3, 1, 0):
+            beside[h, m] = wire.send(far_part.at[h, m], got_core.at[h, m], CORE)
+    two, one = {}, {}
+    for h in range(2):
+        yield flags.wait(("near", h), more=[beside[h, 2], beside[h, 3]])
+
+        def to_two(rows, h=h):
+            for m in (2, 3):
+                term = near_part[h, m, rows].astype(F32) + got_core[h, m, rows].astype(F32)
+                send_two[h, m - 2, rows] = term.astype(BF)
+
+        row_loop(count, 16, to_two)
+        two[h] = wire.send(send_two.at[h], got_two.at[h], (Y, X)[h])
+    for h in range(2):
+        yield [beside[h, 1], two[h]]
+
+        def to_one(rows, h=h):
+            term = near_part[h, 1, rows].astype(F32) + got_core[h, 1, rows].astype(F32)
+            send_one[h, rows] = (term + got_two[h, 1, rows].astype(F32)).astype(BF)
+
+        row_loop(count, 16, to_one)
+        one[h] = wire.send(send_one.at[h], got_one.at[h], (X, Y)[h])
+    for h in range(2):
+        yield [beside[h, 0], one[h]]
+
+        def to_finish(rows, h=h):
+            def load(columns):
+                term = near_part[h, 0, rows, columns].astype(F32)
+                term = term + got_core[h, 0, rows, columns].astype(F32)
+                term = term + got_two[h, 0, rows, columns].astype(F32)
+                return term + got_one[h, rows, columns].astype(F32)
+
+            finish(h, rows, load)
+
+        row_loop(count, 16, to_finish)
+
+
+def plane_buffers(part_shape):
+    halves, _, count, width = part_shape
+    return [
+        pltpu.VMEM(part_shape, BF),
+        pltpu.VMEM((halves, 2, count, width), BF),
+        pltpu.VMEM((halves, 2, count, width), BF),
+        pltpu.VMEM((halves, count, width), BF),
+        pltpu.VMEM((halves, count, width), BF),
+    ]
+
+
+def z_parts(place, load, width):
+    size = width // 4
+    parts = []
+    for m in range(4):
+        there = pl.multiple_of(place.z_turn(m) * size, 128)
+        parts.append(load(pl.ds(there, size)))
+    return jnp.concatenate(parts, axis=-1)
+
+
+def add_into(target, terms, step=32):
+    def work(rows):
+        total = terms[0][rows].astype(F32)
+        for term in terms[1:]:
+            total = total + term[rows].astype(F32)
+        target[rows] = total.astype(BF)
+
+    row_loop(target.shape[0], step, work)
+
+
+def ffn_fold(place, wire, part, bufs, out, flags=None):
+    got_near, got_far, held = bufs
+    first, second, far = [], [], []
+    for z, handles in ((3, first), (1, second)):
+        for y in range(2):
+            if flags is not None:
+                yield flags.wait((z, y))
+            handles.append(wire.send(part.at[z, y], got_near.at[z // 2, y], NEAR))
+    for y in range(2):
+        yield [first[y]] if flags is None else flags.wait((2, y), more=[first[y]])
+        add_into(held.at[0, y], [part.at[2, y], got_near.at[1, y]])
+        far.append(wire.send(held.at[0, y], got_far.at[y], FAR))
+    for y in range(2):
+        yield [second[y], far[y]] if flags is None else flags.wait((0, y), more=[second[y], far[y]])
+        add_into(held.at[1, y], [part.at[0, y], got_near.at[0, y], got_far.at[y]])
+    mine = out.at[place.y]
+    yield [
+        wire.send(held.at[1, 1 - place.y], mine, Y),
+        wire.keep(held.at[1, place.y], mine),
+    ]
+
+
+def weight_tiles(wire, rows_by, order, grads, put, flags=None):
+    for key in order:
+        yield []
+        put(key, mm(rows_by(key), grads(), TN))
+        wire.spend(1.2)
+        if flags is not None:
+            flags.raised(key)
+
+
+def head_tiles(wire, rows, grads, part, flags):
+    side = part.shape[2]
+    for z in (3, 1, 2, 0):
+        for y in range(2):
+            yield []
+            at = (y * 4 + z) * side
+            part[y, z] = mm(rows[:, at : at + side], grads(), TN).astype(BF)
+            wire.spend(0.6)
+        flags.raised(z)
+
+
+def ffn_buffers(part_shape):
+    _, ys, rows, width = part_shape
+    return [
+        pltpu.VMEM((2, ys, rows, width), BF),
+        pltpu.VMEM((ys, rows, width), BF),
+        pltpu.VMEM((2, ys, rows, width), BF),
+    ]
+
+
+def line_fold(place, wire, mine, theirs, bufs, flags=None):
+    got_y, got_near, got_far, held = bufs
+    over = {}
+    for m in (3, 1, 2, 0):
+        if flags is not None:
+            yield flags.wait(m)
+        over[m] = wire.send(theirs(m), got_y.at[m], Y)
+    yield [over[3]]
+    add_into(held.at[1], [mine(3), got_y.at[3]])
+    last = wire.send(held.at[1], got_near.at[1], NEAR)
+    yield [over[1]]
+    add_into(held.at[0], [mine(1), got_y.at[1]])
+    near = wire.send(held.at[0], got_near.at[0], NEAR)
+    yield [over[2], last]
+    add_into(held.at[2], [mine(2), got_y.at[2], got_near.at[1]])
+    far = wire.send(held.at[2], got_far, FAR)
+    yield [over[0], near, far]
+    add_into(held.at[3], [mine(0), got_y.at[0], got_near.at[0], got_far])
+
+
+def line_buffers(rows, width):
+    return [
+        pltpu.VMEM((4, rows, width), BF),
+        pltpu.VMEM((2, rows, width), BF),
+        pltpu.VMEM((rows, width), BF),
+        pltpu.VMEM((4, rows, width), BF),
+    ]
+
+
+def head_fold(place, wire, part, bufs, out, flags=None):
+    yield from line_fold(
+        place, wire, lambda m: part.at[place.y, m], lambda m: part.at[1 - place.y, m], bufs, flags
+    )
+    own = bufs[3].at[3]
+    rows, width = out.shape[0], own.shape[1]
+
+    def block(tp):
+        return own.at[pl.ds(pl.multiple_of(tp * rows, 16), rows)]
+
+    mine = out.at[:, pl.ds(pl.multiple_of(place.tp * width, 128), width)]
+    handles = [wire.keep(block(place.tp), mine)]
+    for mask in (X, X | CORE, CORE):
+        handles.append(wire.send(block(place.partner(mask)[1]), mine, mask))
+    yield handles
+
+
+def output_fold(place, wire, part, bufs, out, flags=None):
+    yield from line_fold(
+        place, wire, lambda m: part.at[m, place.y], lambda m: part.at[m, 1 - place.y], bufs, flags
+    )
+    yield [wire.keep(bufs[3].at[3], out)]
+
+
+def small_fold(place, wire, values, bufs, out):
+    got, total = bufs
+    source, start, size = values, 0, 16
+    steps = ((FAR, place.far), (NEAR, place.near), (Y, place.y), (X, place.x), (CORE, place.core))
+    for mask, bit in steps:
+        here = pl.ds(start, size)
+        theirs = pl.ds(source_start(start, size) + (1 - bit) * size, size)
+        yield [wire.send(source.at[theirs], got.at[here], mask)]
+        mine = pl.ds(source_start(start, size) + bit * size, size)
+        total[here] = source[mine] + got[here]
+        source, start, size = total, start + size, size // 2
+    out[...] = total[pl.ds(start - 1, 1)]
+
+
+def source_start(start, size):
+    return 0 if start == 0 else start - 2 * size
 
 
 class Bits:
@@ -1039,6 +1349,38 @@
     return before
 
 
+@dataclasses.dataclass
+class Mixer:
+    reading: jax.Array
+    scores: jax.Array
+    share: jax.Array
+    branch: jax.Array
+    rows: jax.Array
+    normed: jax.Array
+    low: jax.Array
+    low_rank: jax.Array
+    rank: jax.Array
+    logits: jax.Array
+    keep: jax.Array
+    true_keep: jax.Array
+    written: jax.Array
+    survive: jax.Array
+    slots_in: jax.Array
+    slots_end: jax.Array
+    weights: list
+    raw: list
+    output: jax.Array
+    out_gain: jax.Array
+    ffn_gain: jax.Array
+    attn_gain: jax.Array
+
+
+def alive_rows(seq_cuts, seq, length):
+    positions = seq * length + jnp.arange(length)
+    starts = (positions[None, :] == 0) | (positions[None, :] == seq_cuts[:, None])
+    return jnp.where(starts, 0.0, 1.0).astype(F32)[:, None, :]
+
+
 class Plain:
     def __init__(self):
         self.seq, self.tp = lax.axis_index("seq"), lax.axis_index("tp")
@@ -1070,24 +1412,151 @@
     def small_sum(self, packed):
         return lax.psum_scatter(packed, ("seq", "tp"), scatter_dimension=0, tiled=True)[0]
 
-    def begin(self, packed, tokens, weights, w_output, ffn):
-        self.weights, self.w_output, self.ffn = weights, w_output, ffn
-        return self.small(packed), self.piece(tokens), [self.head_weight(w) for w in weights[:2]]
-
-    def scan_in(self, survive, state):
-        weights = [self.head_weight(w) for w in self.weights[2:]]
-        return self.scan((survive, state), False)[1], weights, self.output_weight(self.w_output)
-
-    def hidden(self, mixed, tokens, gain, cotangent):
+    def start(self, tokens, seq_cuts, weights, w_output, small, ffn, cotangent):
+        self.ffn = ffn
+        devices = self.at.seq_count * self.at.tp_count
+        gathered = self.small(jnp.concatenate([a.reshape(-1) for a in small]))
+        unpacked, taken = [], 0
+        for a in small:
+            part = gathered[:, taken : taken + a.size]
+            unpacked.append(part.reshape((devices * a.shape[0],) + a.shape[1:]))
+            taken += a.size
+        low, full_rank, full_bias, attn, out, ffn_gain = unpacked
+        slots = full_bias.shape[0] // H
+        rank = lax.dynamic_slice_in_dim(full_rank, self.head * slots, slots, 0).astype(F32)
+        bias = lax.dynamic_slice_in_dim(full_bias, self.head * slots, slots, 0).astype(F32)
+        rows = self.piece(tokens)
+        held, length, width = rows.shape
+        inputs = rows.reshape(held * length, width).astype(F32)
+        normed = (inputs * inverse_rms(inputs) * attn.astype(F32)).astype(BF)
+        low_rank = product(normed, low, NN).reshape(held, length, -1)
+        logits = jnp.einsum("mr,str->smt", rank, low_rank, precision=lax.Precision.HIGHEST)
+        logits = logits + bias[None, :, None]
+        true_keep, written = gates(logits)
+        alive = self.own_streams(alive_rows(seq_cuts, self.at.seq, length))
+        keep = true_keep * alive
+        weights = [self.head_weight(w) for w in weights]
+        raw = [product(normed, w, NN).reshape(held, length, -1) for w in weights]
+        hd = raw[0].shape[-1]
+        state, survive = per_stream(
+            piece_state,
+            [raw[0], raw[1], keep, written],
+            [((slots, 2 * hd), F32), ((slots, 1), F32)],
+            1 << 30,
+        )
+        slots_in = self.scan((survive[..., 0], state), False)[1]
+        key_raw, value_raw, query_raw, gate_raw = raw
+        reading, scores, share = per_stream(
+            piece_read,
+            [query_raw, key_raw, value_raw, keep, written, slots_in],
+            [((length, hd), F32), ((slots, length), F32), ((slots, length), F32)],
+            1 << 30,
+        )
+        read_normed = reading * inverse_rms(reading) * out.astype(F32)
+        branch = (read_normed * silu(gate_raw)).astype(BF).reshape(held * length, hd)
+        output = self.output_weight(w_output)
+        self.mixed = product(branch, output, NN).reshape(held, length, width)
+        return Mixer(
+            reading=reading,
+            scores=scores,
+            share=share,
+            branch=branch,
+            rows=rows,
+            normed=normed,
+            low=low,
+            low_rank=low_rank,
+            rank=rank,
+            logits=logits,
+            keep=keep,
+            true_keep=true_keep,
+            written=written,
+            survive=survive[..., 0],
+            slots_in=slots_in,
+            slots_end=survive * slots_in + state,
+            weights=weights,
+            raw=raw,
+            output=output,
+            out_gain=out.astype(F32),
+            ffn_gain=ffn_gain.astype(F32),
+            attn_gain=attn.astype(F32),
+        )
+
+    def feed_forward(self, tokens, gain, cotangent):
         streams, count, width = tokens.shape
-        hidden = tokens.astype(F32) + self.sum_piece(mixed)
-        hidden = hidden.reshape(streams * count, width)
-        ready = (hidden * inverse_rms(hidden) * gain).astype(BF)
-        cot = self.ffn_rows(cotangent.reshape(streams * count, width))
-        return hidden, self.ffn_rows(ready), cot
-
-    def ffn_weights(self):
-        return [lax.all_gather(w, "seq", axis=0, tiled=True) for w in self.ffn]
+        own_rows = streams * count
+        hidden = (tokens.astype(F32) + self.sum_piece(self.mixed)).reshape(own_rows, width)
+        scale = inverse_rms(hidden)
+        ffn_in = self.ffn_rows((hidden * scale * gain).astype(BF))
+        cot = self.ffn_rows(cotangent.reshape(own_rows, width))
+        down, gate, up = [lax.all_gather(w, "seq", axis=0, tiled=True) for w in self.ffn]
+        grad_product = product(cot, down, NN)
+        gate_pre, up_pre = product(ffn_in, gate, NN), product(ffn_in, up, NN)
+        sig = jax.nn.sigmoid(gate_pre)
+        act = (gate_pre * sig * up_pre).astype(BF)
+        slope = sig * (1.0 + gate_pre * (1.0 - sig))
+        grad_gate = (grad_product * up_pre * slope).astype(BF)
+        grad_up = (grad_product * gate_pre * sig).astype(BF)
+        grad = self.ffn_sum(product(grad_gate, gate, NT) + product(grad_up, up, NT))
+        self.gate_grad = self.ffn_grad(product(ffn_in, grad_gate, TN).astype(BF))
+        self.up_grad = self.ffn_grad(product(ffn_in, grad_up, TN).astype(BF))
+        self.down_sum = self.ffn_grad(product(cot, act, TN).astype(BF))
+        self.result = (hidden + self.ffn_sum(product(act, down, NT))).astype(BF)
+        gain_grad = jnp.sum(grad * hidden * scale, axis=0)
+        grad_hidden = cotangent.reshape(own_rows, width).astype(F32)
+        grad_hidden = grad_hidden + norm_back(hidden, scale, gain, grad)
+        return grad_hidden, gain_grad, self.piece(grad_hidden.astype(BF).reshape(cotangent.shape))
+
+    def ffn_grad(self, grad):
+        own = lax.psum_scatter(grad, "seq", scatter_dimension=0, tiled=True)
+        return own.astype(F32)
+
+    def mixer_back(self, mixer, grad_mixed):
+        reading, scores, share, branch_out = mixer.reading, mixer.scores, mixer.share, mixer.branch
+        streams, length, hd = reading.shape
+        slots = scores.shape[1]
+        key_raw, value_raw, query_raw, gate_raw = mixer.raw
+        grad_branch = product(grad_mixed, mixer.output, NT).reshape(reading.shape)
+        self.output_sum = self.output_grad(product(branch_out, grad_mixed, TN))
+        scale = inverse_rms(reading)
+        normed = reading * scale * mixer.out_gain
+        grad_gate = (grad_branch * normed * silu_slope(gate_raw)).astype(BF)
+        grad = grad_branch * silu(gate_raw)
+        gain_sum = jnp.sum(grad * reading * scale, axis=(0, 1))[None]
+        grad_read = norm_back(reading, scale, mixer.out_gain, grad)
+        grad_query, grad_k, grad_v, direct, back, own = per_stream(
+            piece_back,
+            [query_raw, key_raw, value_raw, mixer.keep, mixer.written]
+            + [mixer.slots_in, scores, share, grad_read],
+            [
+                ((length, hd), BF),
+                ((length, hd), F32),
+                ((length, hd), F32),
+                ((slots, 2 * hd), F32),
+                ((slots, length), F32),
+                ((slots, length), F32),
+            ],
+            1 << 30,
+        )
+        after = self.scan((mixer.survive, direct), True)[1]
+        self.head_sums = [
+            self.head_grad(product(mixer.normed, g.reshape(-1, hd), TN))
+            for g in (grad_query, grad_gate)
+        ]
+        return after, gain_sum, grad_query, grad_gate, grad_k, grad_v, back, own
+
+    def end(self, mixer, grads, normed_part, packed):
+        hd = grads[0].shape[-1]
+        heads = [
+            self.head_grad(product(mixer.normed, g.reshape(-1, hd), TN)) for g in grads
+        ]
+        heads = heads + self.head_sums + [self.output_sum]
+        return (
+            heads,
+            [self.gate_grad, self.up_grad, self.down_sum],
+            self.sum_piece(normed_part),
+            self.small_sum(packed),
+            self.result,
+        )
 
     def __init__(self):
         self.at = Plain()
@@ -1140,12 +1609,6 @@
         own = lax.psum_scatter(entire, ("seq", "tp"), scatter_dimension=0, tiled=True)
         return own.astype(F32)
 
-    def to_output(self, branch):
-        return branch
-
-    def from_output(self, grad):
-        return grad
-
     def scan(self, part, reverse):
         return plain_scan(part, self.at, reverse)
 
@@ -1153,21 +1616,10 @@
         entire = lax.all_gather(own, "tp", axis=0)
         return entire.reshape((-1,) + own.shape[1:])
 
-    def ffn_sum(self, work):
-        part = jnp.concatenate([work(0), work(1)], axis=0)
-        parts = part.reshape((self.at.tp_count, -1) + part.shape[1:])
-        own = lax.psum_scatter(parts.astype(BF), "tp", scatter_dimension=0, tiled=True)
+    def ffn_sum(self, part):
+        parts = part.astype(BF).reshape((self.at.tp_count, -1) + part.shape[1:])
+        own = lax.psum_scatter(parts, "tp", scatter_dimension=0, tiled=True)
         return own.reshape((-1,) + part.shape[1:]).astype(F32)
-
-    def ffn_weight(self, weight):
-        return PlainWhole(lax.all_gather(weight, "seq", axis=0, tiled=True))
-
-    def ffn_grad(self, grad):
-        own = lax.psum_scatter(grad.astype(BF), "seq", scatter_dimension=0, tiled=True)
-        return PlainWhole(own.astype(F32))
-
-    def tie(self, value, *after):
-        return value
 
 
 class BitMoves:
@@ -1175,148 +1627,459 @@
         self.at = Bits()
         self.head, self.member = lax.axis_index("tp"), 0
 
-    def begin(self, packed, tokens, weights, w_output, ffn):
+    def start(self, tokens, seq_cuts, weights, w_output, small, ffn, cotangent):
+        w_low, w_rank, bias, attn_gain, out_gain, ffn_gain = small
+        rank = w_low.shape[1]
+        gains = jnp.stack([attn_gain, ffn_gain], axis=1)
+        pack = jnp.concatenate([w_low, gains], axis=1)
+        pack = jnp.pad(pack, ((0, 0), (0, 128 - pack.shape[1])))
+        tall = w_rank.shape[0]
+        lines = jnp.concatenate([w_rank, bias[:, None]], axis=1)
+        lines = jnp.pad(lines, ((0, 0), (0, 128 - lines.shape[1])))
+        gain_line = jnp.pad(out_gain, (0, 128 - out_gain.shape[0]))[None]
+        lines = jnp.concatenate([lines, gain_line], axis=0)
+        lines = jnp.pad(lines, ((0, 16 - lines.shape[0]), (0, 0)))[None]
+        streams, count, width = tokens.shape
+        length = 4 * count
+        hd = width // 4
+        per = out_gain.shape[0]
+        slots = 8 * tall
+        head = (width, hd)
+        cut = (2, ffn[0].shape[0], ffn[0].shape[1] // 2)
+        ffn_shape = (4,) + cut
         block = turn_bits(w_output, False)
-        streams, count, width = tokens.shape
-        length = -(-packed.size // 2048) * 16
-        own = jnp.pad(packed, (0, length * 128 - packed.size)).reshape(1, length, 128)
-        self.rest, self.block = weights[2:], block
-        self.halves = [jnp.swapaxes(w.reshape(w.shape[0], 2, -1), 0, 1) for w in ffn]
-        ffn_shape = (4,) + self.halves[0].shape
-        head = (weights[0].shape[0] * 32, width // 4)
+        alive = alive_rows(seq_cuts, lax.axis_index("seq"), length)
+        state_shape, slim = (streams, slots, 2 * hd), (streams, slots, 128)
+        gate_shape = (streams, slots, length)
 
         def work(place, wire, given, outs, scratch):
+            pack, lines, tokens, alive, own_tokens = given[:5]
+            given = given[1:]
+            heads_in, block, ffn_in, cot = given[4:8], given[8], given[9:12], given[12]
+            pack_out, lines_out, low_out, logits, keep, true_keep, written = outs[:7]
+            survive, slots_in, slots_end, scores, share = outs[7:12]
+            rows_out, normed_out, reading_out, branch_out, hidden_out = outs[12:17]
+            heads_out, raws_out, output_out = outs[17:21], outs[21:25], outs[25]
+            ffn_out, cot_out, ffn_rows, grad_product = outs[26:29], outs[29], outs[30], outs[31]
+            rows, normed, state = scratch[:3]
+            heads, raws, cuts, scan = scratch[3:7], scratch[7:11], scratch[11:14], scratch[14:18]
+            output_w, reading, branch, traded, mixed = scratch[18:23]
+            hidden, ready, gain_rows, cot_rows, down = scratch[23:28]
+            fold_bufs = scratch[28:31]
+            here = Flags()
+
+            def fetch_rows():
+                yield from rows_gather(place, wire, tokens, rows)
+                here.raised("rows")
+                wire.keep(rows, rows_out)
+
+            def fetch_lines():
+                yield from small_gather(place, wire, lines, lines_out)
+                here.raised("lines")
+
+            def norm():
+                gain = jnp.transpose(pack_out[...].astype(F32))[rank : rank + 1]
+                steps = count // 16
+
+                def body(i, carry):
+                    stream, tp, part = i // (4 * steps), i // steps % 4, i % steps
+                    at = pl.multiple_of(part * 16, 16)
+                    x = rows[stream, tp, pl.ds(at, 16)].astype(F32)
+                    to = pl.multiple_of(i * 16, 16)
+                    normed[pl.ds(to, 16)] = (x * inverse_rms(x) * gain).astype(BF)
+                    return carry
+
+                lax.fori_loop(0, streams * 4 * steps, body, 0)
+
+            def project(index):
+                for s in range(streams):
+                    raws[index][s] = mm(normed[s * length : (s + 1) * length], heads[index][...], NN)
+                wire.spend(3.0)
+                here.raised(("raw", index))
+                wire.keep(heads[index], heads_out[index])
+                wire.keep(raws[index], raws_out[index])
+
+            def gains():
+                own = lines_out[...].astype(F32)[:, tall]
+                spot, turn_of = row((128, hd)), column((128, hd))
+                spread = jnp.where(spot == turn_of % per, 1.0, 0.0)
+                wide = mm(own, spread, NN)
+                here_is = row(wide.shape) == column(wide.shape) // per
+                out_row = jnp.sum(jnp.where(here_is, wide, 0.0), axis=0, keepdims=True)
+                gain_rows[0:1, :hd] = out_row
+                ffn_row = jnp.transpose(pack_out[...].astype(F32))[rank + 1 : rank + 2]
+                side = width // 8
+                for y in range(2):
+                    for m in range(4):
+                        to = pl.multiple_of((place.z_turn(m) * 2 + y) * side, 128)
+                        at = (y * 4 + m) * side
+                        gain_rows[1:2, pl.ds(to, side)] = ffn_row[:, at : at + side]
+
+            def read(s, carry):
+                values = piece_read(
+                    raws[2][s], raws[0][s], raws[1][s], keep[s], written[s], slots_in[s]
+                )
+                reading[s], scores[s], share[s] = values
+                return carry
+
+            def gated(s):
+                def chunk(part):
+                    at = pl.ds(pl.multiple_of(s * length + part.start, 16), part.size)
+                    values = reading[s, part]
+                    normed_read = values * inverse_rms(values) * gain_rows[0:1, :hd]
+                    branch[at] = (normed_read * silu(raws[3][s, part])).astype(BF)
+
+                row_loop(length, 32, chunk)
+
+            def finish(stream, rows, part):
+                values = own_tokens[stream, rows].astype(F32) + part
+                hidden[stream, rows] = values
+                normed = (values * inverse_rms(values) * gain_rows[1:2]).astype(BF)
+                size = width // 4
+                for m in range(4):
+                    there = pl.ds(pl.multiple_of(place.z_turn(m) * size, 128), size)
+                    ready[stream, rows, there] = normed[:, m * size : (m + 1) * size]
+
+            def to_rows():
+                yield here.wait("branch")
+                yield from heads_trade(place, wire, branch, traded)
+                here.raised("traded")
+                wire.keep(traded, branch_out)
+                yield here.wait("mixed")
+                yield from rows_fold(place, wire, mixed, *fold_bufs, finish)
+                wire.keep(hidden, hidden_out)
+                yield from plane_gather(place, wire, ready.at[0], ready.at[1], ffn_rows)
+
+            def fetch_down():
+                yield from ffn_gather(place, wire, ffn_in[0], cuts[0], down)
+                here.raised("down")
+                wire.keep(down, ffn_out[0])
+
+            def fetch_cot():
+                yield from plane_gather(place, wire, cot.at[0], cot.at[1], cot_rows)
+                here.raised("cot")
+                wire.keep(cot_rows, cot_out)
+
+            def product_grads():
+                yield here.wait("down", "cot")
+                for c in range(2):
+                    for h in range(2):
+                        values = cot_rows[c, h].reshape(4 * count, width)
+                        total = mm(values, down[...].reshape(width, ffn_shape[-1]), NN)
+                        grad_product[c, h] = total.astype(BF)
+                        wire.spend(1.5)
+                        yield []
+
+            def compute():
+                yield here.wait("rows", "pack")
+                norm()
+                wire.spend(3.0)
+                wire.keep(normed, normed_out)
+                yield here.wait("lines")
+                own = lines_out[pl.ds(place.tp * 8, 8)].astype(F32)[:, :tall].reshape(slots, 128)
+                factor = jnp.where(column(own.shape) < rank, own, 0.0)
+                for s in range(streams):
+                    low = mm(normed[s * length : (s + 1) * length], pack_out[...], NN)
+                    low_out[s] = low
+                    f = mm_fine(factor, low, NT) + own[:, rank : rank + 1]
+                    logits[s] = f
+                    kept, wrote = gates(f)
+                    true_keep[s] = kept
+                    written[s] = wrote
+                    keep[s] = kept * alive[s]
+                wire.spend(2.0)
+                for index in range(2):
+                    yield here.wait(index)
+                    project(index)
+                for s in range(streams):
+                    part, left = piece_state(raws[0][s], raws[1][s], keep[s], written[s])
+                    state[s] = part
+                    survive[s] = jnp.broadcast_to(left, slim[1:])
+                wire.spend(3.0)
+                here.raised("state")
+                for index in (2, 3):
+                    yield here.wait(index)
+                    project(index)
+                gains()
+                yield here.wait("slots")
+                lax.fori_loop(0, streams, read, 0)
+                wire.spend(10.0)
+                for s in range(streams):
+                    gated(s)
+                wire.spend(2.0)
+                here.raised("branch")
+                wire.keep(reading, reading_out)
+                yield here.wait("traded", 4)
+                wire.keep(output_w, output_out)
+                for s in range(streams):
+                    rows_in = traded[s * length : (s + 1) * length]
+                    total = mm(rows_in, output_w[...].reshape(hd, width), NN)
+                    mixed[s] = total.astype(BF).reshape(mixed.shape[1:])
+                wire.spend(2.5)
+                here.raised("mixed")
+
+            def exchange():
+                yield here.wait("state")
+                yield from pieces_scan(place, wire, False, survive, state, slots_in, scan)
+                for s in range(streams):
+                    slots_end[s] = survive[s][:, :1] * slots_in[s] + state[s]
+                here.raised("slots")
+
             wire.run(
-                small_gather(place, wire, given[0], outs[0]),
-                head_gather(place, wire, given[2], outs[2]),
-                head_gather(place, wire, given[3], outs[3]),
-                rows_gather(place, wire, given[1], outs[1]),
-                ffn_gather(place, wire, given[4], outs[4], 2),
+                fetch_lines(),
+                head_gather(place, wire, pack, pack_out, here, "pack", True),
+                fetch_rows(),
+                exchange(),
+                to_rows(),
+                *[
+                    head_gather(place, wire, w, o, here, i)
+                    for i, (w, o) in enumerate(zip(heads_in, heads))
+                ],
+                output_gather(place, wire, block, output_w, here, 4),
+                fetch_down(),
+                fetch_cot(),
+                ffn_gather(place, wire, ffn_in[1], cuts[1], ffn_out[1]),
+                ffn_gather(place, wire, ffn_in[2], cuts[2], ffn_out[2]),
+                product_grads(),
+                compute(),
             )
 
-        small, rows, key_w, value_w, self.down = comm_call(
+        vmem = pltpu.VMEM
+        plane = (2, 2, 4, count, width)
+        flat = (streams * length, width)
+        raw = (streams, length, hd)
+        mixed_shape = (streams, 2, 2, count, width)
+        group = (2, 2, length, ffn_shape[-1])
+        outs = comm_call(
             work,
             1,
             (CORE, X, X | CORE, Y, NEAR, FAR),
-            [own, self.mixer_order(tokens), weights[0], weights[1], self.halves[0]],
-            [False] * 5,
+            [pack, lines, self.mixer_order(tokens), alive, tokens]
+            + list(weights)
+            + [block]
+            + list(ffn)
+            + [self.ffn_order(cotangent)],
+            [False, False, False, True, True] + [False] * 5 + [True] * 3 + [False],
             [
-                ((32, length, 128), BF),
+                ((width, 128), BF),
+                ((32, 16, 128), BF),
+                ((streams, length, 128), F32),
+                (gate_shape, F32),
+                (gate_shape, F32),
+                (gate_shape, F32),
+                (gate_shape, F32),
+                (slim, F32),
+                (state_shape, F32),
+                (state_shape, F32),
+                (gate_shape, F32),
+                (gate_shape, F32),
                 ((streams, 4, count, width), BF),
-                (head, BF),
-                (head, BF),
-                (ffn_shape, BF),
-            ],
-            [False] * 5,
-            [],
-            40,
-            8,
+                (flat, BF),
+                (raw, F32),
+                ((flat[0], hd), BF),
+                (tokens.shape, F32),
+            ]
+            + [(head, BF)] * 4
+            + [(raw, F32)] * 4
+            + [((4, 2) + block.shape, BF)]
+            + [(ffn_shape, BF)] * 3
+            + [(plane, BF)] * 2
+            + [(group, BF)],
+            [True] * 12 + [False] * 19 + [True],
+            [vmem((streams, 4, count, width), BF), vmem(flat, BF), vmem(state_shape, F32)]
+            + [vmem(head, BF)] * 4
+            + [vmem(raw, F32)] * 4
+            + [vmem(cut, BF)] * 3
+            + scan_buffers(state_shape, slim)
+            + [
+                vmem((4, 2) + block.shape, BF),
+                vmem(raw, F32),
+                vmem((flat[0], hd), BF),
+                vmem((flat[0], hd), BF),
+                vmem(mixed_shape, BF),
+                vmem(tokens.shape, F32),
+                vmem(tokens.shape, BF),
+                vmem((8, width), F32),
+                vmem(plane, BF),
+                vmem(ffn_shape, BF),
+            ]
+            + rows_buffers(mixed_shape),
+            150,
+            50,
+            mb=63,
         )
-        small = small.reshape(32, length * 128)[:, : packed.size]
-        return small, rows.reshape(streams, 4 * count, width), [key_w, value_w]
-
-    def scan_in(self, survive, state):
-        streams, slots, width = state.shape
-        head = (self.rest[0].shape[0] * 32, self.rest[0].shape[1] // 4)
-        rows = self.block.shape
-        spread = jnp.broadcast_to(survive[..., None], (streams, slots, 128))
+        pack, lines, low_rank, logits, keep, true_keep, written = outs[:7]
+        survive, slots_in, slots_end, scores, share = outs[7:12]
+        rows, normed, reading, branch, self.hidden_rows = outs[12:17]
+        self.down, self.gate, self.up = outs[26:29]
+        self.cot, self.ffn_in, self.grad_product = outs[29:32]
+        own = lax.dynamic_slice_in_dim(lines, self.head * 8, 8, 0)[:, :tall]
+        gains = self.mixer_unorder(jnp.swapaxes(pack[:, rank : rank + 2], 0, 1)).astype(F32)
+        return Mixer(
+            reading=reading,
+            scores=scores,
+            share=share,
+            branch=branch,
+            rows=rows.reshape(streams, length, width),
+            normed=normed,
+            low=pack[:, :rank],
+            low_rank=low_rank[..., :rank],
+            rank=own[..., :rank].reshape(slots, rank).astype(F32),
+            logits=logits,
+            keep=keep,
+            true_keep=true_keep,
+            written=written,
+            survive=survive[..., 0],
+            slots_in=slots_in,
+            slots_end=slots_end,
+            weights=list(outs[17:21]),
+            raw=list(outs[21:25]),
+            output=outs[25].reshape(8 * block.shape[0], width),
+            out_gain=lines[:, tall, : out_gain.shape[0]].reshape(-1).astype(F32),
+            ffn_gain=gains[1],
+            attn_gain=gains[0],
+        )
+
+    def feed_forward(self, tokens, gain, cotangent):
+        streams, count, width = tokens.shape
+        plane = (2, 2, 4, count, width)
+        half = plane[1:]
+        ffn = self.down.shape
+        cols = ffn[-1]
+        many = 4 * count
+        group = (2, 2, many, cols)
+        z_line = [(z, y) for z in (3, 1, 2, 0) for y in range(2)]
+        side = ffn[2]
 
         def work(place, wire, given, outs, scratch):
+            hidden, gain, cot, rows_in, grad_in, gate_in, up_in = given
+            grad_hidden, gain_sum, act, rows_out, gate_out, up_out = outs
+            ffn_in, turned, part, up_grad, gate, up, grad_gate, grad_up, gate_grad = scratch[:9]
+            plane_bufs, gate_bufs = scratch[9:14], scratch[14:]
+            loaded = Flags()
+            for c in range(2):
+                for h in range(2):
+                    loaded.raised((c, h), [wire.keep(rows_in.at[c, h], ffn_in.at[c, h])])
+                    if (c, h) == (0, 0):
+                        loaded.raised("gate", [wire.keep(gate_in, gate)])
+                        loaded.raised("up", [wire.keep(up_in, up)])
+                        loaded.raised("grad", [wire.keep(grad_in, grad_up)])
+            gain_sum[...] = jnp.zeros_like(gain_sum)
+
+            made, gate_made = Flags(), Flags()
+
+            def rows_of(ref, c, h):
+                return ref[c, h].reshape(many, width)
+
+            def weight(ref):
+                return ref[...].reshape(width, cols)
+
+            def compute():
+                groups = [(c, h) for c in range(2) for h in range(2)]
+                for c, h in groups:
+                    yield loaded.wait((c, h), "gate", "up", "grad")
+                    x = rows_of(ffn_in, c, h)
+                    gate_pre = mm(x, weight(gate), NN)
+                    up_pre = mm(x, weight(up), NN)
+                    grad = grad_up[c, h].astype(F32)
+                    sig = jax.nn.sigmoid(gate_pre)
+                    act[c, h] = (gate_pre * sig * up_pre).astype(BF)
+                    slope = sig * (1.0 + gate_pre * (1.0 - sig))
+                    grad_gate[c, h] = (grad * up_pre * slope).astype(BF)
+                    grad_up[c, h] = (grad * gate_pre * sig).astype(BF)
+                    wire.spend(4.0)
+                for c in (1, 0):
+                    for h in range(2):
+                        yield []
+                        total = mm(grad_gate[c, h], weight(gate), NT)
+                        total = total + mm(grad_up[c, h], weight(up), NT)
+                        part[c, h] = total.astype(BF).reshape(half[1:])
+                        wire.spend(3.0)
+                        made.raised((("near", "far")[c], h))
+
+                def columns(key):
+                    at = (key[0] * 2 + key[1]) * side
+                    return ffn_in[:, :, :, :, at : at + side].reshape(4 * many, side)
+
+                def put(key, value):
+                    gate_grad[key[0], key[1]] = value.astype(BF)
+
+                def gate_rows():
+                    return grad_gate[...].reshape(4 * many, cols)
+
+                yield from weight_tiles(wire, columns, z_line, gate_rows, put, gate_made)
+
+                def put_up(key, value):
+                    up_grad[key[0], key[1]] = value.astype(BF)
+                    wire.keep(up_grad.at[key[0], key[1]], up_out.at[key[0], key[1]])
+
+                def up_rows_all():
+                    return grad_up[...].reshape(4 * many, cols)
+
+                yield from weight_tiles(wire, columns, z_line, up_rows_all, put_up)
+
+            def finish_grad(stream, rows, load):
+                part = z_parts(place, load, width)
+                held = hidden[stream, rows]
+                scale = inverse_rms(held)
+                gain_sum[...] += jnp.sum(part * held * scale, axis=0, keepdims=True)
+                total = cot[stream, rows].astype(F32) + norm_back(held, scale, gain[...], part)
+                grad_hidden[stream, rows] = total
+                turned[stream, rows] = total.astype(BF)
+
+            def back_rows():
+                yield from plane_fold(
+                    place, wire, part.at[0], part.at[1], plane_bufs, finish_grad, made
+                )
+                yield from rows_gather(place, wire, turned, rows_out)
+
             wire.run(
-                pieces_scan(place, wire, False, given[0], given[1], outs[0], scratch),
-                head_gather(place, wire, given[2], outs[1]),
-                head_gather(place, wire, given[3], outs[2]),
-                output_gather(place, wire, given[4], outs[3]),
-                ffn_gather(place, wire, given[5], outs[4], 2),
-                ffn_trade(place, wire, given[6], outs[5]),
+                back_rows(),
+                ffn_fold(place, wire, gate_grad, gate_bufs, gate_out, gate_made),
+                compute(),
             )
 
-        ffn_shape = (4,) + self.halves[0].shape
-        slots_in, query_w, gate_w, output_w, self.gate, self.up = comm_call(
-            work,
-            2,
-            (CORE, X, X | CORE, Y, NEAR, FAR),
-            [spread, state] + list(self.rest) + [self.block] + self.halves[1:],
-            [True, True] + [False] * 5,
-            [
-                (state.shape, F32),
-                (head, BF),
-                (head, BF),
-                ((4, 2) + rows, BF),
-                (ffn_shape, BF),
-                (ffn_shape, BF),
-            ],
-            [True] + [False] * 5,
-            scan_buffers(state.shape, spread.shape),
-            60,
-            8,
-        )
-        return slots_in, [query_w, gate_w], output_w.reshape(8 * rows[0], rows[1])
-
-    def hidden(self, mixed, tokens, gain, cotangent):
-        streams, count, width = tokens.shape
-        cot = self.ffn_order(cotangent)
-        plane = (2, 2, 4, count, width)
-
-        def work(place, wire, given, outs, scratch):
-            ready, sums, got_core, got_x = scratch
-            rows = hidden_rows(
-                place, wire, given[0], given[1], given[2], outs[0], ready, sums, got_core, got_x
-            )
-
-            def then():
-                yield from rows
-                yield from plane_gather(place, wire, ready.at[0], ready.at[1], outs[1])
-
-            wire.run(
-                then(),
-                ffn_spread(place, wire, given[4].at[0], outs[3]),
-                plane_gather(place, wire, given[3].at[0], given[3].at[1], outs[2]),
-            )
-
-        hidden, ready, cot, self.up = comm_call(
+        vmem = pltpu.VMEM
+        outs = comm_call(
             work,
             3,
             (CORE, X, Y, NEAR, FAR),
-            [mixed.reshape(streams, 2, 2, count, width), tokens, gain[None], cot, self.up],
-            [True, True, True, False, False],
+            [self.hidden_rows, gain[None], cotangent, self.ffn_in, self.grad_product]
+            + [self.gate, self.up],
+            [True] * 3 + [False] * 4,
             [
                 ((streams, count, width), F32),
-                (plane, BF),
-                (plane, BF),
-                (self.up.shape, BF),
+                ((1, width), F32),
+                (group, BF),
+                ((streams, 4, count, width), BF),
+                (ffn[1:], BF),
+                (ffn, BF),
             ],
-            [True, False, False, False],
+            [True] * 3 + [False] * 3,
             [
-                pltpu.VMEM((streams, count, width), BF),
-                pltpu.VMEM((streams, count, width), BF),
-                pltpu.VMEM((streams, 2, count, width), BF),
-                pltpu.VMEM((streams, count, width), BF),
-            ],
+                vmem(plane, BF),
+                vmem((streams, count, width), BF),
+                vmem(plane, BF),
+                vmem(ffn, BF),
+                vmem(ffn, BF),
+                vmem(ffn, BF),
+                vmem(group, BF),
+                vmem(group, BF),
+                vmem(ffn, BF),
+            ]
+            + plane_buffers(half)
+            + ffn_buffers(ffn),
             60,
-            8,
+            24,
+            mb=63,
         )
-        flat = 16 * count
-        return (
-            hidden.reshape(streams * count, width),
-            ready.reshape(flat, width),
-            cot.reshape(flat, width),
-        )
-
-    def ffn_weights(self):
-        return [w.reshape(-1, w.shape[-1]) for w in (self.down, self.gate, self.up)]
-
-    def small_sum(self, packed):
-        return fold_all(packed, self.at)[0]
+        grad_hidden, gain_grad, self.act = outs[:3]
+        rows, self.gate_grad, self.up_part = outs[3:]
+        rows = rows.reshape(streams, 4 * count, width)
+        return grad_hidden.reshape(streams * count, width), gain_grad[0], rows
 
     def own_streams(self, values):
         return values
-
-    def piece(self, own):
-        return spread_tp(own, self.at)
-
-    def sum_piece(self, part):
-        return fold_tp(part, self.at)
 
     def mixer_order(self, values):
         lead, width = values.shape[:-1], values.shape[-1]
@@ -1331,58 +2094,317 @@
     def ffn_order(self, values):
         return z_relative(values, self.at.z, values.ndim - 1)
 
-    ffn_unorder = ffn_order
-
-    def head_weight(self, weight):
-        return gather_head(weight, self.at)
-
-    def head_grad(self, grad):
-        return fold_head(grad, self.at)
-
-    def output_weight(self, weight):
-        return gather_output(weight, self.at)
-
-    def output_grad(self, grad):
-        return fold_output(grad, self.at)
-
-    def to_output(self, branch):
+    def mixer_back(self, mixer, grad_mixed):
+        reading, scores, share, branch_out = mixer.reading, mixer.scores, mixer.share, mixer.branch
+        streams, length, hd = reading.shape
+        rows, width = grad_mixed.shape
+        slots = scores.shape[1]
+        state_shape, slim = (streams, slots, 2 * hd), (streams, slots, 128)
+        ffn = self.up_part.shape
+        line = (4, 2, hd // 8, width)
+        head = (2, 4, width // 8, hd)
+        own = (head[2] // 4, width)
+        raw, gate_shape = (streams, length, hd), (streams, slots, length)
+        survive = jnp.broadcast_to(mixer.survive[..., None], slim)
+        key_raw, value_raw, query_raw, gate_raw = mixer.raw
+
         def work(place, wire, given, outs, scratch):
-            wire.run(heads_trade(place, wire, given[0], outs[0]))
-
-        (out,) = comm_call(
+            grad_mixed, output_w, survive, out_gain = given[:4]
+            after, gain_sum, grad_query, grad_gate, grad_k, grad_v, back, own_flow = outs[:8]
+            up_out, output_out, query_out, gate_out = outs[8:]
+            loads = {
+                key: (source, target)
+                for key, source, target in zip(
+                    ("reading", "gate", "query", "key", "value", "keep", "written")
+                    + ("scores", "share", "slots", "branch", "normed", "up"),
+                    given[4:],
+                    scratch,
+                )
+            }
+            here, up_made, lines_made = Flags(), Flags(), Flags()
+            heads_made = [Flags(), Flags()]
+
+            def load(*keys):
+                for key in keys:
+                    here.raised(key, [wire.keep(*loads[key])])
+
+            kept = {key: pair[1] for key, pair in loads.items()}
+            sent, got, grad_read, direct, output_part, query_part, gate_part = scratch[13:20]
+            scan, up_bufs = scratch[20:24], scratch[24:27]
+            lines, query_bufs, gate_bufs = scratch[27:31], scratch[31:35], scratch[35:39]
+            load("up", "branch", "reading", "gate", "normed", "query", "key", "value")
+            load("keep", "written", "scores", "share", "slots")
+            gain_sum[...] = jnp.zeros_like(gain_sum)
+
+            def returned():
+                yield here.wait("sent")
+                yield from heads_return(place, wire, sent, got)
+                here.raised("got")
+
+            def scanned():
+                yield here.wait("direct")
+                yield from pieces_scan(place, wire, True, survive, direct, after, scan)
+
+            def up_rows():
+                yield here.wait("up")
+                yield from ffn_fold(place, wire, kept["up"], up_bufs, up_out)
+
+            def gated(s):
+                def chunk(part):
+                    at = pl.ds(pl.multiple_of(s * length + part.start, 16), part.size)
+                    values, opened = kept["reading"][s, part], kept["gate"][s, part]
+                    grad = got[at].astype(F32)
+                    scale = inverse_rms(values)
+                    normed = values * scale * out_gain[...]
+                    grad_gate[s, part] = (grad * normed * silu_slope(opened)).astype(BF)
+                    grad = grad * silu(opened)
+                    gain_sum[...] += jnp.sum(grad * values * scale, axis=0, keepdims=True)
+                    grad_read[s, part] = norm_back(values, scale, out_gain[...], grad)
+
+                row_loop(length, 32, chunk)
+
+            def streams_back(s, carry):
+                results = piece_back(
+                    *[kept[key][s] for key in ("query", "key", "value", "keep", "written")],
+                    *[kept[key][s] for key in ("slots", "scores", "share")],
+                    grad_read[s],
+                )
+                targets = (grad_query, grad_k, grad_v, direct, back, own_flow)
+                for target, result in zip(targets, results):
+                    target[s] = result.astype(target.dtype)
+                return carry
+
+            def compute():
+                half = rows // 2
+                for at in (0, half):
+                    part = mm(grad_mixed[at : at + half], output_w[...], NT)
+                    sent[at : at + half] = part.astype(BF)
+                wire.spend(3.0)
+                here.raised("sent")
+                yield here.wait("branch")
+                block = hd // 4
+                for m in (3, 1, 2, 0):
+                    yield []
+                    cols = kept["branch"][:, m * block : (m + 1) * block]
+                    total = mm(cols, grad_mixed[...], TN)
+                    output_part[m] = total.astype(BF).reshape(line[1:])
+                    wire.spend(1.2)
+                    lines_made.raised(m)
+                yield here.wait("got", "reading", "gate")
+                for s in range(streams):
+                    gated(s)
+                wire.spend(2.0)
+                yield here.wait("normed")
+                yield from head_tiles(
+                    wire,
+                    kept["normed"],
+                    lambda: grad_gate[...].reshape(rows, hd),
+                    gate_part,
+                    heads_made[1],
+                )
+                yield here.wait("query", "key", "value", "keep", "written", "scores", "share", "slots")
+                lax.fori_loop(0, streams, streams_back, 0)
+                wire.spend(13.0)
+                here.raised("direct")
+                yield from head_tiles(
+                    wire,
+                    kept["normed"],
+                    lambda: grad_query[...].reshape(rows, hd),
+                    query_part,
+                    heads_made[0],
+                )
+
+            wire.run(
+                returned(),
+                scanned(),
+                up_rows(),
+                output_fold(place, wire, output_part, lines, output_out, lines_made),
+                head_fold(place, wire, gate_part, gate_bufs, gate_out, heads_made[1]),
+                head_fold(place, wire, query_part, query_bufs, query_out, heads_made[0]),
+                compute(),
+            )
+
+        vmem = pltpu.VMEM
+        later = [
+            reading,
+            gate_raw,
+            query_raw,
+            key_raw,
+            value_raw,
+            mixer.keep,
+            mixer.written,
+            scores,
+            share,
+            mixer.slots_in,
+            branch_out,
+            mixer.normed,
+            self.up_part,
+        ]
+        outs = comm_call(
             work,
-            4,
-            (CORE, X, X | CORE),
-            [branch],
-            [False],
-            [(branch.shape, BF)],
-            [False],
-            [],
-            4,
-            1,
+            7,
+            (CORE, X, X | CORE, Y, NEAR, FAR),
+            [grad_mixed, mixer.output, survive, mixer.out_gain[None]] + later,
+            [True] * 4 + [False] * len(later),
+            [
+                (state_shape, F32),
+                ((1, hd), F32),
+                (raw, BF),
+                (raw, BF),
+                (raw, F32),
+                (raw, F32),
+                (gate_shape, F32),
+                (gate_shape, F32),
+                (ffn[1:], BF),
+                (line[2:], BF),
+                (own, BF),
+                (own, BF),
+            ],
+            [True] * 8 + [False] * 4,
+            [vmem(a.shape, a.dtype) for a in later]
+            + [
+                vmem((rows, hd), BF),
+                vmem((rows, hd), BF),
+                vmem(raw, F32),
+                vmem(state_shape, F32),
+                vmem(line, BF),
+                vmem(head, BF),
+                vmem(head, BF),
+            ]
+            + scan_buffers(state_shape, slim)
+            + ffn_buffers(ffn)
+            + line_buffers(line[2], line[3])
+            + line_buffers(head[2], head[3])
+            + line_buffers(head[2], head[3]),
+            60,
+            30,
+            mb=62,
         )
-        return out
-
-    def from_output(self, grad):
-        return rows_to_heads(grad, self.at)
-
-    def scan(self, part, reverse):
-        return scan_pieces(part, self.at, reverse)
-
-    def ffn_rows(self, own):
-        return spread_plane(own)
-
-    def ffn_sum(self, work):
-        return fold_plane(work)
-
-    def ffn_weight(self, weight):
-        return FfnGather(weight, self.at)
-
-    def ffn_grad(self, grad):
-        return FfnFold(grad, self.at)
-
-    def tie(self, value, *after):
-        return tie(value, *after)
+        self.up_grad, output_sum, query_sum, gate_sum = outs[8:]
+        self.output_sum = turn_bits(output_sum, True)
+        self.head_sums = [query_sum, gate_sum]
+        return outs[:8]
+
+    def end(self, mixer, grads, normed_part, packed):
+        streams, positions, width = normed_part.shape
+        count = positions // 4
+        part_shape = (streams, 2, 2, count, width)
+        hd = grads[0].shape[-1]
+        rows = streams * positions
+        head = (2, 4, width // 8, hd)
+        own = (head[2] // 4, width)
+        length = -(-packed.shape[1] // 2048) * 16
+        packed = jnp.pad(packed, ((0, 0), (0, length * 128 - packed.shape[1])))
+        plane, group, ffn = self.cot.shape, self.act.shape, self.down.shape
+        half, cols, side = plane[1:], ffn[-1], ffn[2]
+        many = half[1] * half[2]
+        z_line = [(z, y) for z in (3, 1, 2, 0) for y in range(2)]
+
+        def work(place, wire, given, outs, scratch):
+            normed_part, packed, values = given[:3]
+            normed_out, small_out, result, key_out, value_out, down_out = outs
+            loads = dict(
+                zip(("key", "value", "normed", "act", "cot", "down"), zip(given[3:], scratch))
+            )
+            kept = {key: pair[1] for key, pair in loads.items()}
+            down_grad, parts = scratch[6], scratch[7:9]
+            small, sums = scratch[9:11], scratch[11:14]
+            lines = [scratch[14:18], scratch[18:22]]
+            plane_bufs, fold_bufs = scratch[22:27], scratch[27:]
+            part = kept["cot"]
+            here, made, down_made = Flags(), Flags(), Flags()
+            heads_made = [Flags(), Flags()]
+            for key in ("cot", "act", "key", "normed", "value", "down"):
+                here.raised(key, [wire.keep(*loads[key])])
+
+            def finish(stream, rows, total):
+                normed_out[stream, rows] = total
+
+            def finish_result(stream, rows, load):
+                total = values[stream, rows] + z_parts(place, load, width)
+                result[stream, rows] = total.astype(BF)
+
+            def compute():
+                yield here.wait("cot", "act")
+
+                def columns(key):
+                    at = (key[0] * 2 + key[1]) * side
+                    return kept["cot"][:, :, :, :, at : at + side].reshape(4 * many, side)
+
+                def put(key, value):
+                    down_grad[key[0], key[1]] = value.astype(BF)
+
+                def act_rows():
+                    return kept["act"][...].reshape(4 * many, cols)
+
+                yield from weight_tiles(wire, columns, z_line, act_rows, put, down_made)
+                yield here.wait("normed", "key", "value")
+                for index, key in enumerate(("key", "value")):
+                    grad = kept[key]
+                    yield from head_tiles(
+                        wire,
+                        kept["normed"],
+                        lambda: grad[...].reshape(rows, hd),
+                        parts[index],
+                        heads_made[index],
+                    )
+                yield here.wait("down")
+                for c in (1, 0):
+                    for h in range(2):
+                        total = mm(kept["act"][c, h], kept["down"][...].reshape(width, cols), NT)
+                        part[c, h] = total.astype(BF).reshape(half[1:])
+                        wire.spend(2.0)
+                        made.raised((("near", "far")[c], h))
+                        yield []
+
+            wire.run(
+                rows_fold(place, wire, normed_part, *sums, finish),
+                small_fold(place, wire, packed, small, small_out),
+                ffn_fold(place, wire, down_grad, fold_bufs, down_out, down_made),
+                head_fold(place, wire, parts[0], lines[0], key_out, heads_made[0]),
+                head_fold(place, wire, parts[1], lines[1], value_out, heads_made[1]),
+                plane_fold(place, wire, part.at[0], part.at[1], plane_bufs, finish_result, made),
+                compute(),
+            )
+
+        vmem = pltpu.VMEM
+        later = list(grads) + [mixer.normed, self.act, self.cot, self.down]
+        normed, small, result, key_sum, value_sum, self.down_grad = comm_call(
+            work,
+            8,
+            (CORE, X, X | CORE, Y, NEAR, FAR),
+            [normed_part.reshape(part_shape), packed.reshape(32, length, 128), self.hidden_rows]
+            + later,
+            [True] * 3 + [False] * len(later),
+            [
+                ((streams, count, width), F32),
+                ((1, length, 128), F32),
+                (self.hidden_rows.shape, BF),
+                (own, BF),
+                (own, BF),
+                (ffn[1:], BF),
+            ],
+            [True] * 3 + [False] * 3,
+            [vmem(a.shape, a.dtype) for a in later]
+            + [vmem(ffn, BF), vmem(head, BF), vmem(head, BF)]
+            + [vmem((32, length, 128), F32)] * 2
+            + rows_buffers(part_shape)
+            + line_buffers(head[2], head[3])
+            + line_buffers(head[2], head[3])
+            + plane_buffers(half)
+            + ffn_buffers(ffn),
+            80,
+            16,
+            mb=62,
+        )
+
+        def both(parts):
+            return jnp.concatenate([parts[0], parts[1]], axis=1).astype(F32)
+
+        heads = [key_sum, value_sum] + self.head_sums + [self.output_sum]
+        heads = [h.astype(F32) for h in heads]
+        ffn_grads = [both(g) for g in (self.gate_grad, self.up_grad, self.down_grad)]
+        return heads, ffn_grads, normed, small.reshape(-1), result
 
 
 def on_device(
@@ -1406,148 +2428,38 @@
 ):
     seq_count, tp_count = lax.axis_size("seq"), lax.axis_size("tp")
     devices = seq_count * tp_count
-    seq_rank = lax.axis_index("seq")
     move = BitMoves() if (seq_count, tp_count) == (8, 4) else PlainMoves()
     streams, local_len, width = tokens.shape
-    rank = w_low.shape[1]
-
     small = (w_low, w_rank, gate_bias, attn_gain, out_gain, ffn_gain)
-    packed = jnp.concatenate([a.reshape(-1) for a in small])
-    gathered, rows_in, (key_w, value_w) = move.begin(
-        packed, tokens, (w_key, w_value, w_query, w_gate_out), w_output, (w_down, w_gate, w_up)
+    mixer = move.start(
+        tokens,
+        seq_cuts,
+        (w_key, w_value, w_query, w_gate_out),
+        w_output,
+        small,
+        (w_down, w_gate, w_up),
+        cotangent,
     )
-    unpacked, taken = [], 0
-    for a in small:
-        part = gathered[:, taken : taken + a.size]
-        unpacked.append(part.reshape((devices * a.shape[0],) + a.shape[1:]))
-        taken += a.size
-    full_low, full_rank, full_bias, full_attn, full_out, full_ffn = unpacked
-    slots = full_bias.shape[0] // H
-    head_rank = lax.dynamic_slice_in_dim(full_rank, move.head * slots, slots, 0).astype(F32)
-    head_bias = lax.dynamic_slice_in_dim(full_bias, move.head * slots, slots, 0).astype(F32)
-    attn_vec, ffn_vec = full_attn.astype(F32), full_ffn.astype(F32)
-    out_vec = full_out.astype(F32)
-    order_low = jnp.swapaxes(move.mixer_order(jnp.swapaxes(full_low, 0, 1)), 0, 1)
-
-    held, piece_len = rows_in.shape[:2]
+    key_rows, value_rows = mixer.raw[:2]
+    key_w, value_w, query_w, gate_w = mixer.weights
+    keep, true_keep, written = mixer.keep, mixer.true_keep, mixer.written
+    slots_end = mixer.slots_end
+    ffn_vec, attn_vec = mixer.ffn_gain, mixer.attn_gain
+    normed, low_rank = mixer.normed, mixer.low_rank
+    held, piece_len, hd = key_rows.shape
+    slots, rank = keep.shape[1], low_rank.shape[-1]
     flat = held * piece_len
-    positions = seq_rank * piece_len + jnp.arange(piece_len)
-    cuts = move.own_streams(seq_cuts)
-    starts = (positions[None, :] == 0) | (positions[None, :] == cuts[:, None])
-    inputs = rows_in.reshape(flat, width).astype(F32)
+    inputs = mixer.rows.reshape(flat, width).astype(F32)
     attn_scale = inverse_rms(inputs)
-    normed = (inputs * attn_scale * move.mixer_order(attn_vec)).astype(BF)
-    low_rank = product(normed, order_low, NN)
-    logits = lax.dot_general(
-        head_rank,
-        low_rank.reshape(held, piece_len, rank),
-        (((1,), (2,)), ((), ())),
-        precision=lax.Precision.HIGHEST,
+    gflop = 1000 * 1000 * 1000
+    own_tokens = tokens.astype(F32)
+
+    grad_hidden, grad_ffn_gain, grad_mixed = move.feed_forward(tokens, ffn_vec, cotangent)
+
+    after, grad_out_gain, grad_query, grad_gate, grad_k, grad_v, back, own = move.mixer_back(
+        mixer, grad_mixed.reshape(flat, width)
     )
-    logits = jnp.swapaxes(logits, 0, 1) + head_bias[None, :, None]
-    log_keep = jax.nn.log_sigmoid(logits) / GATE_SCALE
-    true_keep, written = jnp.exp(log_keep), -jnp.expm1(log_keep)
-    keep = jnp.where(starts[:, None, :], 0.0, true_keep)
-
-    def project(weight):
-        out = product(normed, weight, NN)
-        return out.reshape(held, piece_len, weight.shape[1])
-
-    key_rows, value_rows = project(key_w), project(value_w)
-    hd = key_rows.shape[-1]
-    gflop = 1000 * 1000 * 1000
-    state, survive = per_stream(
-        piece_state,
-        [key_rows, value_rows, keep, written],
-        [((slots, 2 * hd), F32), ((slots, 1), F32)],
-        gflop,
-    )
-    survive = survive[..., 0]
-    slots_in, (query_w, gate_w), output_w = move.scan_in(survive, state)
-    query, gate_out = project(query_w), project(gate_w)
-    slots_end = survive[..., None] * slots_in + state
-    reading, scores, share = per_stream(
-        piece_read,
-        [query, key_rows, value_rows, keep, written, slots_in],
-        [
-            ((piece_len, hd), F32),
-            ((slots, piece_len), F32),
-            ((slots, piece_len), F32),
-        ],
-        gflop,
-    )
-    read_scale = inverse_rms(reading)
-    gate_act = silu(gate_out)
-    read_normed = reading * read_scale * out_vec
-    branch = (read_normed * gate_act).astype(BF).reshape(flat, hd)
-    branch_out = move.to_output(branch)
-    mixed = product(branch_out, output_w, NN).reshape(held, piece_len, width)
-    own_tokens = tokens.astype(F32)
-    own_rows = streams * local_len
-    hidden, ffn_in, cot_all = move.hidden(mixed.astype(BF), tokens, ffn_vec, cotangent)
-    ffn_down, ffn_gate, ffn_up = move.ffn_weights()
-
-    ffn_scale = inverse_rms(hidden)
-    grad_product = product(cot_all, ffn_down, NN)
-    gate_pre = product(ffn_in, ffn_gate, NN)
-    up_pre = product(ffn_in, ffn_up, NN)
-    gate_sig = jax.nn.sigmoid(gate_pre)
-    product_in = (gate_pre * gate_sig * up_pre).astype(BF)
-    slope = gate_sig * (1.0 + gate_pre * (1.0 - gate_sig))
-    grad_gate_pre = (grad_product * up_pre * slope).astype(BF)
-    grad_up_pre = (grad_product * gate_pre * gate_sig).astype(BF)
-    half_rows = grad_gate_pre.shape[0] // 2
-
-    def grad_ffn_half(which):
-        here = slice(which * half_rows, (which + 1) * half_rows)
-        part = product(grad_gate_pre[here], ffn_gate, NT)
-        return part + product(grad_up_pre[here], ffn_up, NT)
-
-    grad_ffn_in = move.ffn_unorder(move.ffn_sum(grad_ffn_half))
-    gate_fold = move.ffn_grad(product(ffn_in, grad_gate_pre, TN))
-    up_fold = move.ffn_grad(product(ffn_in, grad_up_pre, TN))
-    down_fold = move.ffn_grad(product(cot_all, product_in, TN))
-    moved = gate_fold.near()
-    grad_ffn_in = move.tie(grad_ffn_in, *moved)
-    moved = gate_fold.far(grad_ffn_in) + up_fold.near(grad_ffn_in)
-
-    def ffn_out_half(which):
-        here = slice(which * half_rows, (which + 1) * half_rows)
-        return product(product_late[here], ffn_down, NT)
-
-    product_late = move.tie(product_in, grad_ffn_in)
-    ffn_out = move.ffn_unorder(move.ffn_sum(ffn_out_half))
-    result = (hidden + ffn_out).astype(BF).reshape(tokens.shape)
-    grad_ffn_gain = jnp.sum(grad_ffn_in * hidden * ffn_scale, axis=0)
-    grad_hidden = cotangent.reshape(own_rows, width).astype(F32)
-    grad_hidden = grad_hidden + norm_back(hidden, ffn_scale, ffn_vec, grad_ffn_in)
-
-    grad_mixed = move.piece(grad_hidden.astype(BF).reshape(tokens.shape)).reshape(flat, width)
-    grad_branch_out = product(grad_mixed, output_w, NT).astype(BF)
-    grad_branch = move.from_output(grad_branch_out).astype(F32).reshape(held, piece_len, hd)
-    grad_w_output = move.output_grad(product(branch_out, grad_mixed, TN))
-    grad_gate_rounded = (grad_branch * read_normed * silu_slope(gate_out)).astype(BF)
-    grad_read_normed = grad_branch * gate_act
-    grad_out_gain = jnp.sum(grad_read_normed * reading * read_scale, axis=(0, 1))
-    grad_reading = norm_back(reading, read_scale, out_vec, grad_read_normed)
-    grad_reading = move.tie(grad_reading, *moved)
-    moved = up_fold.far(grad_reading) + down_fold.near(grad_reading)
-    grad_query, grad_k, grad_v, direct, back, own = per_stream(
-        piece_back,
-        [query, key_rows, value_rows, keep, written, slots_in, scores, share, grad_reading],
-        [
-            ((piece_len, hd), BF),
-            ((piece_len, hd), F32),
-            ((piece_len, hd), F32),
-            ((slots, 2 * hd), F32),
-            ((slots, piece_len), F32),
-            ((slots, piece_len), F32),
-        ],
-        gflop,
-    )
-    unused, after = move.scan((survive, direct), True)
-    after = move.tie(after, *moved)
-    down_fold.far(after)
+    grad_out_gain = grad_out_gain[0]
     grad_key, grad_value, grad_log = per_stream(
         piece_after,
         [
@@ -1566,53 +2478,54 @@
         [((piece_len, hd), BF), ((piece_len, hd), BF), ((slots, piece_len), F32)],
         gflop,
     )
-    grad_f = grad_log * jax.nn.sigmoid(-logits) / GATE_SCALE
+    grad_f = grad_log * jax.nn.sigmoid(-mixer.logits) / GATE_SCALE
     grad_bias = jnp.sum(grad_f, axis=(0, 2))
-    low_pieces = low_rank.reshape(held, piece_len, rank)
     highest = lax.Precision.HIGHEST
-    grad_rank = jnp.einsum("smt,str->mr", grad_f, low_pieces, precision=highest)
-    grad_low_rank = jnp.einsum("smt,mr->str", grad_f, head_rank, precision=highest)
+    grad_rank = jnp.einsum("smt,str->mr", grad_f, low_rank, precision=highest)
+    grad_low_rank = jnp.einsum("smt,mr->str", grad_f, mixer.rank, precision=highest)
     grad_low_rank = grad_low_rank.reshape(flat, rank)
-    grads = [g.reshape(flat, hd) for g in (grad_query, grad_key, grad_value, grad_gate_rounded)]
+    grads = [g.reshape(flat, hd) for g in (grad_query, grad_key, grad_value, grad_gate)]
     grad_normed = sum(
         product(g, w, NT) for g, w in zip(grads, (query_w, key_w, value_w, gate_w))
     )
-    grad_normed = grad_normed + product(grad_low_rank, order_low.astype(F32), NT)
-    grad_normed = move.sum_piece(grad_normed.reshape(held, piece_len, width))
+    grad_normed = grad_normed + product(grad_low_rank, mixer.low.astype(F32), NT)
+    attn_part = jnp.sum(grad_normed * inputs * attn_scale, axis=0)
+    grad_low = product(grad_low_rank, normed.astype(F32), TN)
+    grad_low = jnp.swapaxes(move.mixer_unorder(grad_low), 0, 1)
+
+    def placed(part):
+        entire = jnp.zeros((part.shape[0] * H,) + part.shape[1:], F32)
+        return lax.dynamic_update_slice_in_dim(entire, part, move.head * part.shape[0], 0)
+
+    sums = (
+        grad_low,
+        placed(grad_rank),
+        placed(grad_bias),
+        move.mixer_unorder(attn_part),
+        grad_out_gain,
+        grad_ffn_gain,
+    )
+    packed = jnp.concatenate([a.reshape(devices, -1) for a in sums], axis=1)
+    heads, ffn_grads, grad_normed, own_sums, result = move.end(
+        mixer,
+        [grad_key, grad_value],
+        grad_normed.astype(BF).reshape(held, piece_len, width),
+        packed,
+    )
+    grad_w_key, grad_w_value, grad_w_query, grad_w_gate_out, grad_w_output = heads
     grad_normed = move.mixer_unorder(grad_normed)
     own_scale = inverse_rms(own_tokens)
     grad_tokens = grad_hidden.reshape(tokens.shape)
     grad_tokens = grad_tokens + norm_back(own_tokens, own_scale, attn_vec, grad_normed)
-    grad_attn_gain = jnp.sum(grad_normed * own_tokens * own_scale, axis=(0, 1))
-    grad_w_query, grad_w_key, grad_w_value, grad_w_gate_out = (
-        move.head_grad(product(normed, g, TN)) for g in grads
-    )
-    grad_low = product(grad_low_rank, normed.astype(F32), TN)
-    grad_low = jnp.swapaxes(move.mixer_unorder(grad_low), 0, 1)
-
-    def placed(part):
-        entire = jnp.zeros((part.shape[0] * H,) + part.shape[1:], F32)
-        return lax.dynamic_update_slice_in_dim(entire, part, move.head * part.shape[0], 0)
-
-    sums = (
-        grad_low,
-        placed(grad_rank),
-        placed(grad_bias),
-        grad_attn_gain,
-        grad_out_gain,
-        grad_ffn_gain,
-    )
-    packed = jnp.concatenate([a.reshape(devices, -1) for a in sums], axis=1)
-    own_sums = move.small_sum(packed)
     small_grads, taken = [], 0
     for a in small:
         small_grads.append(own_sums[taken : taken + a.size].reshape(a.shape))
         taken += a.size
     return (
-        (result, grad_tokens)
+        (result.reshape(tokens.shape), grad_tokens)
         + (grad_w_query, grad_w_key, grad_w_value, grad_w_gate_out, grad_w_output)
         + tuple(small_grads)
-        + (gate_fold.whole(), up_fold.whole(), down_fold.whole())
+        + tuple(ffn_grads)
     )
 
 

time: 1070 us -> 743 us (0.69)
  Pallas kernels: 363 us -> 636 us
  waiting for transfers between devices: 177 us -> 0.01 us
  local copies, waits for them, and re-layouts: 177 us -> 45 us
  matrix products: 147 us -> 24.9 us
  other arithmetic: 125 us -> 20.2 us
  starting transfers between devices: 66.6 us -> 5.33 us
    pallas_call x4, Pallas kernels: 334 us -> 631 us  [comm_call(): pl.pallas_call(body, in_specs=[space(v) for v in in_vmem], out_specs=[spa...]
    ppermute x66 -> x0, waiting for transfers between devices: 177 us -> none  [swap(): return lax.ppermute(values, ('seq', 'tp'), pairs)]
    dot_general x30 -> x6, matrix products: 143 us -> 22.6 us  [product(): lax.dot_general(left, right, (dims, ((), ())), preferred_element_type=F32)]
    ppermute x66 -> x0, starting transfers between devices: 59.4 us -> none  [swap(): return lax.ppermute(values, ('seq', 'tp'), pairs)]
    unnamed x315 -> x114, local copies, waits for them, and re-layouts: 57.3 us -> 13.6 us
    another operation x14 -> x0, other arithmetic: 35.2 us -> none
    add x22 -> x1, other arithmetic: 25.1 us -> 0.01 us  [alive_rows(): positions = seq * length + jnp.arange(length)]
    pallas_call x4 -> x1, Pallas kernels: 28.6 us -> 5.16 us  [per_stream(): pl.pallas_call(body, grid=(streams,), in_specs=[whole(a.shape) for a in a...]
  transfers between devices with their start and end apart: 68 -> 2, of which waited for: 33 -> 0; matrix products, arithmetic and copies ran while one was open for 32% -> 2% of each run, Pallas kernels for 11% -> 0%
where the time goes in v2:
time: 743 us; the launch traced here: 734 us
  Pallas kernels  636 us (86%)
  local copies, waits for them, and re-layouts  45 us (6%)
  matrix products  24.9 us (3%)
  other arithmetic  20.2 us (3%)
    pallas_call x4, Pallas kernels, comm_call(): pl.pallas_call(body, in_specs=[space(v) for v in in_vmem], out_specs=[spa...  631 us
    dot_general x6, matrix products, product(): lax.dot_general(left, right, (dims, ((), ())), preferred_element_type=F32)  22.6 us
  transfers between devices with their start and end apart: 2, of which 0 were waited for; matrix products, arithmetic and copies ran while one was open for 2% of the time, Pallas kernels for 0%

profile of v2, /device:TPU:0, one launch (start us, length us, event | category | flops | bytes accessed | tf_op | source)
XLA Modules:
  0.0 733.6 jit_solution(9152665265041331127)
XLA Ops:
  0.7 3.7 collective-permute-start
  4.4 2.6 reshape.231
  10.1 1.5 reshape.232.refs_2_
  13.3 286.7 %shard_map.288 = (bf16[2048,128]{1,0:T(8,128)(2,1)}, bf16[32,16,128]{2,1,0:T(8,128)(2,1)}, f32[2,384,128]{2,1,0:T(8,128)}, f32[2,64,384]{2,1,0:T(8,128)}, f32[2,...) custom-call(bf16[64,128]{1,0:T(8,128)(2,1)} %pad.20.refs_0_, ...), custom_call_target="tpu_custom_call" | custom-call | bytes 65536 | tf_op jit(solution)/shard_map/pallas_call | solution.py:613
  304.1 96.2 %shard_map.289 = (f32[2,96,2048]{2,1,0:T(8,128)}, f32[1,2048]{1,0:T(1,128)}, bf16[2,2,384,704]{3,2,1,0:T(8,128)(2,1)}, bf16[2,4,96,2048]{3,2,1,0:T(8,128)(2,1)},...) custom-call(f32[2,96,2048]{2,1,0:T(8,128)} %get-tuple-element.75.refs_0_.refs_2_, ...), custom_call_target="tpu_custom_call" | custom-call | bytes 65536 | tf_op jit(solution)/shard_map/pallas_call | solution.py:613
  401.1 132.2 %shard_map.290 = (f32[2,64,1024]{2,1,0:T(8,128)}, f32[1,512]{1,0:T(1,128)}, bf16[2,384,512]{2,1,0:T(8,128)(2,1)}, bf16[2,384,512]{2,1,0:T(8,128)(2,1)}, f32[2,38...) custom-call(bf16[768,2048]{1,0:T(8,128)(2,1)} %bitcast.85, ...), custom_call_target="tpu_custom_call" | custom-call | bytes 65536 | tf_op jit(solution)/shard_map/pallas_call | solution.py:613
  533.3 1.4 copy-done.1
  534.7 1.4 copy-done.5
  536.1 1.4 copy-done.6
  542.4 5.2 shard_map.291
  549.5 2.6 fusion.28
  552.1 1.8 fusion.25
  554.0 1.8 fusion.24
  555.9 4.5 fusion.26
  560.3 4.4 fusion.27
  564.8 7.5 %fusion.1 = (f32[2048]{0:T(1024)S(1)}, bf16[768,2048]{1,0:T(8,128)(2,1)}) fusion(f32[768]{0:T(1024)S(1)} %rsqrt.23, bf16[2,4,96,2048]{3,2,1,0:T(8,128)(2,1)S(1)} %copy-done.15, bf16[768,16]{0,1:T(8,128)(2,1)S(1)} %fusion.13, bf16[2048,128]{1,0:T(8,128)(2,1)} %get-tuple-element.76, f32[768,2048]{1,0:T(8,128)} %fusion.27, f32[768,2048]{1,0:T(8,128)} %fusion.26, ...), kind=kOutput, calls=%fused_computation.2 | convolution fusion | flops 64485376 | bytes 32017408 | tf_op jit(solution)/shard_map/dot_general | solution.py:419
  572.4 1.4 fusion.7
  578.6 116.1 %shard_map.292 = (f32[2,96,2048]{2,1,0:T(8,128)}, f32[1,16,128]{2,1,0:T(8,128)}, bf16[2,96,2048]{2,1,0:T(8,128)(2,1)}, bf16[64,2048]{1,0:T(8,128)(2,1)}, bf16[64...) custom-call(bf16[2,2,2,96,2048]{4,3,2,1,0:T(8,128)(2,1)} %bitcast.84, f32[32,16,128]{2,1,0:T(8,128)} %bitcast.89, ...), custom_call_target="tpu_custom_call" | custom-call | bytes 65536 | tf_op jit(solution)/shard_map/pallas_call | solution.py:613
  694.7 1.3 slice.77
  697.2 1.3 fusion.23
  701.0 2.1 slice_bitcast_fusion.1
  705.9 1.4 constant_dynamic-slice_fusion.3
  707.3 1.4 maximum_bitcast_fusion
  708.7 2.0 copy.109
  710.7 2.6 reshape.248
  717.3 1.4 copy.110
  718.7 1.3 reshape.250
  720.0 1.6 collective-permute-start.1
  721.6 1.8 convert_element_type.81
  723.4 1.9 convert_element_type.84
  726.6 1.3 maximum_convert_fusion.1
  728.5 1.6 fusion.5
  (180 shorter events, 36.5 us)
Async XLA Ops:
  0.6 6.3 copy-start.45
  0.7 6.4 copy-start.49
  0.7 12.6 %collective-permute-start = (bf16[64,2048]{1,0:T(8,128)(2,1)}, bf16[64,2048]{1,0:T(8,128)(2,1)}, u32[]{:S(2)}, u32[]{:S(2)}) collective-permute-start(bf16[64,2048]{1,0:T(8,128)(2,1)} %param.23), channel_id=1, source_target_pairs={{0,0},{1,4},{2,1},{3,5},{4,2},{5,6},{6,3},{7,7},{8,8},{9,12},{10,9... | collective-permute-start | bytes 786440 | tf_op jit(solution)/shard_map/ppermute | solution.py:1214
  300.0 2.5 copy-start.37
  401.0 132.2 %copy-start = (f32[2,384,512]{2,1,0:T(8,128)S(1)}, f32[2,384,512]{2,1,0:T(8,128)}, u32[]{:S(2)}) copy-start(f32[2,384,512]{2,1,0:T(8,128)} %get-tuple-element.88.refs_7_.refs_0_) | copy-start | bytes 4718596
  401.0 132.2 %copy-start.7 = (f32[2,64,384]{2,1,0:T(8,128)S(1)}, f32[2,64,384]{2,1,0:T(8,128)}, u32[]{:S(2)}) copy-start(f32[2,64,384]{2,1,0:T(8,128)} %get-tuple-element.90.refs_9_.refs_2_) | copy-start | bytes 589828
  401.1 132.2 %copy-start.8 = (f32[2,64,384]{2,1,0:T(8,128)S(1)}, f32[2,64,384]{2,1,0:T(8,128)}, u32[]{:S(2)}) copy-start(f32[2,64,384]{2,1,0:T(8,128)} %get-tuple-element.91.refs_10_.refs_4_) | copy-start | bytes 589828
  542.4 5.2 copy-start.36
  542.4 5.4 copy-start.14
  547.5 4.5 copy-start.2
  549.5 2.6 copy-start.21
  552.1 1.9 copy-start.20
  552.1 1.9 copy-start.30
  555.8 4.5 copy-start.18
  555.8 4.5 copy-start.29
  560.3 4.4 copy-start.15
  574.1 2.1 copy-start.44
  574.1 2.8 copy-start.39
  694.7 8.5 %copy-start.32 = (bf16[2,256,704]{2,1,0:T(8,128)(2,1)S(1)}, bf16[2,256,704]{2,1,0:T(8,128)(2,1)}, u32[]{:S(2)}) copy-start(bf16[2,256,704]{2,1,0:T(8,128)(2,1)} %get-tuple-element.132) | copy-start | bytes 2162692
  701.0 3.0 copy-start.31
  710.7 2.6 copy-start.16
  713.3 2.4 copy-start.34
  713.4 3.2 copy-start.38
  714.9 10.3 %copy-start.25 = (bf16[256,704]{1,0:T(8,128)(2,1)S(1)}, bf16[256,704]{1,0:T(8,128)(2,1)}, u32[]{:S(2)}) copy-start(bf16[256,704]{1,0:T(8,128)(2,1)} %get-tuple-element.208) | copy-start | bytes 1081348
  714.9 10.3 %copy-start.26 = (bf16[256,704]{1,0:T(8,128)(2,1)S(1)}, bf16[256,704]{1,0:T(8,128)(2,1)}, u32[]{:S(2)}) copy-start(bf16[256,704]{1,0:T(8,128)(2,1)} %get-tuple-element.209) | copy-start | bytes 1081348
  720.0 11.4 %collective-permute-start.1 = (bf16[64,2048]{1,0:T(8,128)(2,1)}, bf16[64,2048]{1,0:T(8,128)(2,1)S(1)}, u32[]{:S(2)}, u32[]{:S(2)}) collective-permute-start(bf16[64,2048]{1,0:T(8,128)(2,1)} %get-tuple-element.129), channel_id=1, source_target_pairs={{0,0},{4,1},{1,2},{5,3},{2,4},{6,5},{3,6},{7,7},{8,8},{12,9},{9,10... | collective-permute-start | bytes 786440 | tf_op jit(solution)/shard_map/ppermute | solution.py:1214
  723.4 3.2 copy-start.27
  723.4 3.2 copy-start.28
  726.6 1.9 copy-start.23
  726.6 1.9 copy-start.41
  726.6 1.9 copy-start.42
  730.1 2.1 copy-start.33
  (20 other events, 25.8 us)

commit v3 on v2

--- a/solution.py
+++ b/solution.py
@@ -7,6 +7,20 @@
 from jax.experimental import pallas as pl
 from jax.experimental.pallas import tpu as pltpu
 from jax.sharding import PartitionSpec as P
+
+SEQ, TP = "seq", "tp"
+
+
+class Key:
+    x, y, side, middle, core, remote = range(100, 106)
+    local, far, near, done, rows, lines = range(106, 112)
+    raw, branch, traded, mixed, trade, pack = range(112, 118)
+    state, slots, gate, up, cot, down = range(118, 124)
+    block, reading, query, key, value, keep = range(124, 130)
+    written, scores, share, normed, query_w, gate_w = range(130, 136)
+    sent, got, direct, grad_k, grad_v, part = range(136, 142)
+    key_w, value_w, hidden_grad, down_2, normed_part, sheet = range(142, 148)
+
 
 H = 4
 GATE_SCALE = 8.0
@@ -337,7 +351,7 @@
 
 
 def piece_after(
-    key_raw, value_raw, keep, true_keep, written, grad_k, grad_v, back, own, after, slots_end
+    key_raw, value_raw, keep, written, grad_k, grad_v, back, own, after, slots_end
 ):
     width = key_raw.shape[1]
     keys, values = silu(key_raw), silu(value_raw)
@@ -361,7 +375,7 @@
             step *= 2
         outs.append(total + held)
         held = held + total[:, :1]
-    grad_log = jnp.concatenate(outs[::-1], axis=1) - true_keep * back
+    grad_log = jnp.concatenate(outs[::-1], axis=1) - (1.0 - written) * back
     return grad_k * silu_slope(key_raw), grad_v * silu_slope(value_raw), grad_log
 
 
@@ -428,7 +442,7 @@
 
 class Place:
     def __init__(self):
-        self.seq, self.tp = lax.axis_index("seq"), lax.axis_index("tp")
+        self.seq, self.tp = lax.axis_index(SEQ), lax.axis_index(TP)
         self.core, self.x = self.tp % 2, self.tp // 2
         self.y, self.z = self.seq % 2, self.seq // 2
         self.near, self.far = self.z % 2, self.z // 2
@@ -456,13 +470,13 @@
 
 
 class Wire:
-    LATENCY, LINK, BESIDE, AHEAD = 2.5, 2 / 91e3, 1 / 400e3, 5.0
-
-    def __init__(self, place, sends, receives, locals_):
+    def __init__(self, place, sends, receives, locals_, pace):
+        latency, link, beside, self.AHEAD = pace
+        self.LATENCY, self.LINK, self.BESIDE = latency, 2e-3 / link, 1e-3 / beside
         self.place, self.sends, self.receives, self.locals = place, sends, receives, locals_
         self.remote, self.near_by, self.seen = [], [], set()
         self.now, self.due, self.free, self.rank = 0.0, {}, {}, 0
-        self.queues = {"x": [], "y": [], "side": [], "middle": []}
+        self.queues = {Key.x: [], Key.y: [], Key.side: [], Key.middle: []}
 
     def greet(self, masks):
         barrier = pltpu.get_barrier_semaphore()
@@ -492,20 +506,20 @@
         self.remote[at] = copy
         size = math.prod(source.shape) * jnp.dtype(source.dtype).itemsize
         if mask == CORE:
-            uses = (("core", size * self.BESIDE),)
+            uses = ((Key.core, size * self.BESIDE),)
         elif mask & X:
-            uses = (("x", size * self.LINK),)
+            uses = ((Key.x, size * self.LINK),)
         elif mask == Y:
-            uses = (("y", size * self.LINK),)
+            uses = ((Key.y, size * self.LINK),)
         elif mask == NEAR:
-            uses = (("side", size * self.LINK),)
+            uses = ((Key.side, size * self.LINK),)
         else:
-            uses = (("side", size * self.LINK), ("middle", 2 * size * self.LINK))
+            uses = ((Key.side, size * self.LINK), (Key.middle, 2 * size * self.LINK))
         end = 0.0
         for link, time in uses:
             self.free[link] = max(self.now, self.free.get(link, 0.0)) + time
             end = max(end, self.free[link])
-        self.due["remote", at] = end + self.LATENCY
+        self.due[Key.remote, at] = end + self.LATENCY
 
     def send(self, source, target, mask):
         at = len(self.remote)
@@ -513,9 +527,9 @@
         if mask == CORE:
             self.issue(at)
         else:
-            link = {Y: "y", NEAR: "side", FAR: "middle"}.get(mask, "x")
+            link = {Y: Key.y, NEAR: Key.side, FAR: Key.middle}.get(mask, Key.x)
             self.queues[link].append((self.rank, at))
-        return ("remote", at)
+        return (Key.remote, at)
 
     def feed(self, until):
         fed = False
@@ -532,8 +546,8 @@
         copy = pltpu.make_async_copy(source, target, self.locals.at[at])
         copy.start()
         self.near_by.append(copy)
-        self.due["local", at] = self.now + 2.0
-        return ("local", at)
+        self.due[Key.local, at] = self.now + 2.0
+        return (Key.local, at)
 
     def arrived(self, *handles):
         for handle in handles:
@@ -541,7 +555,7 @@
                 continue
             self.seen.add(handle)
             self.now = max(self.now, self.due[handle])
-            if handle[0] == "remote":
+            if handle[0] == Key.remote:
                 self.remote[handle[1]].wait_recv()
             else:
                 self.near_by[handle[1]].wait()
@@ -576,10 +590,10 @@
 
     def finish(self):
         for at, copy in enumerate(self.remote):
-            self.arrived(("remote", at))
+            self.arrived((Key.remote, at))
             copy.wait_send()
         for at in range(len(self.near_by)):
-            self.arrived(("local", at))
+            self.arrived((Key.local, at))
 
 
 class Flags:
@@ -598,14 +612,18 @@
         return ask
 
 
-def comm_call(work, number, masks, arrays, in_vmem, outs, out_vmem, scratch, copies, stay, mb=48):
+FAST, STEADY = (2.5, 91, 400, 5.0), (3.5, 86, 300, 6.0)
+KEEN, EARLY = (2.5, 91, 400, 2.0), (2.5, 91, 400, 15.0)
+
+
+def comm_call(work, number, masks, arrays, in_vmem, outs, out_vmem, scratch, copies, stay, mb=48, pace=FAST):
     def space(fast):
         return pl.BlockSpec(memory_space=pltpu.VMEM if fast else pl.ANY)
 
     def body(*refs):
         n, m = len(arrays), len(outs)
         place = Place()
-        wire = Wire(place, *refs[-3:])
+        wire = Wire(place, *refs[-3:], pace)
         wire.greet(masks)
         work(place, wire, refs[:n], refs[n : n + m], refs[n + m : -3])
         wire.finish()
@@ -622,7 +640,7 @@
             pltpu.SemaphoreType.DMA((max(stay, 1),)),
         ],
         compiler_params=pltpu.CompilerParams(
-            collective_id=number, has_side_effects=True, vmem_limit_bytes=mb * 1024 * 1024
+            collective_id=number, has_side_effects=True, vmem_limit_bytes=int(mb * 1024 * 1024)
         ),
         cost_estimate=pl.CostEstimate(flops=0, bytes_accessed=1 << 16, transcendentals=0),
     )(*arrays)
@@ -693,16 +711,27 @@
     ]
 
 
-def ffn_gather(place, wire, weight, halves, out):
+def ffn_traded(place, wire, weight, halves, out, flags, key):
     yield from ffn_trade(place, wire, weight, halves, out)
-    yield from ffn_spread(place, wire, None, out)
-
-
-def ffn_spread(place, wire, block, out):
-    start = out.at[0] if block is None else block
-    waits = [] if block is None else [wire.keep(block, out.at[0])]
-    far = [wire.send(start.at[y], out.at[2, y], FAR) for y in range(2)]
-    waits += [wire.send(start.at[y], out.at[1, y], NEAR) for y in range(2)]
+    flags.raised(key)
+
+
+def far_spread(wire, out, flags, first):
+    yield flags.wait(first)
+    far = [wire.send(out.at[0, y], out.at[2, y], FAR) for y in range(2)]
+    yield far + [wire.send(out.at[0, y], out.at[1, y], NEAR) for y in range(2)]
+
+
+def last_spread(place, wire, blocks, out):
+    waits = [wire.keep(blocks.at[z], out.at[z]) for z in range(3)]
+    yield waits + [wire.send(blocks.at[2, y], out.at[3, y], NEAR) for y in range(2)]
+
+
+def ffn_spread(place, wire, out, flags, first, then):
+    yield flags.wait(first)
+    waits = [wire.send(out.at[0, y], out.at[1, y], NEAR) for y in range(2)]
+    yield flags.wait(then)
+    far = [wire.send(out.at[0, y], out.at[2, y], FAR) for y in range(2)]
     for y in range(2):
         yield [far[y]]
         waits.append(wire.send(out.at[2, y], out.at[3, y], NEAR))
@@ -772,6 +801,12 @@
     yield stay + beside[0] + beside[1]
 
 
+def by_tp(values, count, side):
+    first, second = count
+    order = [(a * second + b) * side for b in range(second) for a in range(first)]
+    return jnp.concatenate([values[:, at : at + side] for at in order], axis=1)
+
+
 def heads_trade(place, wire, branch, out):
     width = out.shape[1] // 4
 
@@ -890,26 +925,26 @@
     if flags is None:
         flags = Flags()
         for h in range(2):
-            flags.raised(("far", h))
-            flags.raised(("near", h))
+            flags.raised((Key.far, h))
+            flags.raised((Key.near, h))
     beside = {}
     for h in range(2):
-        yield flags.wait(("far", h))
+        yield flags.wait((Key.far, h))
         for m in (2, 3, 1, 0):
             beside[h, m] = wire.send(far_part.at[h, m], got_core.at[h, m], CORE)
     two, one = {}, {}
     for h in range(2):
-        yield flags.wait(("near", h), more=[beside[h, 2], beside[h, 3]])
-
-        def to_two(rows, h=h):
-            for m in (2, 3):
+        for m in (3, 2):
+            yield flags.wait((Key.near, h), more=[beside[h, m]])
+
+            def to_two(rows, h=h, m=m):
                 term = near_part[h, m, rows].astype(F32) + got_core[h, m, rows].astype(F32)
                 send_two[h, m - 2, rows] = term.astype(BF)
 
-        row_loop(count, 16, to_two)
-        two[h] = wire.send(send_two.at[h], got_two.at[h], (Y, X)[h])
+            row_loop(count, 16, to_two)
+            two[h, m] = wire.send(send_two.at[h, m - 2], got_two.at[h, m - 2], (Y, X)[h])
     for h in range(2):
-        yield [beside[h, 1], two[h]]
+        yield [beside[h, 1], two[h, 3]]
 
         def to_one(rows, h=h):
             term = near_part[h, 1, rows].astype(F32) + got_core[h, 1, rows].astype(F32)
@@ -918,7 +953,7 @@
         row_loop(count, 16, to_one)
         one[h] = wire.send(send_one.at[h], got_one.at[h], (X, Y)[h])
     for h in range(2):
-        yield [beside[h, 0], one[h]]
+        yield [beside[h, 0], two[h, 2], one[h]]
 
         def to_finish(rows, h=h):
             def load(columns):
@@ -930,6 +965,7 @@
             finish(h, rows, load)
 
         row_loop(count, 16, to_finish)
+        flags.raised((Key.done, h))
 
 
 def plane_buffers(part_shape):
@@ -962,7 +998,8 @@
     row_loop(target.shape[0], step, work)
 
 
-def ffn_fold(place, wire, part, bufs, out, flags=None):
+def ffn_fold(place, wire, part, bufs, out, flags=None, added=None):
+    added = (part.at[0], part.at[2]) if added is None else (added.at[0], added.at[1])
     got_near, got_far, held = bufs
     first, second, far = [], [], []
     for z, handles in ((3, first), (1, second)):
@@ -972,11 +1009,11 @@
             handles.append(wire.send(part.at[z, y], got_near.at[z // 2, y], NEAR))
     for y in range(2):
         yield [first[y]] if flags is None else flags.wait((2, y), more=[first[y]])
-        add_into(held.at[0, y], [part.at[2, y], got_near.at[1, y]])
+        add_into(held.at[0, y], [added[1].at[y], got_near.at[1, y]])
         far.append(wire.send(held.at[0, y], got_far.at[y], FAR))
     for y in range(2):
         yield [second[y], far[y]] if flags is None else flags.wait((0, y), more=[second[y], far[y]])
-        add_into(held.at[1, y], [part.at[0, y], got_near.at[0, y], got_far.at[y]])
+        add_into(held.at[1, y], [added[0].at[y], got_near.at[0, y], got_far.at[y]])
     mine = out.at[place.y]
     yield [
         wire.send(held.at[1, 1 - place.y], mine, Y),
@@ -1088,7 +1125,7 @@
     CORE, X, Y, NEAR, FAR = 1, 2, 4, 8, 16
 
     def __init__(self):
-        seq, tp = lax.axis_index("seq"), lax.axis_index("tp")
+        seq, tp = lax.axis_index(SEQ), lax.axis_index(TP)
         self.core, self.x = tp & 1, tp >> 1
         self.y, self.z = seq & 1, seq >> 1
 
@@ -1104,7 +1141,7 @@
 
 def swap(values, mask):
     pairs = [(i, i ^ mask) for i in range(32)]
-    return lax.ppermute(values, ("seq", "tp"), pairs)
+    return lax.ppermute(values, (SEQ, TP), pairs)
 
 
 def half(values, axis, which):
@@ -1211,7 +1248,7 @@
         z, y, x, core = i >> 3, (i >> 2) & 1, (i >> 1) & 1, i & 1
         there = z * 8 + core * 4 + y * 2 + x
         pairs.append((there, i) if back else (i, there))
-    return lax.ppermute(values, ("seq", "tp"), pairs)
+    return lax.ppermute(values, (SEQ, TP), pairs)
 
 
 def gather_output(weight, at):
@@ -1355,24 +1392,23 @@
     scores: jax.Array
     share: jax.Array
     branch: jax.Array
-    rows: jax.Array
     normed: jax.Array
-    low: jax.Array
-    low_rank: jax.Array
-    rank: jax.Array
     logits: jax.Array
     keep: jax.Array
-    true_keep: jax.Array
     written: jax.Array
-    survive: jax.Array
     slots_in: jax.Array
     slots_end: jax.Array
     weights: list
     raw: list
     output: jax.Array
-    out_gain: jax.Array
-    ffn_gain: jax.Array
-    attn_gain: jax.Array
+    rows: jax.Array = None
+    low: jax.Array = None
+    low_rank: jax.Array = None
+    rank: jax.Array = None
+    survive: jax.Array = None
+    out_gain: jax.Array = None
+    ffn_gain: jax.Array = None
+    attn_gain: jax.Array = None
 
 
 def alive_rows(seq_cuts, seq, length):
@@ -1383,16 +1419,16 @@
 
 class Plain:
     def __init__(self):
-        self.seq, self.tp = lax.axis_index("seq"), lax.axis_index("tp")
-        self.seq_count, self.tp_count = lax.axis_size("seq"), lax.axis_size("tp")
+        self.seq, self.tp = lax.axis_index(SEQ), lax.axis_index(TP)
+        self.seq_count, self.tp_count = lax.axis_size(SEQ), lax.axis_size(TP)
         self.sharing = self.tp_count // H
         self.head, self.member = self.tp // self.sharing, self.tp % self.sharing
 
 
 def plain_scan(part, at, reverse):
     gathered = (
-        lax.all_gather(part[0], "seq"),
-        lax.all_gather(part[1].astype(BF), "seq"),
+        lax.all_gather(part[0], SEQ),
+        lax.all_gather(part[1].astype(BF), SEQ),
     )
     state = (jnp.ones_like(part[0]), jnp.zeros_like(part[1]))
 
@@ -1407,10 +1443,10 @@
 
 class PlainMoves:
     def small(self, packed):
-        return lax.all_gather(packed, ("seq", "tp"))
+        return lax.all_gather(packed, (SEQ, TP))
 
     def small_sum(self, packed):
-        return lax.psum_scatter(packed, ("seq", "tp"), scatter_dimension=0, tiled=True)[0]
+        return lax.psum_scatter(packed, (SEQ, TP), scatter_dimension=0, tiled=True)[0]
 
     def start(self, tokens, seq_cuts, weights, w_output, small, ffn, cotangent):
         self.ffn = ffn
@@ -1468,7 +1504,6 @@
             rank=rank,
             logits=logits,
             keep=keep,
-            true_keep=true_keep,
             written=written,
             survive=survive[..., 0],
             slots_in=slots_in,
@@ -1488,7 +1523,7 @@
         scale = inverse_rms(hidden)
         ffn_in = self.ffn_rows((hidden * scale * gain).astype(BF))
         cot = self.ffn_rows(cotangent.reshape(own_rows, width))
-        down, gate, up = [lax.all_gather(w, "seq", axis=0, tiled=True) for w in self.ffn]
+        down, gate, up = [lax.all_gather(w, SEQ, axis=0, tiled=True) for w in self.ffn]
         grad_product = product(cot, down, NN)
         gate_pre, up_pre = product(ffn_in, gate, NN), product(ffn_in, up, NN)
         sig = jax.nn.sigmoid(gate_pre)
@@ -1507,7 +1542,7 @@
         return grad_hidden, gain_grad, self.piece(grad_hidden.astype(BF).reshape(cotangent.shape))
 
     def ffn_grad(self, grad):
-        own = lax.psum_scatter(grad, "seq", scatter_dimension=0, tiled=True)
+        own = lax.psum_scatter(grad, SEQ, scatter_dimension=0, tiled=True)
         return own.astype(F32)
 
     def mixer_back(self, mixer, grad_mixed):
@@ -1544,19 +1579,51 @@
         ]
         return after, gain_sum, grad_query, grad_gate, grad_k, grad_v, back, own
 
-    def end(self, mixer, grads, normed_part, packed):
-        hd = grads[0].shape[-1]
-        heads = [
-            self.head_grad(product(mixer.normed, g.reshape(-1, hd), TN)) for g in grads
-        ]
+    def finish(self, mixer, back, tokens, grad_hidden, ffn_gain_grad, small):
+        after, out_gain_grad, grad_query, grad_gate, grad_k, grad_v, pulled, flow = back
+        held, length, hd = grad_k.shape
+        width, slots = tokens.shape[-1], flow.shape[1]
+        grad_key, grad_value, grad_log = per_stream(
+            piece_after,
+            [mixer.raw[0], mixer.raw[1], mixer.keep, mixer.written]
+            + [grad_k, grad_v, pulled, flow, after, mixer.slots_end],
+            [((length, hd), BF), ((length, hd), BF), ((slots, length), F32)],
+            1 << 30,
+        )
+        highest = lax.Precision.HIGHEST
+        grad_f = grad_log * jax.nn.sigmoid(-mixer.logits) / GATE_SCALE
+        grad_bias = jnp.sum(grad_f, axis=(0, 2))
+        grad_rank = jnp.einsum("smt,str->mr", grad_f, mixer.low_rank, precision=highest)
+        low_grad = jnp.einsum("smt,mr->str", grad_f, mixer.rank, precision=highest)
+        low_grad = low_grad.reshape(held * length, -1)
+        grads = [g.reshape(-1, hd) for g in (grad_key, grad_value, grad_query, grad_gate)]
+        grad_normed = sum(product(g, w, NT) for g, w in zip(grads, mixer.weights))
+        grad_normed = grad_normed + product(low_grad, mixer.low.astype(F32), NT)
+        inputs = mixer.rows.reshape(-1, width).astype(F32)
+        attn_grad = jnp.sum(grad_normed * inputs * inverse_rms(inputs), axis=0)
+        grad_low = product(mixer.normed.astype(F32), low_grad, TN)
+
+        def placed(part):
+            entire = jnp.zeros((part.shape[0] * H,) + part.shape[1:], F32)
+            return lax.dynamic_update_slice_in_dim(entire, part, self.head * part.shape[0], 0)
+
+        sums = (grad_low, placed(grad_rank), placed(grad_bias), attn_grad)
+        sums = sums + (out_gain_grad[0], ffn_gain_grad)
+        devices = self.at.seq_count * self.at.tp_count
+        packed = jnp.concatenate([a.reshape(devices, -1) for a in sums], axis=1)
+        own = self.small_sum(packed)
+        small_grads, taken = [], 0
+        for a in small:
+            small_grads.append(own[taken : taken + a.size].reshape(a.shape))
+            taken += a.size
+        heads = [self.head_grad(product(mixer.normed, g, TN)) for g in grads[:2]]
         heads = heads + self.head_sums + [self.output_sum]
-        return (
-            heads,
-            [self.gate_grad, self.up_grad, self.down_sum],
-            self.sum_piece(normed_part),
-            self.small_sum(packed),
-            self.result,
-        )
+        x = tokens.astype(F32)
+        total = self.sum_piece(grad_normed.reshape(held, length, width))
+        grad_tokens = norm_back(x, inverse_rms(x), mixer.attn_gain, total)
+        grad_tokens = grad_tokens + grad_hidden.reshape(x.shape)
+        ffn_grads = [self.gate_grad, self.up_grad, self.down_sum]
+        return heads, ffn_grads, grad_tokens, self.result, small_grads
 
     def __init__(self):
         self.at = Plain()
@@ -1567,7 +1634,7 @@
         return lax.dynamic_slice_in_dim(values, self.member * count, count, 0)
 
     def piece(self, own):
-        return self.own_streams(lax.all_gather(own, "tp", axis=1, tiled=True))
+        return self.own_streams(lax.all_gather(own, TP, axis=1, tiled=True))
 
     def sum_piece(self, part):
         streams = part.shape[0] * self.at.sharing
@@ -1575,7 +1642,7 @@
         entire = lax.dynamic_update_slice_in_dim(
             entire, part.astype(BF), self.member * part.shape[0], 0
         )
-        own = lax.psum_scatter(entire, "tp", scatter_dimension=1, tiled=True)
+        own = lax.psum_scatter(entire, TP, scatter_dimension=1, tiled=True)
         return own.astype(F32)
 
     def mixer_order(self, values):
@@ -1584,7 +1651,7 @@
     mixer_unorder = ffn_order = ffn_unorder = mixer_order
 
     def head_weight(self, weight):
-        entire = lax.all_gather(weight, ("seq", "tp"), axis=0, tiled=True)
+        entire = lax.all_gather(weight, (SEQ, TP), axis=0, tiled=True)
         width = entire.shape[1] // H
         return lax.dynamic_slice_in_dim(entire, self.head * width, width, 1)
 
@@ -1593,11 +1660,11 @@
         entire = lax.dynamic_update_slice_in_dim(
             entire, grad.astype(BF), self.head * grad.shape[1], 1
         )
-        own = lax.psum_scatter(entire, ("seq", "tp"), scatter_dimension=0, tiled=True)
+        own = lax.psum_scatter(entire, (SEQ, TP), scatter_dimension=0, tiled=True)
         return own.astype(F32)
 
     def output_weight(self, weight):
-        entire = lax.all_gather(weight, ("seq", "tp"), axis=0, tiled=True)
+        entire = lax.all_gather(weight, (SEQ, TP), axis=0, tiled=True)
         rows = entire.shape[0] // H
         return lax.dynamic_slice_in_dim(entire, self.head * rows, rows, 0)
 
@@ -1606,26 +1673,26 @@
         entire = lax.dynamic_update_slice_in_dim(
             entire, grad.astype(BF), self.head * grad.shape[0], 0
         )
-        own = lax.psum_scatter(entire, ("seq", "tp"), scatter_dimension=0, tiled=True)
+        own = lax.psum_scatter(entire, (SEQ, TP), scatter_dimension=0, tiled=True)
         return own.astype(F32)
 
     def scan(self, part, reverse):
         return plain_scan(part, self.at, reverse)
 
     def ffn_rows(self, own):
-        entire = lax.all_gather(own, "tp", axis=0)
+        entire = lax.all_gather(own, TP, axis=0)
         return entire.reshape((-1,) + own.shape[1:])
 
     def ffn_sum(self, part):
         parts = part.astype(BF).reshape((self.at.tp_count, -1) + part.shape[1:])
-        own = lax.psum_scatter(parts, "tp", scatter_dimension=0, tiled=True)
+        own = lax.psum_scatter(parts, TP, scatter_dimension=0, tiled=True)
         return own.reshape((-1,) + part.shape[1:]).astype(F32)
 
 
 class BitMoves:
     def __init__(self):
         self.at = Bits()
-        self.head, self.member = lax.axis_index("tp"), 0
+        self.head, self.member = lax.axis_index(TP), 0
 
     def start(self, tokens, seq_cuts, weights, w_output, small, ffn, cotangent):
         w_low, w_rank, bias, attn_gain, out_gain, ffn_gain = small
@@ -1647,8 +1714,8 @@
         head = (width, hd)
         cut = (2, ffn[0].shape[0], ffn[0].shape[1] // 2)
         ffn_shape = (4,) + cut
-        block = turn_bits(w_output, False)
-        alive = alive_rows(seq_cuts, lax.axis_index("seq"), length)
+        block = w_output
+        alive = alive_rows(seq_cuts, lax.axis_index(SEQ), length)
         state_shape, slim = (streams, slots, 2 * hd), (streams, slots, 128)
         gate_shape = (streams, slots, length)
 
@@ -1656,37 +1723,52 @@
             pack, lines, tokens, alive, own_tokens = given[:5]
             given = given[1:]
             heads_in, block, ffn_in, cot = given[4:8], given[8], given[9:12], given[12]
-            pack_out, lines_out, low_out, logits, keep, true_keep, written = outs[:7]
-            survive, slots_in, slots_end, scores, share = outs[7:12]
-            rows_out, normed_out, reading_out, branch_out, hidden_out = outs[12:17]
-            heads_out, raws_out, output_out = outs[17:21], outs[21:25], outs[25]
-            ffn_out, cot_out, ffn_rows, grad_product = outs[26:29], outs[29], outs[30], outs[31]
+            pack_out, lines_out, low_out, logits, keep, written = outs[:6]
+            survive, slots_in, slots_end, scores, share = outs[6:11]
+            factor_out, normed_out, reading_out, branch_out, hidden_out = outs[11:16]
+            gain_rows = outs[30]
+            heads_out, raws_out, output_out = outs[16:20], outs[20:24], outs[24]
+            ffn_out, cot_out, ffn_rows = outs[25:28], outs[28], outs[29]
             rows, normed, state = scratch[:3]
             heads, raws, cuts, scan = scratch[3:7], scratch[7:11], scratch[11:14], scratch[14:18]
             output_w, reading, branch, traded, mixed = scratch[18:23]
-            hidden, ready, gain_rows, cot_rows, down = scratch[23:28]
-            fold_bufs = scratch[28:31]
+            hidden, ready = scratch[23:25]
+            fold_bufs, cot_own = scratch[25:28], scratch[28]
             here = Flags()
 
             def fetch_rows():
                 yield from rows_gather(place, wire, tokens, rows)
-                here.raised("rows")
-                wire.keep(rows, rows_out)
+                here.raised(Key.rows)
 
             def fetch_lines():
                 yield from small_gather(place, wire, lines, lines_out)
-                here.raised("lines")
+                here.raised(Key.lines)
+
+            def across(row_at):
+                side = width // 8
+                for y in range(2):
+                    for m in range(4):
+                        to = pl.multiple_of((place.z_turn(m) * 2 + y) * side, 128)
+                        yield pl.ds(to, side), slice((y * 4 + m) * side, (y * 4 + m + 1) * side)
 
             def norm():
-                gain = jnp.transpose(pack_out[...].astype(F32))[rank : rank + 1]
+                tall_rows = jnp.transpose(pack_out[...].astype(F32))
+                gain_rows[2:3] = tall_rows[rank : rank + 1]
+                for there, at in across(0):
+                    gain_rows[3:4, there] = tall_rows[rank : rank + 1, at]
+                    gain_rows[1:2, there] = tall_rows[rank + 1 : rank + 2, at]
                 steps = count // 16
 
                 def body(i, carry):
                     stream, tp, part = i // (4 * steps), i // steps % 4, i % steps
                     at = pl.multiple_of(part * 16, 16)
                     x = rows[stream, tp, pl.ds(at, 16)].astype(F32)
-                    to = pl.multiple_of(i * 16, 16)
-                    normed[pl.ds(to, 16)] = (x * inverse_rms(x) * gain).astype(BF)
+                    to = pl.ds(pl.multiple_of(i * 16, 16), 16)
+                    scale = inverse_rms(x)
+                    for there, here_at in across(0):
+                        part = rows[stream, tp, pl.ds(at, 16), there].astype(F32)
+                        part = part * scale * gain_rows[2:3, here_at]
+                        normed[to, here_at] = part.astype(BF)
                     return carry
 
                 lax.fori_loop(0, streams * 4 * steps, body, 0)
@@ -1695,7 +1777,7 @@
                 for s in range(streams):
                     raws[index][s] = mm(normed[s * length : (s + 1) * length], heads[index][...], NN)
                 wire.spend(3.0)
-                here.raised(("raw", index))
+                here.raised((Key.raw, index))
                 wire.keep(heads[index], heads_out[index])
                 wire.keep(raws[index], raws_out[index])
 
@@ -1707,13 +1789,6 @@
                 here_is = row(wide.shape) == column(wide.shape) // per
                 out_row = jnp.sum(jnp.where(here_is, wide, 0.0), axis=0, keepdims=True)
                 gain_rows[0:1, :hd] = out_row
-                ffn_row = jnp.transpose(pack_out[...].astype(F32))[rank + 1 : rank + 2]
-                side = width // 8
-                for y in range(2):
-                    for m in range(4):
-                        to = pl.multiple_of((place.z_turn(m) * 2 + y) * side, 128)
-                        at = (y * 4 + m) * side
-                        gain_rows[1:2, pl.ds(to, side)] = ffn_row[:, at : at + side]
 
             def read(s, carry):
                 values = piece_read(
@@ -1727,7 +1802,8 @@
                     at = pl.ds(pl.multiple_of(s * length + part.start, 16), part.size)
                     values = reading[s, part]
                     normed_read = values * inverse_rms(values) * gain_rows[0:1, :hd]
-                    branch[at] = (normed_read * silu(raws[3][s, part])).astype(BF)
+                    opened = normed_read * silu(raws[3][s, part])
+                    branch[at] = by_tp(opened, (2, 4), hd // 8).astype(BF)
 
                 row_loop(length, 32, chunk)
 
@@ -1741,50 +1817,45 @@
                     ready[stream, rows, there] = normed[:, m * size : (m + 1) * size]
 
             def to_rows():
-                yield here.wait("branch")
+                yield here.wait(Key.branch)
                 yield from heads_trade(place, wire, branch, traded)
-                here.raised("traded")
+                here.raised(Key.traded)
                 wire.keep(traded, branch_out)
-                yield here.wait("mixed")
+                yield here.wait(Key.mixed)
                 yield from rows_fold(place, wire, mixed, *fold_bufs, finish)
                 wire.keep(hidden, hidden_out)
                 yield from plane_gather(place, wire, ready.at[0], ready.at[1], ffn_rows)
 
-            def fetch_down():
-                yield from ffn_gather(place, wire, ffn_in[0], cuts[0], down)
-                here.raised("down")
-                wire.keep(down, ffn_out[0])
+            def trade(i):
+                return ffn_traded(place, wire, ffn_in[i], cuts[i], ffn_out[i], here, (Key.trade, i))
 
             def fetch_cot():
-                yield from plane_gather(place, wire, cot.at[0], cot.at[1], cot_rows)
-                here.raised("cot")
-                wire.keep(cot_rows, cot_out)
-
-            def product_grads():
-                yield here.wait("down", "cot")
-                for c in range(2):
-                    for h in range(2):
-                        values = cot_rows[c, h].reshape(4 * count, width)
-                        total = mm(values, down[...].reshape(width, ffn_shape[-1]), NN)
-                        grad_product[c, h] = total.astype(BF)
-                        wire.spend(1.5)
-                        yield []
+                side = width // 4
+
+                def turn_row(at, stream):
+                    for m in range(4):
+                        there = pl.ds(pl.multiple_of(place.z_turn(m) * side, 128), side)
+                        cot_own[stream, at, m * side : (m + 1) * side] = cot[stream, at, there]
+
+                for stream in range(streams):
+                    row_loop(count, 16, lambda at, stream=stream: turn_row(at, stream))
+                yield from plane_gather(place, wire, cot_own.at[0], cot_own.at[1], cot_out)
 
             def compute():
-                yield here.wait("rows", "pack")
+                yield here.wait(Key.rows, Key.pack)
                 norm()
                 wire.spend(3.0)
                 wire.keep(normed, normed_out)
-                yield here.wait("lines")
+                yield here.wait(Key.lines)
                 own = lines_out[pl.ds(place.tp * 8, 8)].astype(F32)[:, :tall].reshape(slots, 128)
                 factor = jnp.where(column(own.shape) < rank, own, 0.0)
+                factor_out[...] = factor
                 for s in range(streams):
                     low = mm(normed[s * length : (s + 1) * length], pack_out[...], NN)
                     low_out[s] = low
                     f = mm_fine(factor, low, NT) + own[:, rank : rank + 1]
                     logits[s] = f
                     kept, wrote = gates(f)
-                    true_keep[s] = kept
                     written[s] = wrote
                     keep[s] = kept * alive[s]
                 wire.spend(2.0)
@@ -1796,51 +1867,53 @@
                     state[s] = part
                     survive[s] = jnp.broadcast_to(left, slim[1:])
                 wire.spend(3.0)
-                here.raised("state")
+                here.raised(Key.state)
                 for index in (2, 3):
                     yield here.wait(index)
                     project(index)
                 gains()
-                yield here.wait("slots")
+                yield here.wait(Key.slots)
                 lax.fori_loop(0, streams, read, 0)
                 wire.spend(10.0)
                 for s in range(streams):
                     gated(s)
                 wire.spend(2.0)
-                here.raised("branch")
+                here.raised(Key.branch)
                 wire.keep(reading, reading_out)
-                yield here.wait("traded", 4)
+                yield here.wait(Key.traded, 4)
                 wire.keep(output_w, output_out)
                 for s in range(streams):
                     rows_in = traded[s * length : (s + 1) * length]
                     total = mm(rows_in, output_w[...].reshape(hd, width), NN)
                     mixed[s] = total.astype(BF).reshape(mixed.shape[1:])
                 wire.spend(2.5)
-                here.raised("mixed")
+                here.raised(Key.mixed)
 
             def exchange():
-                yield here.wait("state")
+                yield here.wait(Key.state)
                 yield from pieces_scan(place, wire, False, survive, state, slots_in, scan)
                 for s in range(streams):
                     slots_end[s] = survive[s][:, :1] * slots_in[s] + state[s]
-                here.raised("slots")
+                here.raised(Key.slots)
 
             wire.run(
                 fetch_lines(),
-                head_gather(place, wire, pack, pack_out, here, "pack", True),
-                fetch_rows(),
+                head_gather(place, wire, pack, pack_out, here, Key.pack, True),
                 exchange(),
                 to_rows(),
                 *[
                     head_gather(place, wire, w, o, here, i)
                     for i, (w, o) in enumerate(zip(heads_in, heads))
                 ],
+                fetch_rows(),
+                trade(0),
+                trade(1),
                 output_gather(place, wire, block, output_w, here, 4),
-                fetch_down(),
+                trade(2),
+                far_spread(wire, ffn_out[0], here, (Key.trade, 0)),
+                ffn_spread(place, wire, ffn_out[1], here, (Key.trade, 1), Key.slots),
+                ffn_spread(place, wire, ffn_out[2], here, (Key.trade, 2), Key.slots),
                 fetch_cot(),
-                ffn_gather(place, wire, ffn_in[1], cuts[1], ffn_out[1]),
-                ffn_gather(place, wire, ffn_in[2], cuts[2], ffn_out[2]),
-                product_grads(),
                 compute(),
             )
 
@@ -1849,22 +1922,20 @@
         flat = (streams * length, width)
         raw = (streams, length, hd)
         mixed_shape = (streams, 2, 2, count, width)
-        group = (2, 2, length, ffn_shape[-1])
         outs = comm_call(
             work,
             1,
             (CORE, X, X | CORE, Y, NEAR, FAR),
-            [pack, lines, self.mixer_order(tokens), alive, tokens]
+            [pack, lines, tokens, alive, tokens]
             + list(weights)
             + [block]
             + list(ffn)
-            + [self.ffn_order(cotangent)],
-            [False, False, False, True, True] + [False] * 5 + [True] * 3 + [False],
+            + [cotangent],
+            [False, False, False, True, True] + [False] * 5 + [True] * 4,
             [
                 ((width, 128), BF),
                 ((32, 16, 128), BF),
                 ((streams, length, 128), F32),
-                (gate_shape, F32),
                 (gate_shape, F32),
                 (gate_shape, F32),
                 (gate_shape, F32),
@@ -1873,7 +1944,7 @@
                 (state_shape, F32),
                 (gate_shape, F32),
                 (gate_shape, F32),
-                ((streams, 4, count, width), BF),
+                ((slots, 128), F32),
                 (flat, BF),
                 (raw, F32),
                 ((flat[0], hd), BF),
@@ -1884,8 +1955,8 @@
             + [((4, 2) + block.shape, BF)]
             + [(ffn_shape, BF)] * 3
             + [(plane, BF)] * 2
-            + [(group, BF)],
-            [True] * 12 + [False] * 19 + [True],
+            + [((8, width), F32)],
+            [True] * 12 + [False] * 18 + [True],
             [vmem((streams, 4, count, width), BF), vmem(flat, BF), vmem(state_shape, F32)]
             + [vmem(head, BF)] * 4
             + [vmem(raw, F32)] * 4
@@ -1899,45 +1970,34 @@
                 vmem(mixed_shape, BF),
                 vmem(tokens.shape, F32),
                 vmem(tokens.shape, BF),
-                vmem((8, width), F32),
-                vmem(plane, BF),
-                vmem(ffn_shape, BF),
             ]
-            + rows_buffers(mixed_shape),
+            + rows_buffers(mixed_shape)
+            + [vmem(tokens.shape, BF)],
             150,
             50,
             mb=63,
+            pace=STEADY,
         )
-        pack, lines, low_rank, logits, keep, true_keep, written = outs[:7]
-        survive, slots_in, slots_end, scores, share = outs[7:12]
-        rows, normed, reading, branch, self.hidden_rows = outs[12:17]
-        self.down, self.gate, self.up = outs[26:29]
-        self.cot, self.ffn_in, self.grad_product = outs[29:32]
-        own = lax.dynamic_slice_in_dim(lines, self.head * 8, 8, 0)[:, :tall]
-        gains = self.mixer_unorder(jnp.swapaxes(pack[:, rank : rank + 2], 0, 1)).astype(F32)
+        pack, lines, low_rank, logits, keep, written = outs[:6]
+        survive, slots_in, slots_end, scores, share = outs[6:11]
+        self.ranks, normed, reading, branch, self.hidden_rows = outs[11:16]
+        self.down, self.gate, self.up = outs[25:28]
+        self.cot, self.ffn_in, self.gains = outs[28:31]
+        self.low_rank, self.pack, self.survive = low_rank, pack, survive
         return Mixer(
             reading=reading,
             scores=scores,
             share=share,
             branch=branch,
-            rows=rows.reshape(streams, length, width),
             normed=normed,
-            low=pack[:, :rank],
-            low_rank=low_rank[..., :rank],
-            rank=own[..., :rank].reshape(slots, rank).astype(F32),
             logits=logits,
             keep=keep,
-            true_keep=true_keep,
             written=written,
-            survive=survive[..., 0],
             slots_in=slots_in,
             slots_end=slots_end,
-            weights=list(outs[17:21]),
-            raw=list(outs[21:25]),
-            output=outs[25].reshape(8 * block.shape[0], width),
-            out_gain=lines[:, tall, : out_gain.shape[0]].reshape(-1).astype(F32),
-            ffn_gain=gains[1],
-            attn_gain=gains[0],
+            weights=list(outs[16:20]),
+            raw=list(outs[20:24]),
+            output=outs[24].reshape(8 * block.shape[0], width),
         )
 
     def feed_forward(self, tokens, gain, cotangent):
@@ -1952,21 +2012,26 @@
         side = ffn[2]
 
         def work(place, wire, given, outs, scratch):
-            hidden, gain, cot, rows_in, grad_in, gate_in, up_in = given
-            grad_hidden, gain_sum, act, rows_out, gate_out, up_out = outs
+            hidden, gains, cot, rows_in, gate_in, up_in, cot_in, down_in = given
+            grad_hidden, gain_sum, rows_out, gate_out, up_out, down_out, result_out = outs
             ffn_in, turned, part, up_grad, gate, up, grad_gate, grad_up, gate_grad = scratch[:9]
-            plane_bufs, gate_bufs = scratch[9:14], scratch[14:]
+            act, cot_rows, down, tile, block = scratch[9:14]
+            plane_bufs, gate_bufs = scratch[14:19], scratch[19:]
             loaded = Flags()
             for c in range(2):
                 for h in range(2):
                     loaded.raised((c, h), [wire.keep(rows_in.at[c, h], ffn_in.at[c, h])])
                     if (c, h) == (0, 0):
-                        loaded.raised("gate", [wire.keep(gate_in, gate)])
-                        loaded.raised("up", [wire.keep(up_in, up)])
-                        loaded.raised("grad", [wire.keep(grad_in, grad_up)])
+                        loaded.raised(Key.gate, [wire.keep(gate_in, gate)])
+                        loaded.raised(Key.up, [wire.keep(up_in, up)])
+            loaded.raised(Key.cot, [wire.keep(cot_in, cot_rows)])
             gain_sum[...] = jnp.zeros_like(gain_sum)
 
             made, gate_made = Flags(), Flags()
+
+            def down_rows():
+                yield from last_spread(place, wire, down_in, down)
+                loaded.raised(Key.down)
 
             def rows_of(ref, c, h):
                 return ref[c, h].reshape(many, width)
@@ -1976,18 +2041,36 @@
 
             def compute():
                 groups = [(c, h) for c in range(2) for h in range(2)]
+
+                def columns(key):
+                    at = (key[0] * 2 + key[1]) * side
+                    return ffn_in[:, :, :, :, at : at + side].reshape(4 * many, side)
+
+                def put(key, value):
+                    gate_grad[key[0], key[1]] = value.astype(BF)
+
+                def gate_rows():
+                    return grad_gate[...].reshape(4 * many, cols)
+
                 for c, h in groups:
-                    yield loaded.wait((c, h), "gate", "up", "grad")
+                    yield loaded.wait((c, h), Key.gate, Key.up)
                     x = rows_of(ffn_in, c, h)
-                    gate_pre = mm(x, weight(gate), NN)
-                    up_pre = mm(x, weight(up), NN)
-                    grad = grad_up[c, h].astype(F32)
+                    grad_gate[c, h] = mm(x, weight(gate), NN).astype(BF)
+                    act[c, h] = mm(x, weight(up), NN).astype(BF)
+                    wire.spend(3.2)
+                yield loaded.wait(Key.cot, Key.down)
+                for c, h in groups:
+                    yield []
+                    grad = mm(rows_of(cot_rows, c, h), weight(down), NN)
+                    gate_pre = grad_gate[c, h].astype(F32)
+                    up_pre = act[c, h].astype(F32)
                     sig = jax.nn.sigmoid(gate_pre)
                     act[c, h] = (gate_pre * sig * up_pre).astype(BF)
                     slope = sig * (1.0 + gate_pre * (1.0 - sig))
                     grad_gate[c, h] = (grad * up_pre * slope).astype(BF)
                     grad_up[c, h] = (grad * gate_pre * sig).astype(BF)
-                    wire.spend(4.0)
+                    wire.spend(2.3)
+                yield from weight_tiles(wire, columns, z_line[:2], gate_rows, put, gate_made)
                 for c in (1, 0):
                     for h in range(2):
                         yield []
@@ -1995,19 +2078,9 @@
                         total = total + mm(grad_up[c, h], weight(up), NT)
                         part[c, h] = total.astype(BF).reshape(half[1:])
                         wire.spend(3.0)
-                        made.raised((("near", "far")[c], h))
-
-                def columns(key):
-                    at = (key[0] * 2 + key[1]) * side
-                    return ffn_in[:, :, :, :, at : at + side].reshape(4 * many, side)
-
-                def put(key, value):
-                    gate_grad[key[0], key[1]] = value.astype(BF)
-
-                def gate_rows():
-                    return grad_gate[...].reshape(4 * many, cols)
-
-                yield from weight_tiles(wire, columns, z_line, gate_rows, put, gate_made)
+                        made.raised(((Key.near, Key.far)[c], h))
+
+                yield from weight_tiles(wire, columns, z_line[2:], gate_rows, put, gate_made)
 
                 def put_up(key, value):
                     up_grad[key[0], key[1]] = value.astype(BF)
@@ -2017,13 +2090,37 @@
                     return grad_up[...].reshape(4 * many, cols)
 
                 yield from weight_tiles(wire, columns, z_line, up_rows_all, put_up)
+                busy = {}
+
+                def cot_columns(key):
+                    at = (key[0] * 2 + key[1]) * side
+                    return cot_rows[:, :, :, :, at : at + side].reshape(4 * many, side)
+
+                def put_down(key, value):
+                    slot = key[1]
+                    wire.arrived(*busy.get(slot, ()))
+                    tile[slot] = value.astype(BF)
+                    busy[slot] = [wire.keep(tile.at[slot], down_out.at[key[0], key[1]])]
+
+                def act_rows():
+                    return act[...].reshape(4 * many, cols)
+
+                yield from weight_tiles(wire, cot_columns, z_line, act_rows, put_down)
+                for c in (1, 0):
+                    for h in range(2):
+                        yield []
+                        wire.arrived(*busy.get(Key.block, ()))
+                        total = mm(act[c, h], weight(down), NT)
+                        block[...] = total.astype(BF).reshape(half[1:])
+                        busy[Key.block] = [wire.keep(block, result_out.at[c, h])]
+                        wire.spend(2.0)
 
             def finish_grad(stream, rows, load):
                 part = z_parts(place, load, width)
                 held = hidden[stream, rows]
                 scale = inverse_rms(held)
                 gain_sum[...] += jnp.sum(part * held * scale, axis=0, keepdims=True)
-                total = cot[stream, rows].astype(F32) + norm_back(held, scale, gain[...], part)
+                total = cot[stream, rows].astype(F32) + norm_back(held, scale, gains[1:2], part)
                 grad_hidden[stream, rows] = total
                 turned[stream, rows] = total.astype(BF)
 
@@ -2031,9 +2128,16 @@
                 yield from plane_fold(
                     place, wire, part.at[0], part.at[1], plane_bufs, finish_grad, made
                 )
-                yield from rows_gather(place, wire, turned, rows_out)
+
+            def back_stream(h):
+                here = pl.ds(h, 1)
+                yield made.wait((Key.done, h))
+                yield from rows_gather(place, wire, turned.at[here], rows_out.at[here])
 
             wire.run(
+                down_rows(),
+                back_stream(0),
+                back_stream(1),
                 back_rows(),
                 ffn_fold(place, wire, gate_grad, gate_bufs, gate_out, gate_made),
                 compute(),
@@ -2044,18 +2148,19 @@
             work,
             3,
             (CORE, X, Y, NEAR, FAR),
-            [self.hidden_rows, gain[None], cotangent, self.ffn_in, self.grad_product]
-            + [self.gate, self.up],
-            [True] * 3 + [False] * 4,
+            [self.hidden_rows, self.gains, cotangent, self.ffn_in]
+            + [self.gate, self.up, self.cot, self.down],
+            [True] * 3 + [False] * 5,
             [
                 ((streams, count, width), F32),
                 ((1, width), F32),
-                (group, BF),
                 ((streams, 4, count, width), BF),
                 (ffn[1:], BF),
                 (ffn, BF),
+                (ffn, BF),
+                (plane, BF),
             ],
-            [True] * 3 + [False] * 3,
+            [True] * 2 + [False] * 5,
             [
                 vmem(plane, BF),
                 vmem((streams, count, width), BF),
@@ -2066,15 +2171,21 @@
                 vmem(group, BF),
                 vmem(group, BF),
                 vmem(ffn, BF),
+                vmem(group, BF),
+                vmem(plane, BF),
+                vmem(ffn, BF),
+                vmem((2,) + ffn[2:], BF),
+                vmem(half[1:], BF),
             ]
             + plane_buffers(half)
             + ffn_buffers(ffn),
             60,
-            24,
+            40,
             mb=63,
+            pace=KEEN,
         )
-        grad_hidden, gain_grad, self.act = outs[:3]
-        rows, self.gate_grad, self.up_part = outs[3:]
+        grad_hidden, gain_grad, rows, self.gate_grad = outs[:4]
+        self.up_part, self.down_part, self.result_part = outs[4:]
         rows = rows.reshape(streams, 4 * count, width)
         return grad_hidden.reshape(streams * count, width), gain_grad[0], rows
 
@@ -2105,18 +2216,19 @@
         head = (2, 4, width // 8, hd)
         own = (head[2] // 4, width)
         raw, gate_shape = (streams, length, hd), (streams, slots, length)
-        survive = jnp.broadcast_to(mixer.survive[..., None], slim)
         key_raw, value_raw, query_raw, gate_raw = mixer.raw
 
         def work(place, wire, given, outs, scratch):
-            grad_mixed, output_w, survive, out_gain = given[:4]
+            grad_mixed, output_w, survive, gains = given[:4]
+            out_gain = gains.at[0:1, :hd]
             after, gain_sum, grad_query, grad_gate, grad_k, grad_v, back, own_flow = outs[:8]
-            up_out, output_out, query_out, gate_out = outs[8:]
+            up_out, output_out, query_out, gate_out, part_out = outs[8:]
             loads = {
                 key: (source, target)
                 for key, source, target in zip(
-                    ("reading", "gate", "query", "key", "value", "keep", "written")
-                    + ("scores", "share", "slots", "branch", "normed", "up"),
+                    (Key.reading, Key.gate, Key.query, Key.key, Key.value, Key.keep, Key.written)
+                    + (Key.scores, Key.share, Key.slots, Key.branch, Key.normed, Key.up)
+                    + (Key.query_w, Key.gate_w),
                     given[4:],
                     scratch,
                 )
@@ -2129,31 +2241,32 @@
                     here.raised(key, [wire.keep(*loads[key])])
 
             kept = {key: pair[1] for key, pair in loads.items()}
-            sent, got, grad_read, direct, output_part, query_part, gate_part = scratch[13:20]
-            scan, up_bufs = scratch[20:24], scratch[24:27]
-            lines, query_bufs, gate_bufs = scratch[27:31], scratch[31:35], scratch[35:39]
-            load("up", "branch", "reading", "gate", "normed", "query", "key", "value")
-            load("keep", "written", "scores", "share", "slots")
+            sent, got, grad_read, direct, output_part, query_part, gate_part = scratch[15:22]
+            scan, up_bufs = scratch[22:26], scratch[26:29]
+            lines, query_bufs, gate_bufs = scratch[29:33], scratch[33:37], scratch[37:41]
+            normed_part = scratch[41]
+            load(Key.up, Key.branch, Key.reading, Key.gate, Key.normed, Key.query, Key.key, Key.value)
+            load(Key.keep, Key.written, Key.scores, Key.share, Key.slots, Key.query_w, Key.gate_w)
             gain_sum[...] = jnp.zeros_like(gain_sum)
 
             def returned():
-                yield here.wait("sent")
+                yield here.wait(Key.sent)
                 yield from heads_return(place, wire, sent, got)
-                here.raised("got")
+                here.raised(Key.got)
 
             def scanned():
-                yield here.wait("direct")
+                yield here.wait(Key.direct)
                 yield from pieces_scan(place, wire, True, survive, direct, after, scan)
 
             def up_rows():
-                yield here.wait("up")
-                yield from ffn_fold(place, wire, kept["up"], up_bufs, up_out)
+                yield here.wait(Key.up)
+                yield from ffn_fold(place, wire, kept[Key.up], up_bufs, up_out)
 
             def gated(s):
                 def chunk(part):
                     at = pl.ds(pl.multiple_of(s * length + part.start, 16), part.size)
-                    values, opened = kept["reading"][s, part], kept["gate"][s, part]
-                    grad = got[at].astype(F32)
+                    values, opened = kept[Key.reading][s, part], kept[Key.gate][s, part]
+                    grad = by_tp(got[at].astype(F32), (4, 2), hd // 8)
                     scale = inverse_rms(values)
                     normed = values * scale * out_gain[...]
                     grad_gate[s, part] = (grad * normed * silu_slope(opened)).astype(BF)
@@ -2165,8 +2278,8 @@
 
             def streams_back(s, carry):
                 results = piece_back(
-                    *[kept[key][s] for key in ("query", "key", "value", "keep", "written")],
-                    *[kept[key][s] for key in ("slots", "scores", "share")],
+                    *[kept[key][s] for key in (Key.query, Key.key, Key.value, Key.keep, Key.written)],
+                    *[kept[key][s] for key in (Key.slots, Key.scores, Key.share)],
                     grad_read[s],
                 )
                 targets = (grad_query, grad_k, grad_v, direct, back, own_flow)
@@ -2180,39 +2293,47 @@
                     part = mm(grad_mixed[at : at + half], output_w[...], NT)
                     sent[at : at + half] = part.astype(BF)
                 wire.spend(3.0)
-                here.raised("sent")
-                yield here.wait("branch")
+                here.raised(Key.sent)
+                yield here.wait(Key.branch)
                 block = hd // 4
                 for m in (3, 1, 2, 0):
                     yield []
-                    cols = kept["branch"][:, m * block : (m + 1) * block]
+                    cols = kept[Key.branch][:, m * block : (m + 1) * block]
                     total = mm(cols, grad_mixed[...], TN)
                     output_part[m] = total.astype(BF).reshape(line[1:])
                     wire.spend(1.2)
                     lines_made.raised(m)
-                yield here.wait("got", "reading", "gate")
+                yield here.wait(Key.got, Key.reading, Key.gate)
                 for s in range(streams):
                     gated(s)
                 wire.spend(2.0)
-                yield here.wait("normed")
+                yield here.wait(Key.normed)
                 yield from head_tiles(
                     wire,
-                    kept["normed"],
+                    kept[Key.normed],
                     lambda: grad_gate[...].reshape(rows, hd),
                     gate_part,
                     heads_made[1],
                 )
-                yield here.wait("query", "key", "value", "keep", "written", "scores", "share", "slots")
+                yield here.wait(Key.query, Key.key, Key.value, Key.keep, Key.written, Key.scores, Key.share, Key.slots)
                 lax.fori_loop(0, streams, streams_back, 0)
                 wire.spend(13.0)
-                here.raised("direct")
+                here.raised(Key.direct)
                 yield from head_tiles(
                     wire,
-                    kept["normed"],
+                    kept[Key.normed],
                     lambda: grad_query[...].reshape(rows, hd),
                     query_part,
                     heads_made[0],
                 )
+                yield here.wait(Key.query_w, Key.gate_w)
+                for s in range(streams):
+                    yield []
+                    total = mm(grad_query[s], kept[Key.query_w][...], NT)
+                    total = total + mm(grad_gate[s], kept[Key.gate_w][...], NT)
+                    normed_part[s] = total.astype(BF)
+                    wire.keep(normed_part.at[s], part_out.at[s])
+                    wire.spend(2.5)
 
             wire.run(
                 returned(),
@@ -2239,28 +2360,31 @@
             branch_out,
             mixer.normed,
             self.up_part,
+            mixer.weights[2],
+            mixer.weights[3],
         ]
         outs = comm_call(
             work,
             7,
             (CORE, X, X | CORE, Y, NEAR, FAR),
-            [grad_mixed, mixer.output, survive, mixer.out_gain[None]] + later,
+            [grad_mixed, mixer.output, self.survive, self.gains] + later,
             [True] * 4 + [False] * len(later),
             [
                 (state_shape, F32),
                 ((1, hd), F32),
                 (raw, BF),
                 (raw, BF),
-                (raw, F32),
-                (raw, F32),
+                (raw, BF),
+                (raw, BF),
                 (gate_shape, F32),
                 (gate_shape, F32),
                 (ffn[1:], BF),
                 (line[2:], BF),
                 (own, BF),
                 (own, BF),
+                ((streams, length, width), BF),
             ],
-            [True] * 8 + [False] * 4,
+            [True] * 8 + [False] * 5,
             [vmem(a.shape, a.dtype) for a in later]
             + [
                 vmem((rows, hd), BF),
@@ -2275,136 +2399,243 @@
             + ffn_buffers(ffn)
             + line_buffers(line[2], line[3])
             + line_buffers(head[2], head[3])
-            + line_buffers(head[2], head[3]),
+            + line_buffers(head[2], head[3])
+            + [vmem((streams, length, width), BF)],
             60,
             30,
-            mb=62,
+            mb=63,
+            pace=EARLY,
         )
-        self.up_grad, output_sum, query_sum, gate_sum = outs[8:]
-        self.output_sum = turn_bits(output_sum, True)
+        self.up_grad, output_sum, query_sum, gate_sum, self.normed_part = outs[8:]
+        self.output_sum = output_sum
         self.head_sums = [query_sum, gate_sum]
         return outs[:8]
 
-    def end(self, mixer, grads, normed_part, packed):
-        streams, positions, width = normed_part.shape
-        count = positions // 4
+    def finish(self, mixer, back, tokens, grad_hidden, ffn_gain_grad, small):
+        after, out_gain_grad, unused, unused, grad_k, grad_v, pulled, flow = back
+        streams, count, width = tokens.shape
+        slots, length = flow.shape[1:]
+        rank, hd = small[0].shape[1], grad_k.shape[-1]
+        rows = streams * length
         part_shape = (streams, 2, 2, count, width)
-        hd = grads[0].shape[-1]
-        rows = streams * positions
         head = (2, 4, width // 8, hd)
         own = (head[2] // 4, width)
-        length = -(-packed.shape[1] // 2048) * 16
-        packed = jnp.pad(packed, ((0, 0), (0, length * 128 - packed.shape[1])))
-        plane, group, ffn = self.cot.shape, self.act.shape, self.down.shape
-        half, cols, side = plane[1:], ffn[-1], ffn[2]
-        many = half[1] * half[2]
-        z_line = [(z, y) for z in (3, 1, 2, 0) for y in range(2)]
+        plane, ffn = self.cot.shape, self.down.shape
+        half = plane[1:]
+        raw = (streams, length, hd)
+        sheet = (24, width + H * slots)
+        key_raw, value_raw = mixer.raw[:2]
 
         def work(place, wire, given, outs, scratch):
-            normed_part, packed, values = given[:3]
-            normed_out, small_out, result, key_out, value_out, down_out = outs
-            loads = dict(
-                zip(("key", "value", "normed", "act", "cot", "down"), zip(given[3:], scratch))
-            )
+            after, slots_end, keep, written, pulled, flow, logits = given[:7]
+            low, ranks, gains, tokens, hidden, ffn_sum, out_sum = given[7:14]
+            result_in, down_in, hidden_grad = given[14:17]
+            far_in = result_in.at[1]
+            grad_tokens, result, total_out, key_out, value_out, down_out = outs
+            names = (Key.key, Key.value, Key.grad_k, Key.grad_v, Key.normed, Key.part, Key.key_w, Key.value_w)
+            names = names + (Key.pack,)
+            loads = dict(zip(names, zip(given[17:], scratch)))
+            loads[Key.near] = (result_in.at[0], scratch[9])
+            loads[Key.down] = (down_in.at[0], scratch[10].at[0])
             kept = {key: pair[1] for key, pair in loads.items()}
-            down_grad, parts = scratch[6], scratch[7:9]
-            small, sums = scratch[9:11], scratch[11:14]
-            lines = [scratch[14:18], scratch[18:22]]
-            plane_bufs, fold_bufs = scratch[22:27], scratch[27:]
-            part = kept["cot"]
-            here, made, down_made = Flags(), Flags(), Flags()
+            kept[Key.down] = scratch[10]
+            grads, parts, grad_f = scratch[11:13], scratch[13:15], scratch[15]
+            normed_part, sums, tidy = scratch[16], scratch[17:20], scratch[20]
+            lines = [scratch[21:25], scratch[25:29]]
+            plane_bufs, fold_bufs = scratch[29:34], scratch[34:37]
+            sheets, got_sheets, far_row = scratch[37], scratch[38], scratch[39]
+            here, made = Flags(), Flags()
             heads_made = [Flags(), Flags()]
-            for key in ("cot", "act", "key", "normed", "value", "down"):
+            for key in (Key.down, Key.key, Key.value, Key.grad_k, Key.grad_v, Key.normed, Key.near, Key.part):
                 here.raised(key, [wire.keep(*loads[key])])
-
-            def finish(stream, rows, total):
-                normed_out[stream, rows] = total
+            for key in (Key.pack, Key.key_w, Key.value_w):
+                here.raised(key, [wire.keep(*loads[key])])
+            here.raised(Key.hidden_grad, [wire.keep(hidden_grad, grad_tokens)])
+            here.raised(Key.down_2, [wire.keep(down_in.at[2], scratch[10].at[1])])
+            made.raised((Key.far, 0))
+            made.raised((Key.far, 1))
+
+            def down_rows():
+                yield here.wait(Key.down, Key.down_2)
+                yield from ffn_fold(
+                    place, wire, down_in, fold_bufs, down_out, None, kept[Key.down]
+                )
+
+            def result_rows():
+                yield here.wait(Key.near)
+                made.raised((Key.near, 0))
+                made.raised((Key.near, 1))
+                yield from plane_fold(
+                    place, wire, kept[Key.near], far_in, plane_bufs, finish_result, made
+                )
 
             def finish_result(stream, rows, load):
-                total = values[stream, rows] + z_parts(place, load, width)
+                total = hidden[stream, rows] + z_parts(place, load, width)
                 result[stream, rows] = total.astype(BF)
 
+            def finish_tokens(stream, rows, total):
+                side = width // 8
+                for y in range(2):
+                    for m in range(4):
+                        to = pl.multiple_of((place.z_turn(m) * 2 + y) * side, 128)
+                        at = (y * 4 + m) * side
+                        tidy[:, pl.ds(to, side)] = total[:, at : at + side]
+                x = tokens[stream, rows].astype(F32)
+                grad = norm_back(x, inverse_rms(x), gains[3:4], tidy[...])
+                grad_tokens[stream, rows] += grad
+
+            def token_rows():
+                yield here.wait(Key.normed_part, Key.hidden_grad)
+                yield from rows_fold(place, wire, normed_part, *sums, finish_tokens)
+
+            def all_sums():
+                yield here.wait(Key.sheet)
+                total = sheets.at[0]
+                for step, mask in enumerate((CORE, X, Y, NEAR, FAR)):
+                    yield [wire.send(total, got_sheets.at[step], mask)]
+                    got_sheets[step] += total[...]
+                    total = got_sheets.at[step]
+                total_out[...] = total[...]
+
+            def ending(s, carry):
+                results = piece_after(
+                    *[kept[key][s] for key in (Key.key, Key.value)],
+                    *[ref[s] for ref in (keep, written)],
+                    *[kept[key][s] for key in (Key.grad_k, Key.grad_v)],
+                    *[ref[s] for ref in (pulled, flow, after, slots_end)],
+                )
+                for target, value in zip((grads[0], grads[1], grad_f), results):
+                    target[s] = value.astype(target.dtype)
+                grad_f[s] = grad_f[s] * jax.nn.sigmoid(-logits[s]) / GATE_SCALE
+                return carry
+
+            def unorder(target_row, count, values):
+                side = width // 8
+                for y in range(2):
+                    for m in range(4):
+                        to = pl.multiple_of((place.z_turn(m) * 2 + y) * side, 128)
+                        at = (y * 4 + m) * side
+                        there = (0, slice(target_row, target_row + count), pl.ds(to, side))
+                        sheets[there] = values[:, at : at + side]
+
             def compute():
-                yield here.wait("cot", "act")
-
-                def columns(key):
-                    at = (key[0] * 2 + key[1]) * side
-                    return kept["cot"][:, :, :, :, at : at + side].reshape(4 * many, side)
-
-                def put(key, value):
-                    down_grad[key[0], key[1]] = value.astype(BF)
-
-                def act_rows():
-                    return kept["act"][...].reshape(4 * many, cols)
-
-                yield from weight_tiles(wire, columns, z_line, act_rows, put, down_made)
-                yield here.wait("normed", "key", "value")
-                for index, key in enumerate(("key", "value")):
-                    grad = kept[key]
+                yield here.wait(Key.key, Key.value, Key.grad_k, Key.grad_v)
+                lax.fori_loop(0, streams, ending, 0)
+                wire.spend(6.0)
+                yield here.wait(Key.normed)
+                for index in range(2):
                     yield from head_tiles(
                         wire,
-                        kept["normed"],
-                        lambda: grad[...].reshape(rows, hd),
+                        kept[Key.normed],
+                        lambda: grads[index][...].reshape(rows, hd),
                         parts[index],
                         heads_made[index],
                     )
-                yield here.wait("down")
-                for c in (1, 0):
-                    for h in range(2):
-                        total = mm(kept["act"][c, h], kept["down"][...].reshape(width, cols), NT)
-                        part[c, h] = total.astype(BF).reshape(half[1:])
-                        wire.spend(2.0)
-                        made.raised((("near", "far")[c], h))
-                        yield []
+                yield here.wait(Key.part, Key.pack, Key.key_w, Key.value_w)
+                sheets[0] = jnp.zeros(sheet, F32)
+                far_row[...] = jnp.zeros_like(far_row)
+                low_sum, rank_sum, bias_sum = 0.0, 0.0, 0.0
+                for s in range(streams):
+                    normed = kept[Key.normed][s * length : (s + 1) * length]
+                    f = grad_f[s]
+                    low_grad = mm_fine(f, ranks[...], TN)
+                    total = kept[Key.part][s].astype(F32)
+                    total = total + mm(grads[0][s], kept[Key.key_w][...], NT)
+                    total = total + mm(grads[1][s], kept[Key.value_w][...], NT)
+                    total = total + mm(low_grad, kept[Key.pack][...], NT)
+                    normed_part[s] = total.astype(BF).reshape(part_shape[1:])
+                    far_row[...] += jnp.sum(total * normed.astype(F32), axis=0, keepdims=True)
+                    wire.spend(4.0)
+                    yield []
+                    low_sum = low_sum + mm_fine(low_grad, normed, TN)
+                    rank_sum = rank_sum + mm_fine(f, low[s], NN)
+                    bias_sum = bias_sum + jnp.sum(f, axis=1, keepdims=True)
+                    wire.spend(2.0)
+                here.raised(Key.normed_part)
+                wide = (slots, H * slots)
+                spot = column(wide) - place.tp * slots
+                spread = jnp.where(row(wide) == spot, 1.0, 0.0)
+                unorder(0, rank, low_sum[:rank])
+                unorder(16, 1, far_row[...] / gains[2:3])
+                sheets[0, 0:rank, width:] = mm_fine(rank_sum, spread, TN)[:rank]
+                bias_sum = jnp.broadcast_to(bias_sum, (slots, 128))
+                sheets[0, 16:17, width:] = mm_fine(bias_sum, spread, TN)[:1]
+                sheets[0, 17:18, :width] = ffn_sum[...]
+                sheets[0, 18:19, :hd] = out_sum[...]
+                here.raised(Key.sheet)
 
             wire.run(
-                rows_fold(place, wire, normed_part, *sums, finish),
-                small_fold(place, wire, packed, small, small_out),
-                ffn_fold(place, wire, down_grad, fold_bufs, down_out, down_made),
+                token_rows(),
+                all_sums(),
                 head_fold(place, wire, parts[0], lines[0], key_out, heads_made[0]),
                 head_fold(place, wire, parts[1], lines[1], value_out, heads_made[1]),
-                plane_fold(place, wire, part.at[0], part.at[1], plane_bufs, finish_result, made),
+                down_rows(),
+                result_rows(),
                 compute(),
             )
 
         vmem = pltpu.VMEM
-        later = list(grads) + [mixer.normed, self.act, self.cot, self.down]
-        normed, small, result, key_sum, value_sum, self.down_grad = comm_call(
+        soon = [after, mixer.slots_end, mixer.keep, mixer.written, pulled, flow]
+        soon = soon + [mixer.logits, self.low_rank, self.ranks, self.gains, tokens]
+        soon = soon + [self.hidden_rows]
+        soon = soon + [ffn_gain_grad[None], out_gain_grad]
+        later = [key_raw, value_raw, grad_k, grad_v, mixer.normed, self.normed_part]
+        later = later + [mixer.weights[0], mixer.weights[1], self.pack]
+        aside = [self.result_part, self.down_part, grad_hidden.reshape(tokens.shape)]
+        grad_tokens, result, total, key_sum, value_sum, down_grad = comm_call(
             work,
             8,
             (CORE, X, X | CORE, Y, NEAR, FAR),
-            [normed_part.reshape(part_shape), packed.reshape(32, length, 128), self.hidden_rows]
-            + later,
-            [True] * 3 + [False] * len(later),
+            soon + aside + later,
+            [True] * len(soon) + [False] * (len(aside) + len(later)),
             [
-                ((streams, count, width), F32),
-                ((1, length, 128), F32),
-                (self.hidden_rows.shape, BF),
+                (tokens.shape, F32),
+                (tokens.shape, BF),
+                (sheet, F32),
                 (own, BF),
                 (own, BF),
                 (ffn[1:], BF),
             ],
             [True] * 3 + [False] * 3,
             [vmem(a.shape, a.dtype) for a in later]
-            + [vmem(ffn, BF), vmem(head, BF), vmem(head, BF)]
-            + [vmem((32, length, 128), F32)] * 2
+            + [vmem(half, BF), vmem((2,) + ffn[1:], BF)]
+            + [vmem(raw, BF)] * 2
+            + [vmem(head, BF)] * 2
+            + [vmem((streams, slots, length), F32), vmem(part_shape, BF)]
             + rows_buffers(part_shape)
+            + [vmem((16, width), F32)]
             + line_buffers(head[2], head[3])
             + line_buffers(head[2], head[3])
             + plane_buffers(half)
-            + ffn_buffers(ffn),
+            + ffn_buffers(ffn)
+            + [vmem((1,) + sheet, F32), vmem((5,) + sheet, F32), vmem((1, width), F32)],
             80,
-            16,
-            mb=62,
+            20,
+            mb=63.5,
         )
+        heads = [h.astype(F32) for h in [key_sum, value_sum] + self.head_sums + [self.output_sum]]
 
         def both(parts):
             return jnp.concatenate([parts[0], parts[1]], axis=1).astype(F32)
 
-        heads = [key_sum, value_sum] + self.head_sums + [self.output_sum]
-        heads = [h.astype(F32) for h in heads]
-        ffn_grads = [both(g) for g in (self.gate_grad, self.up_grad, self.down_grad)]
-        return heads, ffn_grads, normed, small.reshape(-1), result
+        ffn_grads = [both(g) for g in (self.gate_grad, self.up_grad, down_grad)]
+        seq, tp = lax.axis_index(SEQ), lax.axis_index(TP)
+
+        def share_of(values, size):
+            return lax.dynamic_slice_in_dim(values, (seq * 4 + tp) * size, size, 1)
+
+        w_low, w_rank, bias, attn_gain, out_gain, ffn_gain = small
+        in_low = share_of(total[:, :width], w_low.shape[0])
+        in_rank = share_of(total[:, width:], w_rank.shape[0])
+        small_grads = (
+            jnp.swapaxes(in_low[:rank], 0, 1),
+            jnp.swapaxes(in_rank[:rank], 0, 1),
+            in_rank[16],
+            in_low[16],
+            share_of(total[18:19, :hd], out_gain.shape[0])[0],
+            in_low[17],
+        )
+        return heads, ffn_grads, grad_tokens, result, small_grads
 
 
 def on_device(
@@ -2426,10 +2657,8 @@
     w_down,
     cotangent,
 ):
-    seq_count, tp_count = lax.axis_size("seq"), lax.axis_size("tp")
-    devices = seq_count * tp_count
-    move = BitMoves() if (seq_count, tp_count) == (8, 4) else PlainMoves()
-    streams, local_len, width = tokens.shape
+    sizes = lax.axis_size(SEQ), lax.axis_size(TP)
+    move = BitMoves() if sizes == (8, 4) else PlainMoves()
     small = (w_low, w_rank, gate_bias, attn_gain, out_gain, ffn_gain)
     mixer = move.start(
         tokens,
@@ -2440,87 +2669,14 @@
         (w_down, w_gate, w_up),
         cotangent,
     )
-    key_rows, value_rows = mixer.raw[:2]
-    key_w, value_w, query_w, gate_w = mixer.weights
-    keep, true_keep, written = mixer.keep, mixer.true_keep, mixer.written
-    slots_end = mixer.slots_end
-    ffn_vec, attn_vec = mixer.ffn_gain, mixer.attn_gain
-    normed, low_rank = mixer.normed, mixer.low_rank
-    held, piece_len, hd = key_rows.shape
-    slots, rank = keep.shape[1], low_rank.shape[-1]
-    flat = held * piece_len
-    inputs = mixer.rows.reshape(flat, width).astype(F32)
-    attn_scale = inverse_rms(inputs)
-    gflop = 1000 * 1000 * 1000
-    own_tokens = tokens.astype(F32)
-
-    grad_hidden, grad_ffn_gain, grad_mixed = move.feed_forward(tokens, ffn_vec, cotangent)
-
-    after, grad_out_gain, grad_query, grad_gate, grad_k, grad_v, back, own = move.mixer_back(
-        mixer, grad_mixed.reshape(flat, width)
+    grad_hidden, grad_ffn_gain, grad_mixed = move.feed_forward(
+        tokens, mixer.ffn_gain, cotangent
     )
-    grad_out_gain = grad_out_gain[0]
-    grad_key, grad_value, grad_log = per_stream(
-        piece_after,
-        [
-            key_rows,
-            value_rows,
-            keep,
-            true_keep,
-            written,
-            grad_k,
-            grad_v,
-            back,
-            own,
-            after,
-            slots_end,
-        ],
-        [((piece_len, hd), BF), ((piece_len, hd), BF), ((slots, piece_len), F32)],
-        gflop,
-    )
-    grad_f = grad_log * jax.nn.sigmoid(-mixer.logits) / GATE_SCALE
-    grad_bias = jnp.sum(grad_f, axis=(0, 2))
-    highest = lax.Precision.HIGHEST
-    grad_rank = jnp.einsum("smt,str->mr", grad_f, low_rank, precision=highest)
-    grad_low_rank = jnp.einsum("smt,mr->str", grad_f, mixer.rank, precision=highest)
-    grad_low_rank = grad_low_rank.reshape(flat, rank)
-    grads = [g.reshape(flat, hd) for g in (grad_query, grad_key, grad_value, grad_gate)]
-    grad_normed = sum(
-        product(g, w, NT) for g, w in zip(grads, (query_w, key_w, value_w, gate_w))
-    )
-    grad_normed = grad_normed + product(grad_low_rank, mixer.low.astype(F32), NT)
-    attn_part = jnp.sum(grad_normed * inputs * attn_scale, axis=0)
-    grad_low = product(grad_low_rank, normed.astype(F32), TN)
-    grad_low = jnp.swapaxes(move.mixer_unorder(grad_low), 0, 1)
-
-    def placed(part):
-        entire = jnp.zeros((part.shape[0] * H,) + part.shape[1:], F32)
-        return lax.dynamic_update_slice_in_dim(entire, part, move.head * part.shape[0], 0)
-
-    sums = (
-        grad_low,
-        placed(grad_rank),
-        placed(grad_bias),
-        move.mixer_unorder(attn_part),
-        grad_out_gain,
-        grad_ffn_gain,
-    )
-    packed = jnp.concatenate([a.reshape(devices, -1) for a in sums], axis=1)
-    heads, ffn_grads, grad_normed, own_sums, result = move.end(
-        mixer,
-        [grad_key, grad_value],
-        grad_normed.astype(BF).reshape(held, piece_len, width),
-        packed,
+    back = move.mixer_back(mixer, grad_mixed.reshape(-1, tokens.shape[-1]))
+    heads, ffn_grads, grad_tokens, result, small_grads = move.finish(
+        mixer, back, tokens, grad_hidden, grad_ffn_gain, small
     )
     grad_w_key, grad_w_value, grad_w_query, grad_w_gate_out, grad_w_output = heads
-    grad_normed = move.mixer_unorder(grad_normed)
-    own_scale = inverse_rms(own_tokens)
-    grad_tokens = grad_hidden.reshape(tokens.shape)
-    grad_tokens = grad_tokens + norm_back(own_tokens, own_scale, attn_vec, grad_normed)
-    small_grads, taken = [], 0
-    for a in small:
-        small_grads.append(own_sums[taken : taken + a.size].reshape(a.shape))
-        taken += a.size
     return (
         (result.reshape(tokens.shape), grad_tokens)
         + (grad_w_query, grad_w_key, grad_w_value, grad_w_gate_out, grad_w_output)
@@ -2530,8 +2686,8 @@
 
 
 def solution(mesh):
-    both, row_split, line = ("seq", "tp"), P(("seq", "tp"), None), P(("seq", "tp"))
-    tokens_at, ffn_at = P(None, both, None), P("seq", "tp")
+    both, row_split, line = (SEQ, TP), P((SEQ, TP), None), P((SEQ, TP))
+    tokens_at, ffn_at = P(None, both, None), P(SEQ, TP)
     params = (row_split,) * 7 + (line,) * 4 + (ffn_at,) * 3
     return jax.shard_map(
         on_device,

time: 743 us -> 641 us (0.86)
  local copies, waits for them, and re-layouts: 45 us -> 8.72 us
  Pallas kernels: 636 us -> 611 us
  matrix products: 24.9 us -> 0 us
  other arithmetic: 20.2 us -> 10.9 us
    dot_general x8 -> x0, matrix products: 24.9 us -> none  [the longest x6 22.6 us: product(): lax.dot_general(left, right, (dims, ((), ())), preferred_element_type=F32)]
    pallas_call x4, Pallas kernels: 631 us -> 611 us  [comm_call(): pl.pallas_call(body, in_specs=[space(v) for v in in_vmem], out_specs=[spa...]
    unnamed x114 -> x23, local copies, waits for them, and re-layouts: 13.6 us -> 2.73 us
    reshape x12 -> x0, local copies, waits for them, and re-layouts: 10.7 us -> none  [the longest x2 2.71 us: mixer_unorder(): return jnp.swapaxes(parts, -3, -2).reshape(lead + (width,))]
    slice x8 -> x3, local copies, waits for them, and re-layouts: 8.33 us -> 0.02 us  [the longest x1 0.01 us: finish(): in_low = share_of(total[:, :width], w_low.shape[0])]
  transfers between devices with their start and end apart: 2 -> 0, of which waited for: 0 -> 0; matrix products, arithmetic and copies ran while one was open for 2% -> 0% of each run, Pallas kernels for 0% -> 0%
where the time goes in v3:
time: 641 us; the launch traced here: 631 us
  Pallas kernels  611 us (95%)
  other arithmetic  10.9 us (2%)
  local copies, waits for them, and re-layouts  8.72 us (1%)
    pallas_call x4, Pallas kernels, comm_call(): pl.pallas_call(body, in_specs=[space(v) for v in in_vmem], out_specs=[spa...  611 us

profile of v3, /device:TPU:0, one launch (start us, length us, event | category | flops | bytes accessed | tf_op | source)
XLA Modules:
  0.0 631.3 jit_solution(14399511880742485830)
XLA Ops:
  0.7 1.3 or_select_fusion.refs_3_
  2.0 0.7 pad_maximum_fusion
  2.7 0.1 copy.38
  2.8 0.6 pad.16.refs_0_
  3.4 0.7 copy.39
  4.2 0.8 fusion.6
  4.9 0.7 pad_bitcast_fusion
  5.6 0.6 fusion.3.refs_1_
  6.2 259.5 %shard_map.288 = (bf16[2048,128]{1,0:T(8,128)(2,1)}, bf16[32,16,128]{2,1,0:T(8,128)(2,1)}, f32[2,384,128]{2,1,0:T(8,128)}, f32[2,64,384]{2,1,0:T(8,128)}, f32[2,...) custom-call(bf16[64,128]{1,0:T(8,128)(2,1)} %pad.16.refs_0_, ...), custom_call_target="tpu_custom_call" | custom-call | bytes 65536 | tf_op jit(solution)/shard_map/pallas_call | solution.py:631
  265.7 98.7 %shard_map.289 = (f32[2,96,2048]{2,1,0:T(8,128)}, f32[1,2048]{1,0:T(1,128)}, bf16[2,4,96,2048]{3,2,1,0:T(8,128)(2,1)}, bf16[2,256,704]{2,1,0:T(8,128)(2,1)}, bf1...) custom-call(f32[2,96,2048]{2,1,0:T(8,128)} %get-tuple-element.70.refs_0_.refs_1, ...), custom_call_target="tpu_custom_call" | custom-call | bytes 65536 | tf_op jit(solution)/shard_map/pallas_call | solution.py:631
  364.4 135.6 %shard_map.290 = (f32[2,64,1024]{2,1,0:T(8,128)}, f32[1,512]{1,0:T(1,128)}, bf16[2,384,512]{2,1,0:T(8,128)(2,1)}, bf16[2,384,512]{2,1,0:T(8,128)(2,1)}, bf16[2,3...) custom-call(bf16[768,2048]{1,0:T(8,128)(2,1)} %bitcast.33, ...), custom_call_target="tpu_custom_call" | custom-call | bytes 65536 | tf_op jit(solution)/shard_map/pallas_call | solution.py:631
  500.0 116.7 %shard_map.291 = (f32[2,96,2048]{2,1,0:T(8,128)}, bf16[2,96,2048]{2,1,0:T(8,128)(2,1)}, f32[24,2304]{1,0:T(8,128)}, bf16[64,2048]{1,0:T(8,128)(2,1)}, bf16[64,20...) custom-call(f32[2,64,1024]{2,1,0:T(8,128)} %get-tuple-element.95.refs_0_, f32[2,64,1024]{2,1,0:T(8,128)} %get-tuple-element.96.refs_1_, ...), custom_call_target="tpu_custom_call" | custom-call | bytes 65536 | tf_op jit(solution)/shard_map/pallas_call | solution.py:631
  616.8 1.2 slice_bitcast_fusion.1
  618.0 0.0 copy-start.2
  618.0 1.3 maximum_convert_fusion.2
  619.3 0.1 slice_bitcast_fusion.3
  619.4 0.0 copy-done.2
  619.4 0.1 slice_bitcast_fusion.5
  619.5 2.0 maximum_convert_fusion
  621.5 0.8 convert_element_type.33
  622.3 0.8 convert_element_type.34
  623.2 0.7 dynamic-slice_bitcast_fusion.1
  623.9 0.6 dynamic-slice_bitcast_fusion.2
  624.5 0.1 dynamic-slice_bitcast_fusion
  624.5 0.7 copy.40
  625.2 0.6 dynamic-slice_bitcast_fusion.4
  625.8 0.6 fusion.7
  626.4 0.8 convert_element_type.32
  627.2 0.8 convert_element_type.35
  628.1 0.8 convert_element_type.36
  628.9 0.9 copy.43
  629.8 1.1 copy.44
  (23 shorter events, 0.1 us)
Async XLA Ops:
  616.8 2.6 copy-start.3
  618.0 1.4 copy-start.2
  619.5 2.0 copy-start.8
  619.5 2.9 copy-start.7
  621.5 1.7 copy-start.9
  621.5 4.9 copy-start.6
  621.5 5.7 copy-start.5
  622.3 5.7 copy-start.4
  623.2 5.7 copy-start.1
  627.2 2.6 copy-start

commit v4 on v3

--- a/solution.py
+++ b/solution.py
@@ -613,7 +613,7 @@
 
 
 FAST, STEADY = (2.5, 91, 400, 5.0), (3.5, 86, 300, 6.0)
-KEEN, EARLY = (2.5, 91, 400, 2.0), (2.5, 91, 400, 15.0)
+KEEN, EARLY = (2.5, 91, 400, 2.0), (2.5, 91, 400, 25.0)
 
 
 def comm_call(work, number, masks, arrays, in_vmem, outs, out_vmem, scratch, copies, stay, mb=48, pace=FAST):
@@ -998,11 +998,13 @@
     row_loop(target.shape[0], step, work)
 
 
-def ffn_fold(place, wire, part, bufs, out, flags=None, added=None):
+def ffn_fold(place, wire, part, bufs, out, flags=None, added=None, ahead=None):
     added = (part.at[0], part.at[2]) if added is None else (added.at[0], added.at[1])
     got_near, got_far, held = bufs
-    first, second, far = [], [], []
+    first, second, far = list(ahead or []), [], []
     for z, handles in ((3, first), (1, second)):
+        if z == 3 and ahead is not None:
+            continue
         for y in range(2):
             if flags is not None:
                 yield flags.wait((z, y))
@@ -2013,7 +2015,7 @@
 
         def work(place, wire, given, outs, scratch):
             hidden, gains, cot, rows_in, gate_in, up_in, cot_in, down_in = given
-            grad_hidden, gain_sum, rows_out, gate_out, up_out, down_out, result_out = outs
+            grad_hidden, gain_sum, rows_out, gate_out, up_out, down_out, result_out, up_ahead = outs
             ffn_in, turned, part, up_grad, gate, up, grad_gate, grad_up, gate_grad = scratch[:9]
             act, cot_rows, down, tile, block = scratch[9:14]
             plane_bufs, gate_bufs = scratch[14:19], scratch[19:]
@@ -2027,11 +2029,18 @@
             loaded.raised(Key.cot, [wire.keep(cot_in, cot_rows)])
             gain_sum[...] = jnp.zeros_like(gain_sum)
 
-            made, gate_made = Flags(), Flags()
+            made, gate_made, up_made = Flags(), Flags(), Flags()
 
             def down_rows():
                 yield from last_spread(place, wire, down_in, down)
                 loaded.raised(Key.down)
+
+            def up_rows():
+                handles = []
+                for y in range(2):
+                    yield up_made.wait((3, y))
+                    handles.append(wire.send(up_grad.at[3, y], up_ahead.at[y], NEAR))
+                yield handles
 
             def rows_of(ref, c, h):
                 return ref[c, h].reshape(many, width)
@@ -2085,6 +2094,7 @@
                 def put_up(key, value):
                     up_grad[key[0], key[1]] = value.astype(BF)
                     wire.keep(up_grad.at[key[0], key[1]], up_out.at[key[0], key[1]])
+                    up_made.raised(key)
 
                 def up_rows_all():
                     return grad_up[...].reshape(4 * many, cols)
@@ -2140,6 +2150,7 @@
                 back_stream(1),
                 back_rows(),
                 ffn_fold(place, wire, gate_grad, gate_bufs, gate_out, gate_made),
+                up_rows(),
                 compute(),
             )
 
@@ -2159,8 +2170,9 @@
                 (ffn, BF),
                 (ffn, BF),
                 (plane, BF),
+                (ffn[1:], BF),
             ],
-            [True] * 2 + [False] * 5,
+            [True] * 2 + [False] * 6,
             [
                 vmem(plane, BF),
                 vmem((streams, count, width), BF),
@@ -2185,7 +2197,7 @@
             pace=KEEN,
         )
         grad_hidden, gain_grad, rows, self.gate_grad = outs[:4]
-        self.up_part, self.down_part, self.result_part = outs[4:]
+        self.up_part, self.down_part, self.result_part, self.up_ahead = outs[4:]
         rows = rows.reshape(streams, 4 * count, width)
         return grad_hidden.reshape(streams * count, width), gain_grad[0], rows
 
@@ -2220,6 +2232,7 @@
 
         def work(place, wire, given, outs, scratch):
             grad_mixed, output_w, survive, gains = given[:4]
+            up_ahead = given[-1]
             out_gain = gains.at[0:1, :hd]
             after, gain_sum, grad_query, grad_gate, grad_k, grad_v, back, own_flow = outs[:8]
             up_out, output_out, query_out, gate_out, part_out = outs[8:]
@@ -2260,7 +2273,11 @@
 
             def up_rows():
                 yield here.wait(Key.up)
-                yield from ffn_fold(place, wire, kept[Key.up], up_bufs, up_out)
+                got = up_bufs[0].at[1]
+                ahead = [wire.keep(up_ahead.at[y], got.at[y]) for y in range(2)]
+                yield from ffn_fold(
+                    place, wire, kept[Key.up], up_bufs, up_out, None, None, ahead
+                )
 
             def gated(s):
                 def chunk(part):
@@ -2367,8 +2384,8 @@
             work,
             7,
             (CORE, X, X | CORE, Y, NEAR, FAR),
-            [grad_mixed, mixer.output, self.survive, self.gains] + later,
-            [True] * 4 + [False] * len(later),
+            [grad_mixed, mixer.output, self.survive, self.gains] + later + [self.up_ahead],
+            [True] * 4 + [False] * (1 + len(later)),
             [
                 (state_shape, F32),
                 ((1, hd), F32),
@@ -2424,6 +2441,7 @@
         half = plane[1:]
         raw = (streams, length, hd)
         sheet = (24, width + H * slots)
+        halves = [width // 2, width // 4, width // 8, width // 16, width // 16]
         key_raw, value_raw = mixer.raw[:2]
 
         def work(place, wire, given, outs, scratch):
@@ -2443,12 +2461,12 @@
             normed_part, sums, tidy = scratch[16], scratch[17:20], scratch[20]
             lines = [scratch[21:25], scratch[25:29]]
             plane_bufs, fold_bufs = scratch[29:34], scratch[34:37]
-            sheets, got_sheets, far_row = scratch[37], scratch[38], scratch[39]
+            sheets, got_sheets, far_row = scratch[37], scratch[38:43], scratch[43]
             here, made = Flags(), Flags()
             heads_made = [Flags(), Flags()]
-            for key in (Key.down, Key.key, Key.value, Key.grad_k, Key.grad_v, Key.normed, Key.near, Key.part):
+            for key in (Key.key, Key.value, Key.grad_k, Key.grad_v, Key.normed, Key.part):
                 here.raised(key, [wire.keep(*loads[key])])
-            for key in (Key.pack, Key.key_w, Key.value_w):
+            for key in (Key.pack, Key.key_w, Key.value_w, Key.near, Key.down):
                 here.raised(key, [wire.keep(*loads[key])])
             here.raised(Key.hidden_grad, [wire.keep(hidden_grad, grad_tokens)])
             here.raised(Key.down_2, [wire.keep(down_in.at[2], scratch[10].at[1])])
@@ -2490,12 +2508,22 @@
 
             def all_sums():
                 yield here.wait(Key.sheet)
-                total = sheets.at[0]
-                for step, mask in enumerate((CORE, X, Y, NEAR, FAR)):
-                    yield [wire.send(total, got_sheets.at[step], mask)]
-                    got_sheets[step] += total[...]
-                    total = got_sheets.at[step]
-                total_out[...] = total[...]
+                total, rest, half = sheets.at[0, :, :width], sheets.at[0, :, width:], width // 2
+                steps = ((FAR, place.far), (NEAR, place.near), (Y, place.y), (X, place.x))
+                for step, (mask, bit) in enumerate(steps):
+                    theirs = pl.ds(pl.multiple_of((1 - bit) * half, 128), half)
+                    mine = pl.ds(pl.multiple_of(bit * half, 128), half)
+                    got = got_sheets[step]
+                    yield [
+                        wire.send(total.at[:, theirs], got.at[:, :half], mask),
+                        wire.send(rest, got.at[:, half:], mask),
+                    ]
+                    got[:, :half] += total[:, mine]
+                    got[:, half:] += rest[...]
+                    total, rest, half = got.at[:, :half], got.at[:, half:], half // 2
+                got = got_sheets[4]
+                yield [wire.send(got_sheets[3], got, CORE)]
+                total_out[...] = got[...] + got_sheets[3][...]
 
             def ending(s, carry):
                 results = piece_after(
@@ -2518,19 +2546,21 @@
                         there = (0, slice(target_row, target_row + count), pl.ds(to, side))
                         sheets[there] = values[:, at : at + side]
 
+            def weight_grad(index):
+                return head_tiles(
+                    wire,
+                    kept[Key.normed],
+                    lambda: grads[index][...].reshape(rows, hd),
+                    parts[index],
+                    heads_made[index],
+                )
+
             def compute():
                 yield here.wait(Key.key, Key.value, Key.grad_k, Key.grad_v)
                 lax.fori_loop(0, streams, ending, 0)
                 wire.spend(6.0)
                 yield here.wait(Key.normed)
-                for index in range(2):
-                    yield from head_tiles(
-                        wire,
-                        kept[Key.normed],
-                        lambda: grads[index][...].reshape(rows, hd),
-                        parts[index],
-                        heads_made[index],
-                    )
+                yield from weight_grad(0)
                 yield here.wait(Key.part, Key.pack, Key.key_w, Key.value_w)
                 sheets[0] = jnp.zeros(sheet, F32)
                 far_row[...] = jnp.zeros_like(far_row)
@@ -2561,8 +2591,11 @@
                 bias_sum = jnp.broadcast_to(bias_sum, (slots, 128))
                 sheets[0, 16:17, width:] = mm_fine(bias_sum, spread, TN)[:1]
                 sheets[0, 17:18, :width] = ffn_sum[...]
-                sheets[0, 18:19, :hd] = out_sum[...]
+                per = H * slots
+                for at in range(hd // per):
+                    sheets[0, 17 + at : 18 + at, width:] = out_sum[:, at * per : (at + 1) * per]
                 here.raised(Key.sheet)
+                yield from weight_grad(1)
 
             wire.run(
                 token_rows(),
@@ -2591,7 +2624,7 @@
             [
                 (tokens.shape, F32),
                 (tokens.shape, BF),
-                (sheet, F32),
+                ((24, width // 16 + H * slots), F32),
                 (own, BF),
                 (own, BF),
                 (ffn[1:], BF),
@@ -2608,7 +2641,9 @@
             + line_buffers(head[2], head[3])
             + plane_buffers(half)
             + ffn_buffers(ffn)
-            + [vmem((1,) + sheet, F32), vmem((5,) + sheet, F32), vmem((1, width), F32)],
+            + [vmem((1,) + sheet, F32)]
+            + [vmem((24, size + H * slots), F32) for size in halves]
+            + [vmem((1, width), F32)],
             80,
             20,
             mb=63.5,
@@ -2619,20 +2654,21 @@
             return jnp.concatenate([parts[0], parts[1]], axis=1).astype(F32)
 
         ffn_grads = [both(g) for g in (self.gate_grad, self.up_grad, down_grad)]
-        seq, tp = lax.axis_index(SEQ), lax.axis_index(TP)
-
-        def share_of(values, size):
-            return lax.dynamic_slice_in_dim(values, (seq * 4 + tp) * size, size, 1)
-
+        tp = lax.axis_index(TP)
+        flat = lax.axis_index(SEQ) * 4 + tp
         w_low, w_rank, bias, attn_gain, out_gain, ffn_gain = small
-        in_low = share_of(total[:, :width], w_low.shape[0])
-        in_rank = share_of(total[:, width:], w_rank.shape[0])
+        tall, wide = w_low.shape[0], width // 16
+        in_low = lax.dynamic_slice_in_dim(total[:, :wide], tp % 2 * tall, tall, 1)
+        in_rank = lax.dynamic_slice_in_dim(
+            total[:, wide:], flat * w_rank.shape[0], w_rank.shape[0], 1
+        )
+        out_sums = total[17 : 17 + hd // (H * slots), wide:].reshape(-1)
         small_grads = (
             jnp.swapaxes(in_low[:rank], 0, 1),
             jnp.swapaxes(in_rank[:rank], 0, 1),
             in_rank[16],
             in_low[16],
-            share_of(total[18:19, :hd], out_gain.shape[0])[0],
+            lax.dynamic_slice_in_dim(out_sums, flat * out_gain.shape[0], out_gain.shape[0], 0),
             in_low[17],
         )
         return heads, ffn_grads, grad_tokens, result, small_grads

time: 641 us -> 627 us (0.978)
  Pallas kernels: 611 us -> 597 us
    pallas_call x4, Pallas kernels: 611 us -> 597 us  [comm_call(): pl.pallas_call(body, in_specs=[space(v) for v in in_vmem], out_specs=[spa...]
where the time goes in v4:
time: 627 us; the launch traced here: 618 us
  Pallas kernels  597 us (95%)
  other arithmetic  10.9 us (2%)
  local copies, waits for them, and re-layouts  8.71 us (1%)
    pallas_call x4, Pallas kernels, comm_call(): pl.pallas_call(body, in_specs=[space(v) for v in in_vmem], out_specs=[spa...  597 us

profile of v4, /device:TPU:0, one launch (start us, length us, event | category | flops | bytes accessed | tf_op | source)
XLA Modules:
  0.0 617.7 jit_solution(2118574222163731837)
XLA Ops:
  0.7 1.3 or_select_fusion.refs_3_
  2.0 0.7 pad_maximum_fusion
  2.7 0.1 copy.38
  2.8 0.6 pad.16.refs_0_
  3.4 0.7 copy.39
  4.2 0.8 fusion.6
  4.9 0.7 pad_bitcast_fusion
  5.6 0.6 fusion.3.refs_1_
  6.2 259.6 %shard_map.288 = (bf16[2048,128]{1,0:T(8,128)(2,1)}, bf16[32,16,128]{2,1,0:T(8,128)(2,1)}, f32[2,384,128]{2,1,0:T(8,128)}, f32[2,64,384]{2,1,0:T(8,128)}, f32[2,...) custom-call(bf16[64,128]{1,0:T(8,128)(2,1)} %pad.16.refs_0_, ...), custom_call_target="tpu_custom_call" | custom-call | bytes 65536 | tf_op jit(solution)/shard_map/pallas_call | solution.py:631
  265.8 99.3 %shard_map.289 = (f32[2,96,2048]{2,1,0:T(8,128)}, f32[1,2048]{1,0:T(1,128)}, bf16[2,4,96,2048]{3,2,1,0:T(8,128)(2,1)}, bf16[2,256,704]{2,1,0:T(8,128)(2,1)}, bf1...) custom-call(f32[2,96,2048]{2,1,0:T(8,128)} %get-tuple-element.71.ref, ...), custom_call_target="tpu_custom_call" | custom-call | bytes 65536 | tf_op jit(solution)/shard_map/pallas_call | solution.py:631
  365.0 121.4 %shard_map.290 = (f32[2,64,1024]{2,1,0:T(8,128)}, f32[1,512]{1,0:T(1,128)}, bf16[2,384,512]{2,1,0:T(8,128)(2,1)}, bf16[2,384,512]{2,1,0:T(8,128)(2,1)}, bf16[2,3...) custom-call(bf16[768,2048]{1,0:T(8,128)(2,1)} %bitcast.34, ...), custom_call_target="tpu_custom_call" | custom-call | bytes 65536 | tf_op jit(solution)/shard_map/pallas_call | solution.py:631
  486.5 116.7 %shard_map.291 = (f32[2,96,2048]{2,1,0:T(8,128)}, bf16[2,96,2048]{2,1,0:T(8,128)(2,1)}, f32[24,384]{1,0:T(8,128)}, bf16[64,2048]{1,0:T(8,128)(2,1)}, bf16[64,204...) custom-call(f32[2,64,1024]{2,1,0:T(8,128)} %get-tuple-element.97.refs_0_, f32[2,64,1024]{2,1,0:T(8,128)} %get-tuple-element.98.refs_1_, ...), custom_call_target="tpu_custom_call" | custom-call | bytes 65536 | tf_op jit(solution)/shard_map/pallas_call | solution.py:631
  603.2 1.2 slice_bitcast_fusion.1
  604.4 1.3 maximum_convert_fusion.2
  605.7 0.1 slice_bitcast_fusion.3
  605.8 0.0 copy-done.2
  605.8 0.1 slice_bitcast_fusion.5
  605.9 2.0 maximum_convert_fusion
  607.9 0.0 copy-done.8
  607.9 0.8 convert_element_type.33
  608.8 0.8 convert_element_type.34
  609.6 0.7 dynamic-slice_bitcast_fusion.1
  610.3 0.6 dynamic-slice_bitcast_fusion.2
  610.9 0.1 dynamic-slice_bitcast_fusion
  610.9 0.7 copy.40
  611.6 0.6 dynamic-slice_bitcast_fusion.4
  612.2 0.6 dynamic_slice.11
  612.8 0.8 convert_element_type.32
  613.6 0.8 convert_element_type.35
  614.5 0.8 convert_element_type.36
  615.3 0.9 copy.44
  616.2 1.1 copy.45
  (24 shorter events, 0.1 us)
Async XLA Ops:
  603.2 2.6 copy-start.3
  604.4 1.4 copy-start.2
  605.9 2.0 copy-start.8
  605.9 2.9 copy-start.7
  607.9 1.7 copy-start.9
  607.9 4.9 copy-start.6
  607.9 5.7 copy-start.5
  607.9 6.5 %copy-start.4 = (bf16[64,2048]{1,0:T(8,128)(2,1)S(1)}, bf16[64,2048]{1,0:T(8,128)(2,1)}, u32[]{:S(2)}) copy-start(bf16[64,2048]{1,0:T(8,128)(2,1)} %get-tuple-element.121) | copy-start | bytes 786436
  608.8 6.5 %copy-start.1 = (bf16[2,96,2048]{2,1,0:T(8,128)(2,1)S(1)}, bf16[2,96,2048]{2,1,0:T(8,128)(2,1)}, u32[]{:S(2)}) copy-start(bf16[2,96,2048]{2,1,0:T(8,128)(2,1)} %get-tuple-element.184) | copy-start | bytes 2359300
  613.6 2.6 copy-start
